TPU v7x, 32 devices: a whole 2x2x4 slice. The times are simulated.
32 devices in a mesh: groups: 2 (over y), tiles: 4 (over z), split: 2 (over x), depth: 2 (over core).
Axes of the slice: x: 2, y: 2, z: 4, core: 2. Of those that a mesh axis runs over, the one named last changes fastest.
Arguments:
- tile_codes: bfloat16 [2048, 256, 256], P(('groups', 'tiles', 'split', 'depth')), parts along dimension 0, may hold values from -127 to 127, as said below
- tile_scale: float32 [2048], P(('groups', 'tiles', 'split', 'depth')), parts along dimension 0, may hold values from 9.375e-05 to 0.00078125
- tile_row: int32 [2048], P(('groups', 'tiles', 'split', 'depth')), parts along dimension 0, may hold values from 0 to 15
- tile_column: int32 [2048], P(('groups', 'tiles', 'split', 'depth')), parts along dimension 0, may hold values from 0 to 11, as said below
- send_index: int32 [32, 4, 2], P(('groups', 'tiles', 'split', 'depth')), parts along dimension 0, may hold values from 0 to 3
- model_start: float32 [128, 256], P(('groups', 'tiles', 'split', 'depth')), parts along dimension 0, may hold values from -6 to 6
- reg_weight: float32 [128, 256], P(('groups', 'tiles', 'split', 'depth')), parts along dimension 0, may hold values from 0.05 to 1
- observed: float32 [128, 256], P(('groups', 'tiles')), parts along dimension 0, may hold values from -6 to 6
- data_weight: float32 [128, 256], P(('groups', 'tiles')), parts along dimension 0, may hold values from 0.5 to 2
Outputs:
- model: float32 [128, 256], P(('groups', 'tiles', 'split', 'depth')), parts along dimension 0
- residual: float32 [128, 256], P(('groups', 'tiles', 'split', 'depth')), parts along dimension 0
There are 2 independent parts, one for each index of `groups`. A program takes and returns all parts, laid end to end along the dimension named above; each array names one. Nothing has to cross between parts.
Inputs may be any that keep to these rules, and one draw needn't show every extreme that they name: `tile_column`: below 4 a position names a block of the device itself; position c >= 4 names slot (c - 4) % 2 of what map tile (c - 4) // 2 sends from the device with the same split and depth index. Every position is named on every device. `send_index`: entry [d, t, j] is the block of device d's own 4 blocks placed in slot j of what d sends to map tile t. `tile_codes`: each value is an integer.
All inputs are finite; a program needn't handle non-finite values.
Results may differ from a plain program's by a relative error of at most 0.0088.
Values may be sent and summed in bfloat16 or wider, within the bound.
No kernel may reach another device: no remote copies, remote signals or barrier semaphores. Data moves between devices by JAX's collectives and lax.ppermute only.
A program may use at most 64 MiB of HBM per device.

v0:
```python
import functools

import jax
import jax.numpy as jnp
from jax import lax
from jax.experimental import pallas as pl
from jax.experimental.pallas import tpu as pltpu
from jax.sharding import PartitionSpec as P

HIGH = lax.Precision.HIGHEST
EXTRA = 8
LIMIT = 16 * 1024 * 1024
GROUP = 16
CHUNK = 8
F32 = jnp.float32
BF16 = jnp.bfloat16


def exchange(values, axes, size):
    parts = [values[0]] + [None] * (size - 1)
    for shift in range(size - 1, 0, -1):
        perm = [(i, i ^ shift) for i in range(size)]
        parts[shift] = lax.ppermute(values[shift], axes, perm)
    return parts


def total_rows(parts):
    total = parts[0][...]
    for part in parts[1:]:
        total = total + part[...]
    return total


def total_blocks(parts, blocks):
    count = len(parts)
    groups = []
    for group in range(count):
        total = None
        for shift in range(count):
            start = (group ^ shift) * blocks
            piece = parts[shift][start : start + blocks, :]
            total = piece if total is None else total + piece
        groups.append(total)
    return jnp.concatenate(groups, axis=0)


def extra_rows(parts, start):
    total = parts[0][start : start + EXTRA, :]
    for part in parts[1:]:
        total = total + part[start : start + EXTRA, :]
    return total


def whole(value):
    return jnp.sum(value, axis=(0, 1), keepdims=True)


def columns(value):
    return jnp.sum(value, axis=0, keepdims=True)


def pack_rows(rows, width):
    filled = list(rows)
    while len(filled) < EXTRA:
        filled.append(jnp.zeros((1, width), F32))
    return jnp.concatenate(filled, axis=0)


def products(tile_of, picked):
    tiles, width = picked.shape
    index = lax.broadcasted_iota(jnp.int32, (GROUP, width), 0)
    pieces = []
    for first in range(0, tiles, GROUP):
        rows = picked[first : first + GROUP, :]
        total = None
        for i in range(GROUP):
            value = jnp.dot(rows, tile_of(first + i), preferred_element_type=F32)
            total = value if total is None else jnp.where(index == i, value, total)
        pieces.append(total)
    return jnp.concatenate(pieces, axis=0)


def kept_tiles(low, high):
    half = low.shape[0]
    return lambda k: low[k] if k < half else high[k - half]


def pick(table, values):
    return jnp.dot(table, values, preferred_element_type=F32).astype(BF16)


def gather(table, scale, terms):
    scaled = scale * terms
    upper = scaled.astype(BF16)
    lower = (scaled - upper.astype(F32)).astype(BF16)
    both = jnp.concatenate([upper, lower], axis=0)
    return jnp.dot(table, both, preferred_element_type=F32)


def loading_kernel(codes, opening, low, low_turned, done):
    half = low.shape[0]
    copies = []
    for chunk in range(half // CHUNK):
        span = pl.ds(chunk * CHUNK, CHUNK)
        copies.append(pltpu.make_async_copy(codes.at[span], low.at[span], done.at[chunk]))
        copies[-1].start()
    for chunk, copy in enumerate(copies):
        copy.wait()
        for k in range(chunk * CHUNK, (chunk + 1) * CHUNK):
            low_turned[k] = low[k].T


def opening_kernel(start, weight, named, out, sources, weights, names, done):
    copies = [
        pltpu.make_async_copy(start, sources, done.at[0]),
        pltpu.make_async_copy(weight, weights, done.at[1]),
        pltpu.make_async_copy(named, names, done.at[2]),
    ]
    for copy in copies:
        copy.start()
    blocks, width = sources.shape
    slots, count = names.shape
    rest = out.shape[0] - 2 * blocks
    out[2 * blocks :, :] = jnp.zeros((rest, width), F32)
    for copy in copies:
        copy.wait()
    out[:blocks, :] = sources[...]
    out[blocks : 2 * blocks, :] = weights[...]
    out[2 * blocks : 2 * blocks + slots, :count] = names[...].astype(F32)


def first_kernel(blocks, slots, count, *refs):
    codes, low_turned, scale, row, column, place = refs[:6]
    parts = refs[6 : 6 + count]
    (out, high, high_turned, rows_pick, rows_pair, source_pick, source_pair, wide_scale) = refs[
        6 + count : 14 + count
    ]
    start, weight, done = refs[14 + count :]
    half = low_turned.shape[0]
    copies = []
    for chunk in range(high.shape[0] // CHUNK):
        copies.append(
            pltpu.make_async_copy(
                codes.at[pl.ds(half + chunk * CHUNK, CHUNK)],
                high.at[pl.ds(chunk * CHUNK, CHUNK)],
                done.at[chunk],
            )
        )
        copies[-1].start()
    tiles = scale.shape[1]
    width = out.shape[1]
    data_rows = out.shape[0]
    here = place[0]
    columns_of = column[...]
    source = jnp.where(columns_of < blocks, columns_of, 0)
    lane = lax.broadcasted_iota(jnp.int32, (1, width), 1)
    for shift in range(count):
        other = jnp.bitwise_xor(here, shift)
        for slot in range(slots):
            named = parts[shift][2 * blocks + slot : 2 * blocks + slot + 1, :]
            mine = jnp.where(lane == here, named, 0.0)
            block = jnp.sum(mine, axis=1, keepdims=True).astype(jnp.int32) + shift * blocks
            source = jnp.where(columns_of == blocks + other * slots + slot, block, source)

    def tables(index, values, picks, pairs):
        hits = lax.broadcasted_iota(jnp.int32, (values, tiles), 0) == index
        ones = jnp.where(hits, 1.0, 0.0)
        turned = ones.T.astype(BF16)
        picks[...] = turned
        pairs[...] = jnp.concatenate([ones, ones], axis=1).astype(BF16)
        return turned

    source_table = tables(source, count * blocks, source_pick, source_pair)
    field = jnp.concatenate([part[:blocks, :] for part in parts], axis=0)
    start[...] = field
    weight[...] = jnp.concatenate([part[blocks : 2 * blocks, :] for part in parts], axis=0)
    tables(row[...], data_rows, rows_pick, rows_pair)
    square = (tiles, tiles)
    same = lax.broadcasted_iota(jnp.int32, square, 0) == lax.broadcasted_iota(jnp.int32, square, 1)
    scales = jnp.dot(
        jnp.where(same, scale[...], 0.0),
        jnp.ones((tiles, width), F32),
        precision=HIGH,
        preferred_element_type=F32,
    )
    wide_scale[...] = scales

    def tile_of(k):
        if k < half:
            return low_turned[k]
        k -= half
        if k % CHUNK == 0:
            copies[k // CHUNK].wait()
        tile = high[k].T
        high_turned[k] = tile
        return tile

    terms = products(tile_of, pick(source_table, field.astype(BF16)))
    out[...] = gather(rows_pair[...], scales, terms)


def start_data_kernel(count, *refs):
    low, high, rows_pick, source_pair, scale, observed, data_weight = refs[:7]
    parts = refs[7 : 7 + count]
    out = refs[7 + count]
    total = total_rows(parts)
    data = (data_weight[...] * (observed[...] - total)).astype(BF16)
    terms = products(kept_tiles(low, high), pick(rows_pick[...], data))
    out[...] = gather(source_pair[...], scale[...], terms)


def start_residual_kernel(blocks, count, *refs):
    low, high, source_pick, rows_pair, scale, start, weight = refs[:7]
    parts = refs[7 : 7 + count]
    out, residual = refs[7 + count :]
    weights = weight[...]
    value = total_blocks(parts, blocks) - weights * start[...]
    residual[...] = value
    terms = products(kept_tiles(low, high), pick(source_pick[...], value.astype(BF16)))
    data_rows = rows_pair.shape[0]
    out[:data_rows, :] = gather(rows_pair[...], scale[...], terms)
    out[data_rows:, :] = pack_rows(
        [columns(value * value), columns(value * weights * value)], value.shape[1]
    )


def image_data_kernel(count, *refs):
    low, high, rows_pick, source_pair, scale, data_weight = refs[:6]
    parts = refs[6 : 6 + count]
    out, predicted, sums = refs[6 + count :]
    data_rows = data_weight.shape[0]
    whole_part = total_rows(parts)
    total = whole_part[:data_rows, :]
    predicted[...] = total
    sums[...] = whole_part[data_rows:, :]
    data = (data_weight[...] * (0.0 - total)).astype(BF16)
    terms = products(kept_tiles(low, high), pick(rows_pick[...], data))
    cells = source_pair.shape[0]
    out[:cells, :] = gather(source_pair[...], scale[...], terms)
    out[cells:, :] = pack_rows([columns(total * data.astype(F32))], total.shape[1])


def residual_kernel(blocks, count, *refs):
    low, high, source_pick, rows_pair, scale, weight, direction, sums = refs[:8]
    parts = refs[8 : 8 + count]
    out, residual, step = refs[8 + count :]
    cells = source_pick.shape[1]
    weights = weight[...]
    along = direction[...]
    image = weights * along - total_blocks(parts, blocks)
    curve = whole(sums[1:2, :]) - whole(extra_rows(parts, cells)[0:1, :])
    alpha = whole(sums[0:1, :]) / curve
    step[...] = jnp.broadcast_to(alpha, step.shape)
    value = residual_of(along, alpha, image)
    residual[...] = value
    terms = products(kept_tiles(low, high), pick(source_pick[...], value.astype(BF16)))
    data_rows = rows_pair.shape[0]
    out[:data_rows, :] = gather(rows_pair[...], scale[...], terms)
    weighted = value * weights
    out[data_rows:, :] = pack_rows(
        [columns(value * value), columns(weighted * value), columns(weighted * along)],
        value.shape[1],
    )


def residual_of(residual, alpha, image):
    return residual - alpha * image


def second_data_kernel(blocks, count, *refs):
    low, high, rows_pick, source_pair, scale, data_weight, predicted, sums = refs[:8]
    parts = refs[8 : 8 + count]
    outs, scalars = refs[8 + count : -1], refs[-1]
    data_rows = data_weight.shape[0]
    whole_part = total_rows(parts)
    norm = whole(whole_part[data_rows : data_rows + 1, :])
    beta = norm / whole(sums[0:1, :])
    curve = whole(
        whole_part[data_rows + 1 : data_rows + 2, :]
        + 2.0 * beta * whole_part[data_rows + 2 : data_rows + 3, :]
        + beta * beta * sums[1:2, :]
    )
    total = whole_part[:data_rows, :] + beta * predicted[...]
    data = (data_weight[...] * (0.0 - total)).astype(BF16)
    terms = products(kept_tiles(low, high), pick(rows_pick[...], data))
    cells = gather(source_pair[...], scale[...], terms)
    curved = columns(total * data.astype(F32))
    for group, out in enumerate(outs):
        out[:blocks, :] = cells[group * blocks : (group + 1) * blocks, :]
        out[blocks:, :] = jnp.broadcast_to(curved, (out.shape[0] - blocks, total.shape[1]))
    wide = (1, scalars.shape[1])
    scalars[...] = pack_rows(
        [jnp.broadcast_to(value, wide) for value in (norm, beta, curve)], scalars.shape[1]
    )


def last_kernel(blocks, count, *refs):
    weight, start, first, second, step, scalars = refs[:6]
    parts = refs[6 : 6 + count]
    model, residual = refs[6 + count :]
    norm = scalars[0:1, 0:1]
    beta = scalars[1:2, 0:1]
    curve = scalars[2:3, 0:1]
    along = first[:blocks, :]
    left = second[:blocks, :]
    direction = left + beta * along
    whole_part = total_rows(parts)
    image = weight[:blocks, :] * direction - whole_part[:blocks, :]
    alpha = norm / (curve - whole(whole_part[blocks : blocks + 1, :]))
    model[...] = start[:blocks, :] + step[0:1, 0:1] * along + alpha * direction
    residual[...] = left - alpha * image


def call(body, outs, *args, scratch=()):
    specs = []
    for arg in args:
        far = getattr(jax.typeof(arg), "memory_space", None) == pltpu.HBM
        space = pl.ANY if far else pltpu.SMEM if arg.ndim == 1 else pltpu.VMEM
        specs.append(pl.BlockSpec(memory_space=space))
    return pl.pallas_call(
        body,
        out_shape=[jax.ShapeDtypeStruct(shape, dtype) for shape, dtype in outs],
        in_specs=specs,
        out_specs=[pl.BlockSpec(memory_space=pltpu.VMEM)] * len(outs),
        scratch_shapes=list(scratch),
        compiler_params=pltpu.CompilerParams(vmem_limit_bytes=LIMIT),
    )(*args)


def shards(
    tile_codes,
    tile_scale,
    tile_row,
    tile_column,
    send_index,
    model_start,
    reg_weight,
    observed,
    data_weight,
):
    blocks, width = model_start.shape
    slots = send_index.shape[2]
    data_rows = observed.shape[0]
    tiles = tile_codes.shape[0]
    count = lax.axis_size("tiles")
    sharing = lax.axis_size(("split", "depth"))
    cells = count * blocks
    half = tiles // 2
    codes = pltpu.with_memory_space_constraint(tile_codes, pltpu.HBM)
    half_shape = (half, width, width)
    place = lax.axis_index("tiles").astype(jnp.int32).reshape(1)

    def across(values):
        return exchange(values, "tiles", count)

    def within(value):
        return exchange([value] * sharing, ("split", "depth"), sharing)

    named = jnp.transpose(send_index, (0, 2, 1)).reshape(slots, count)
    (opening,) = call(
        opening_kernel,
        [((2 * blocks + EXTRA, width), F32)],
        pltpu.with_memory_space_constraint(model_start, pltpu.HBM),
        pltpu.with_memory_space_constraint(reg_weight, pltpu.HBM),
        pltpu.with_memory_space_constraint(named, pltpu.HBM),
        scratch=[
            pltpu.VMEM((blocks, width), F32),
            pltpu.VMEM((blocks, width), F32),
            pltpu.VMEM((slots, count), jnp.int32),
            pltpu.SemaphoreType.DMA((3,)),
        ],
    )
    begin = across([opening] * count)
    low, low_turned = call(
        loading_kernel,
        [(half_shape, BF16)] * 2,
        codes,
        opening,
        scratch=[pltpu.SemaphoreType.DMA((half // CHUNK,))],
    )
    (part, high, high_turned, rows_pick, rows_pair, source_pick, source_pair, scale, start, weight) = call(
        functools.partial(first_kernel, blocks, slots, count),
        [
            ((data_rows, width), F32),
            (half_shape, BF16),
            (half_shape, BF16),
            ((tiles, data_rows), BF16),
            ((data_rows, 2 * tiles), BF16),
            ((tiles, cells), BF16),
            ((cells, 2 * tiles), BF16),
            ((tiles, width), F32),
            ((cells, width), F32),
            ((cells, width), F32),
        ],
        codes,
        low_turned,
        tile_scale.reshape(1, -1),
        tile_row.reshape(1, -1),
        tile_column.reshape(1, -1),
        place,
        *begin,
        scratch=[pltpu.SemaphoreType.DMA((half // CHUNK,))],
    )
    (part,) = call(
        functools.partial(start_data_kernel, sharing),
        [((cells, width), F32)],
        low,
        high,
        rows_pick,
        source_pair,
        scale,
        observed,
        data_weight,
        *within(part),
    )
    part, first = call(
        functools.partial(start_residual_kernel, blocks, count),
        [((data_rows + EXTRA, width), F32), ((cells, width), F32)],
        low_turned,
        high_turned,
        source_pick,
        rows_pair,
        scale,
        start,
        weight,
        *across([part] * count),
    )
    part, predicted, sums = call(
        functools.partial(image_data_kernel, sharing),
        [((cells + EXTRA, width), F32), ((data_rows, width), F32), ((EXTRA, width), F32)],
        low,
        high,
        rows_pick,
        source_pair,
        scale,
        data_weight,
        *within(part),
    )
    part, second, step = call(
        functools.partial(residual_kernel, blocks, count),
        [((data_rows + EXTRA, width), F32), ((cells, width), F32), ((8, 128), F32)],
        low_turned,
        high_turned,
        source_pick,
        rows_pair,
        scale,
        weight,
        first,
        sums,
        *across([part] * count),
    )
    *part, scalars = call(
        functools.partial(second_data_kernel, blocks, sharing),
        [((blocks + 4, width), F32)] * count + [((EXTRA, width), F32)],
        low,
        high,
        rows_pick,
        source_pair,
        scale,
        data_weight,
        predicted,
        sums,
        *within(part),
    )
    model, residual = call(
        functools.partial(last_kernel, blocks, count),
        [((blocks, width), F32), ((blocks, width), F32)],
        weight,
        start,
        first,
        second,
        step,
        scalars,
        *across(part),
    )
    return (model, residual)


def solution(mesh):
    both = P(("groups", "tiles", "split", "depth"))
    owned = P(("groups", "tiles", "split", "depth"), None)
    wide = P(("groups", "tiles", "split", "depth"), None, None)
    data = P(("groups", "tiles"), None)
    in_specs = (wide, both, both, both, wide, owned, owned, data, data)
    return jax.shard_map(
        shards, mesh=mesh, in_specs=in_specs, out_specs=(owned, owned), check_vma=False
    )
```

profile of v0, /device:TPU:0, one launch (start us, length us, event | category | flops | bytes accessed | tf_op | source)
XLA Modules:
  0.0 56.6 jit_solution(1679814199448495279)
XLA Ops:
  0.6 0.7 %shard_map.104.opening.refs_6_ = f32[16,256]{1,0:T(8,128)S(1)} custom-call(f32[4,256]{1,0:T(4,128)} %start.1, f32[4,256]{1,0:T(4,128)} %weight.1, s32[2,4]{1,0:T(2,128)} %bitcast.10), custom_call_target="tpu_custom_call" | custom-call | tf_op jit(solution)/shard_map/pallas_call | solution.py:320
  1.4 5.1 %collective-permute-start.2 = (f32[16,256]{1,0:T(8,128)S(1)}, f32[16,256]{1,0:T(8,128)S(1)}, u32[]{:S(2)}, u32[]{:S(2)}) collective-permute-start(f32[16,256]{1,0:T(8,128)S(1)} %shard_map.104.opening.refs_6_), channel_id=1, source_target_pairs={{0,12},{4,8},{8,4},{12,0},{1,13},{5,9},{9,5},{13,1},{2,14},{6,10},... | collective-permute-start | bytes 49160 | tf_op jit(solution)/shard_map/ppermute | solution.py:23
  6.5 0.0 collective-permute-start.1
  6.5 0.6 %collective-permute-start = (f32[16,256]{1,0:T(8,128)S(1)}, f32[16,256]{1,0:T(8,128)S(1)}, u32[]{:S(2)}, u32[]{:S(2)}) collective-permute-start(f32[16,256]{1,0:T(8,128)S(1)} %shard_map.104.opening.refs_6_), channel_id=1, source_target_pairs={{0,4},{4,0},{8,12},{12,8},{1,5},{5,1},{9,13},{13,9},{2,6},{6,2},{1... | collective-permute-start | bytes 49160 | tf_op jit(solution)/shard_map/ppermute | solution.py:23
  7.1 0.0 copy-start.2
  7.1 0.0 copy-start.3
  7.1 0.0 copy-start.4
  7.1 2.6 %shard_map.105 = (bf16[32,256,256]{2,1,0:T(8,128)(2,1)S(1)}, bf16[32,256,256]{2,1,0:T(8,128)(2,1)S(1)}) custom-call(bf16[64,256,256]{2,1,0:T(8,128)(2,1)} %refs_0_.1, f32[16,256]{1,0:T(8,128)S(1)} %shard_map.104.opening.refs_6_), custom_call_target="tpu_custom_call" | custom-call | tf_op jit(solution)/shard_map/pallas_call | solution.py:320
  9.8 0.0 collective-permute-done.2.refs_9_
  9.8 1.4 %collective-permute-done.1.refs_8_ = f32[16,256]{1,0:T(8,128)S(1)} collective-permute-done((f32[16,256]{1,0:T(8,128)S(1)}, f32[16,256]{1,0:T(8,128)S(1)}, u32[]{:S(2)}, u32[]{:S(2)}) %collective-permute-start.1) | collective-permute-done | bytes 16416 | tf_op jit(solution)/shard_map/ppermute | solution.py:23
  11.1 0.0 collective-permute-done.refs_7_
  11.1 0.0 copy-done.2
  11.1 0.0 copy-done.3
  11.1 0.0 copy-done.4
  11.2 0.0 copy-start
  11.2 0.0 copy-start.1
  11.2 3.6 %shard_map.106 = (f32[16,256]{1,0:T(8,128)S(1)}, bf16[32,256,256]{2,1,0:T(8,128)(2,1)S(1)}, bf16[32,256,256]{2,1,0:T(8,128)(2,1)S(1)}, bf16[64,16]{1,0:T(8,128)(...) custom-call(bf16[64,256,256]{2,1,0:T(8,128)(2,1)} %refs_0_.1, ...), custom_call_target="tpu_custom_call" | custom-call | tf_op jit(solution)/shard_map/pallas_call | solution.py:320
  14.8 0.1 collective-permute-start.5
  14.8 1.6 %collective-permute-start.4 = (f32[16,256]{1,0:T(8,128)S(1)}, f32[16,256]{1,0:T(8,128)S(1)}, u32[]{:S(2)}, u32[]{:S(2)}) collective-permute-start(f32[16,256]{1,0:T(8,128)S(1)} %get-tuple-element.38.refs_7_), channel_id=1, source_target_pairs={{0,2},{1,3},{2,0},{3,1},{4,6},{5,7},{6,4},{7,5},{8,10},{9,11},{10,... | collective-permute-start | bytes 49160 | tf_op jit(solution)/shard_map/ppermute | solution.py:23
  16.4 0.3 collective-permute-start.3
  16.7 1.4 %collective-permute-done.5.refs_10_ = f32[16,256]{1,0:T(8,128)S(1)} collective-permute-done((f32[16,256]{1,0:T(8,128)S(1)}, f32[16,256]{1,0:T(8,128)S(1)}, u32[]{:S(2)}, u32[]{:S(2)}) %collective-permute-start.5) | collective-permute-done | bytes 16416 | tf_op jit(solution)/shard_map/ppermute | solution.py:23
  18.1 0.5 collective-permute-done.4.refs_9_
  18.7 0.0 collective-permute-done.3.refs_8_
  18.7 0.0 copy-done
  18.7 0.0 copy-done.1
  18.7 1.4 %shard_map.107.refs_7_ = f32[16,256]{1,0:T(8,128)S(1)} custom-call(bf16[32,256,256]{2,1,0:T(8,128)(2,1)S(1)} %get-tuple-element.34.refs_0_, bf16[32,256,256]{2,1,0:T(8,128)(2,1)S(1)} %get-tuple-element.35.refs_1_, bf16[64,16]{1,0:T(8,128)(2,1)S(1)} %get-tuple-element.36.refs_2_, bf16[16,128]{1,0:T(8,128)(2,1)S(1)} %get-tuple-element.37.refs_3_, ...), custom_call_target="tpu_custom_call" | custom-call | tf_op jit(solution)/shard_map/pallas_call | solution.py:320
  20.1 2.4 %collective-permute-start.8 = (f32[16,256]{1,0:T(8,128)S(1)}, f32[16,256]{1,0:T(8,128)S(1)}, u32[]{:S(2)}, u32[]{:S(2)}) collective-permute-start(f32[16,256]{1,0:T(8,128)S(1)} %shard_map.107.refs_7_), channel_id=1, source_target_pairs={{0,12},{4,8},{8,4},{12,0},{1,13},{5,9},{9,5},{13,1},{2,14},{6,10},... | collective-permute-start | bytes 49160 | tf_op jit(solution)/shard_map/ppermute | solution.py:23
  22.5 0.0 collective-permute-start.7
  22.5 2.0 %collective-permute-start.6 = (f32[16,256]{1,0:T(8,128)S(1)}, f32[16,256]{1,0:T(8,128)S(1)}, u32[]{:S(2)}, u32[]{:S(2)}) collective-permute-start(f32[16,256]{1,0:T(8,128)S(1)} %shard_map.107.refs_7_), channel_id=1, source_target_pairs={{0,4},{4,0},{8,12},{12,8},{1,5},{5,1},{9,13},{13,9},{2,6},{6,2},{1... | collective-permute-start | bytes 49160 | tf_op jit(solution)/shard_map/ppermute | solution.py:23
  24.5 1.1 %collective-permute-done.8.refs_10_ = f32[16,256]{1,0:T(8,128)S(1)} collective-permute-done((f32[16,256]{1,0:T(8,128)S(1)}, f32[16,256]{1,0:T(8,128)S(1)}, u32[]{:S(2)}, u32[]{:S(2)}) %collective-permute-start.8) | collective-permute-done | bytes 16416 | tf_op jit(solution)/shard_map/ppermute | solution.py:23
  25.7 1.5 %collective-permute-done.7.refs_9_ = f32[16,256]{1,0:T(8,128)S(1)} collective-permute-done((f32[16,256]{1,0:T(8,128)S(1)}, f32[16,256]{1,0:T(8,128)S(1)}, u32[]{:S(2)}, u32[]{:S(2)}) %collective-permute-start.7) | collective-permute-done | bytes 16416 | tf_op jit(solution)/shard_map/ppermute | solution.py:23
  27.2 0.0 collective-permute-done.6.refs_8_
  27.2 1.4 %shard_map.108 = (f32[24,256]{1,0:T(8,128)S(1)}, f32[16,256]{1,0:T(8,128)S(1)}) custom-call(bf16[32,256,256]{2,1,0:T(8,128)(2,1)S(1)} %get-tuple-element.27.refs_1_.refs_0_, bf16[32,256,256]{2,1,0:T(8,128)(2,1)S(1)} %get-tuple-element.30.refs_1_, bf16[64,16]{1,0:T(8,128)(2,1)S(1)} %get-tuple-element.31.refs_2_, ...), custom_call_target="tpu_custom_call" | custom-call | tf_op jit(solution)/shard_map/pallas_call | solution.py:320
  28.6 0.0 collective-permute-start.11
  28.6 1.5 %collective-permute-start.10 = (f32[24,256]{1,0:T(8,128)S(1)}, f32[24,256]{1,0:T(8,128)S(1)}, u32[]{:S(2)}, u32[]{:S(2)}) collective-permute-start(f32[24,256]{1,0:T(8,128)S(1)} %get-tuple-element.40.refs_6_), channel_id=1, source_target_pairs={{0,2},{1,3},{2,0},{3,1},{4,6},{5,7},{6,4},{7,5},{8,10},{9,11},{10,... | collective-permute-start | bytes 73736 | tf_op jit(solution)/shard_map/ppermute | solution.py:23
  30.1 0.3 collective-permute-start.9
  30.5 1.6 %collective-permute-done.11.refs_9_ = f32[24,256]{1,0:T(8,128)S(1)} collective-permute-done((f32[24,256]{1,0:T(8,128)S(1)}, f32[24,256]{1,0:T(8,128)S(1)}, u32[]{:S(2)}, u32[]{:S(2)}) %collective-permute-start.11) | collective-permute-done | bytes 24608 | tf_op jit(solution)/shard_map/ppermute | solution.py:23
  32.1 0.4 collective-permute-done.10.refs_8_
  32.5 0.0 collective-permute-done.9.refs_7_
  32.5 1.4 %shard_map.109 = (f32[24,256]{1,0:T(8,128)S(1)}, f32[16,256]{1,0:T(8,128)S(1)}, f32[8,256]{1,0:T(8,128)S(1)}) custom-call(bf16[32,256,256]{2,1,0:T(8,128)(2,1)S(1)} %get-tuple-element.34.refs_0_, bf16[32,256,256]{2,1,0:T(8,128)(2,1)S(1)} %get-tuple-element.35.refs_1_, bf16[64,16]{1,0:T(8,128)(2,1)S(1)} %get-tuple-element.36.refs_2_, ...), custom_call_target="tpu_custom_call" | custom-call | tf_op jit(solution)/shard_map/pallas_call | solution.py:320
  33.9 1.7 %collective-permute-start.14 = (f32[24,256]{1,0:T(8,128)S(1)}, f32[24,256]{1,0:T(8,128)S(1)}, u32[]{:S(2)}, u32[]{:S(2)}) collective-permute-start(f32[24,256]{1,0:T(8,128)S(1)} %get-tuple-element.42.refs_8_), channel_id=1, source_target_pairs={{0,12},{4,8},{8,4},{12,0},{1,13},{5,9},{9,5},{13,1},{2,14},{6,10},... | collective-permute-start | bytes 73736 | tf_op jit(solution)/shard_map/ppermute | solution.py:23
  35.6 0.9 %collective-permute-start.13 = (f32[24,256]{1,0:T(8,128)S(1)}, f32[24,256]{1,0:T(8,128)S(1)}, u32[]{:S(2)}, u32[]{:S(2)}) collective-permute-start(f32[24,256]{1,0:T(8,128)S(1)} %get-tuple-element.42.refs_8_), channel_id=1, source_target_pairs={{0,8},{4,12},{8,0},{12,4},{1,9},{5,13},{9,1},{13,5},{2,10},{6,14},... | collective-permute-start | bytes 73736 | tf_op jit(solution)/shard_map/ppermute | solution.py:23
  36.5 1.8 %collective-permute-start.12 = (f32[24,256]{1,0:T(8,128)S(1)}, f32[24,256]{1,0:T(8,128)S(1)}, u32[]{:S(2)}, u32[]{:S(2)}) collective-permute-start(f32[24,256]{1,0:T(8,128)S(1)} %get-tuple-element.42.refs_8_), channel_id=1, source_target_pairs={{0,4},{4,0},{8,12},{12,8},{1,5},{5,1},{9,13},{13,9},{2,6},{6,2},{1... | collective-permute-start | bytes 73736 | tf_op jit(solution)/shard_map/ppermute | solution.py:23
  38.3 1.4 %collective-permute-done.14.refs_11_ = f32[24,256]{1,0:T(8,128)S(1)} collective-permute-done((f32[24,256]{1,0:T(8,128)S(1)}, f32[24,256]{1,0:T(8,128)S(1)}, u32[]{:S(2)}, u32[]{:S(2)}) %collective-permute-start.14) | collective-permute-done | bytes 24608 | tf_op jit(solution)/shard_map/ppermute | solution.py:23
  39.8 0.6 collective-permute-done.13.refs_10_
  40.3 0.2 collective-permute-done.12.refs_9_
  40.6 1.5 %shard_map.110 = (f32[24,256]{1,0:T(8,128)S(1)}, f32[16,256]{1,0:T(8,128)S(1)}, f32[8,128]{1,0:T(8,128)S(1)}) custom-call(bf16[32,256,256]{2,1,0:T(8,128)(2,1)S(1)} %get-tuple-element.27.refs_1_.refs_0_, bf16[32,256,256]{2,1,0:T(8,128)(2,1)S(1)} %get-tuple-element.30.refs_1_, bf16[64,16]{1,0:T(8,128)(2,1)S(1)} %get-tuple-element.31.refs_2_, ...), custom_call_target="tpu_custom_call" | custom-call | tf_op jit(solution)/shard_map/pallas_call | solution.py:320
  42.1 0.0 collective-permute-start.17
  42.1 1.5 %collective-permute-start.16 = (f32[24,256]{1,0:T(8,128)S(1)}, f32[24,256]{1,0:T(8,128)S(1)}, u32[]{:S(2)}, u32[]{:S(2)}) collective-permute-start(f32[24,256]{1,0:T(8,128)S(1)} %get-tuple-element.46.refs_8_), channel_id=1, source_target_pairs={{0,2},{1,3},{2,0},{3,1},{4,6},{5,7},{6,4},{7,5},{8,10},{9,11},{10,... | collective-permute-start | bytes 73736 | tf_op jit(solution)/shard_map/ppermute | solution.py:23
  43.6 0.4 collective-permute-start.15
  44.0 1.7 %collective-permute-done.17.refs_11_ = f32[24,256]{1,0:T(8,128)S(1)} collective-permute-done((f32[24,256]{1,0:T(8,128)S(1)}, f32[24,256]{1,0:T(8,128)S(1)}, u32[]{:S(2)}, u32[]{:S(2)}) %collective-permute-start.17) | collective-permute-done | bytes 24608 | tf_op jit(solution)/shard_map/ppermute | solution.py:23
  45.6 0.4 collective-permute-done.16.refs_10_
  46.0 0.0 collective-permute-done.15.refs_9_
  46.0 1.6 %shard_map.111 = (f32[8,256]{1,0:T(8,128)S(1)}, f32[8,256]{1,0:T(8,128)S(1)}, f32[8,256]{1,0:T(8,128)S(1)}, f32[8,256]{1,0:T(8,128)S(1)}, f32[8,256]{1,0:T(8,128)S(1)}) custom-call(bf16[32,256,256]{2,1,0:T(8,128)(2,1)S(1)} %get-tuple-element.34.refs_0_, bf16[32,256,256]{2,1,0:T(8,128)(2,1)S(1)} %get-tuple-element.35.refs_1_, ...), custom_call_target="tpu_custom_call" | custom-call | tf_op jit(solution)/shard_map/pallas_call | solution.py:320
  47.5 1.6 %collective-permute-start.18 = (f32[8,256]{1,0:T(8,128)S(1)}, f32[8,256]{1,0:T(8,128)S(1)}, u32[]{:S(2)}, u32[]{:S(2)}) collective-permute-start(f32[8,256]{1,0:T(8,128)S(1)} %get-tuple-element.49), channel_id=1, source_target_pairs={{0,4},{4,0},{8,12},{12,8},{1,5},{5,1},{9,13},{13,9},{2,6},{6,2},{1... | collective-permute-start | bytes 24584 | tf_op jit(solution)/shard_map/ppermute | solution.py:23
  49.2 1.2 %collective-permute-start.19 = (f32[8,256]{1,0:T(8,128)S(1)}, f32[8,256]{1,0:T(8,128)S(1)}, u32[]{:S(2)}, u32[]{:S(2)}) collective-permute-start(f32[8,256]{1,0:T(8,128)S(1)} %get-tuple-element.50), channel_id=1, source_target_pairs={{0,8},{4,12},{8,0},{12,4},{1,9},{5,13},{9,1},{13,5},{2,10},{6,14},... | collective-permute-start | bytes 24584 | tf_op jit(solution)/shard_map/ppermute | solution.py:23
  50.3 1.6 %collective-permute-start.20 = (f32[8,256]{1,0:T(8,128)S(1)}, f32[8,256]{1,0:T(8,128)S(1)}, u32[]{:S(2)}, u32[]{:S(2)}) collective-permute-start(f32[8,256]{1,0:T(8,128)S(1)} %get-tuple-element.51), channel_id=1, source_target_pairs={{0,12},{4,8},{8,4},{12,0},{1,13},{5,9},{9,5},{13,1},{2,14},{6,10},... | collective-permute-start | bytes 24584 | tf_op jit(solution)/shard_map/ppermute | solution.py:23
  52.0 0.0 collective-permute-done.18.refs_7_
  52.0 1.8 %collective-permute-done.19.refs_8_ = f32[8,256]{1,0:T(8,128)S(1)} collective-permute-done((f32[8,256]{1,0:T(8,128)S(1)}, f32[8,256]{1,0:T(8,128)S(1)}, u32[]{:S(2)}, u32[]{:S(2)}) %collective-permute-start.19) | collective-permute-done | bytes 8224 | tf_op jit(solution)/shard_map/ppermute | solution.py:23
  53.7 2.1 %collective-permute-done.20.refs_9_ = f32[8,256]{1,0:T(8,128)S(1)} collective-permute-done((f32[8,256]{1,0:T(8,128)S(1)}, f32[8,256]{1,0:T(8,128)S(1)}, u32[]{:S(2)}, u32[]{:S(2)}) %collective-permute-start.20) | collective-permute-done | bytes 8224 | tf_op jit(solution)/shard_map/ppermute | solution.py:23
  55.8 0.8 %shard_map.112 = (f32[4,256]{1,0:T(4,128)}, f32[4,256]{1,0:T(4,128)}) custom-call(f32[16,256]{1,0:T(8,128)S(1)} %get-tuple-element.28.refs_6_.refs_5_.refs_0_, f32[16,256]{1,0:T(8,128)S(1)} %get-tuple-element.29.refs_5_.refs_1_, f32[16,256]{1,0:T(8,128)S(1)} %get-tuple-element.39.refs_6_.refs_2_, f32[16,256]{1,0:T(8,128)S(1)} %get-tuple-element.43.refs_3_, ...), custom_call_target="tpu_custom_call" | custom-call | tf_op jit(solution)/shard_map/pallas_call | solution.py:320
Async XLA Ops:
  1.4 8.4 %collective-permute-start.2 = (f32[16,256]{1,0:T(8,128)S(1)}, f32[16,256]{1,0:T(8,128)S(1)}, u32[]{:S(2)}, u32[]{:S(2)}) collective-permute-start(f32[16,256]{1,0:T(8,128)S(1)} %shard_map.104.opening.refs_6_), channel_id=1, source_target_pairs={{0,12},{4,8},{8,4},{12,0},{1,13},{5,9},{9,5},{13,1},{2,14},{6,10},... | collective-permute-start | bytes 49160 | tf_op jit(solution)/shard_map/ppermute | solution.py:23
  6.5 4.6 %collective-permute-start.1 = (f32[16,256]{1,0:T(8,128)S(1)}, f32[16,256]{1,0:T(8,128)S(1)}, u32[]{:S(2)}, u32[]{:S(2)}) collective-permute-start(f32[16,256]{1,0:T(8,128)S(1)} %shard_map.104.opening.refs_6_), channel_id=1, source_target_pairs={{0,8},{4,12},{8,0},{12,4},{1,9},{5,13},{9,1},{13,5},{2,10},{6,14},... | collective-permute-start | bytes 49160 | tf_op jit(solution)/shard_map/ppermute | solution.py:23
  6.5 4.6 %collective-permute-start = (f32[16,256]{1,0:T(8,128)S(1)}, f32[16,256]{1,0:T(8,128)S(1)}, u32[]{:S(2)}, u32[]{:S(2)}) collective-permute-start(f32[16,256]{1,0:T(8,128)S(1)} %shard_map.104.opening.refs_6_), channel_id=1, source_target_pairs={{0,4},{4,0},{8,12},{12,8},{1,5},{5,1},{9,13},{13,9},{2,6},{6,2},{1... | collective-permute-start | bytes 49160 | tf_op jit(solution)/shard_map/ppermute | solution.py:23
  7.1 4.0 %copy-start.2 = (f32[64]{0:T(128)S(1)}, f32[64]{0:T(128)}, u32[]{:S(2)}) copy-start(f32[64]{0:T(128)} %param.10) | copy-start | bytes 772
  7.1 4.0 %copy-start.3 = (s32[64]{0:T(128)S(1)}, s32[64]{0:T(128)}, u32[]{:S(2)}) copy-start(s32[64]{0:T(128)} %param.11) | copy-start | bytes 772
  7.1 4.0 %copy-start.4 = (s32[64]{0:T(128)S(1)}, s32[64]{0:T(128)}, u32[]{:S(2)}) copy-start(s32[64]{0:T(128)} %param.12) | copy-start | bytes 772
  11.2 7.5 %copy-start = (f32[16,256]{1,0:T(8,128)S(1)}, f32[16,256]{1,0:T(8,128)}, u32[]{:S(2)}) copy-start(f32[16,256]{1,0:T(8,128)} %refs_5_.5) | copy-start | bytes 49156
  11.2 7.5 %copy-start.1 = (f32[16,256]{1,0:T(8,128)S(1)}, f32[16,256]{1,0:T(8,128)}, u32[]{:S(2)}) copy-start(f32[16,256]{1,0:T(8,128)} %refs_5_.3) | copy-start | bytes 49156
  14.8 3.4 %collective-permute-start.5 = (f32[16,256]{1,0:T(8,128)S(1)}, f32[16,256]{1,0:T(8,128)S(1)}, u32[]{:S(2)}, u32[]{:S(2)}) collective-permute-start(f32[16,256]{1,0:T(8,128)S(1)} %get-tuple-element.38.refs_7_), channel_id=1, source_target_pairs={{0,3},{1,2},{2,1},{3,0},{4,7},{5,6},{6,5},{7,4},{8,11},{9,10},{10,... | collective-permute-start | bytes 49160 | tf_op jit(solution)/shard_map/ppermute | solution.py:23
  14.8 3.8 %collective-permute-start.4 = (f32[16,256]{1,0:T(8,128)S(1)}, f32[16,256]{1,0:T(8,128)S(1)}, u32[]{:S(2)}, u32[]{:S(2)}) collective-permute-start(f32[16,256]{1,0:T(8,128)S(1)} %get-tuple-element.38.refs_7_), channel_id=1, source_target_pairs={{0,2},{1,3},{2,0},{3,1},{4,6},{5,7},{6,4},{7,5},{8,10},{9,11},{10,... | collective-permute-start | bytes 49160 | tf_op jit(solution)/shard_map/ppermute | solution.py:23
  16.4 2.3 %collective-permute-start.3 = (f32[16,256]{1,0:T(8,128)S(1)}, f32[16,256]{1,0:T(8,128)S(1)}, u32[]{:S(2)}, u32[]{:S(2)}) collective-permute-start(f32[16,256]{1,0:T(8,128)S(1)} %get-tuple-element.38.refs_7_), channel_id=1, source_target_pairs={{0,1},{1,0},{2,3},{3,2},{4,5},{5,4},{6,7},{7,6},{8,9},{9,8},{10,11... | collective-permute-start | bytes 49160 | tf_op jit(solution)/shard_map/ppermute | solution.py:23
  20.1 5.6 %collective-permute-start.8 = (f32[16,256]{1,0:T(8,128)S(1)}, f32[16,256]{1,0:T(8,128)S(1)}, u32[]{:S(2)}, u32[]{:S(2)}) collective-permute-start(f32[16,256]{1,0:T(8,128)S(1)} %shard_map.107.refs_7_), channel_id=1, source_target_pairs={{0,12},{4,8},{8,4},{12,0},{1,13},{5,9},{9,5},{13,1},{2,14},{6,10},... | collective-permute-start | bytes 49160 | tf_op jit(solution)/shard_map/ppermute | solution.py:23
  22.5 4.6 %collective-permute-start.7 = (f32[16,256]{1,0:T(8,128)S(1)}, f32[16,256]{1,0:T(8,128)S(1)}, u32[]{:S(2)}, u32[]{:S(2)}) collective-permute-start(f32[16,256]{1,0:T(8,128)S(1)} %shard_map.107.refs_7_), channel_id=1, source_target_pairs={{0,8},{4,12},{8,0},{12,4},{1,9},{5,13},{9,1},{13,5},{2,10},{6,14},... | collective-permute-start | bytes 49160 | tf_op jit(solution)/shard_map/ppermute | solution.py:23
  22.5 4.6 %collective-permute-start.6 = (f32[16,256]{1,0:T(8,128)S(1)}, f32[16,256]{1,0:T(8,128)S(1)}, u32[]{:S(2)}, u32[]{:S(2)}) collective-permute-start(f32[16,256]{1,0:T(8,128)S(1)} %shard_map.107.refs_7_), channel_id=1, source_target_pairs={{0,4},{4,0},{8,12},{12,8},{1,5},{5,1},{9,13},{13,9},{2,6},{6,2},{1... | collective-permute-start | bytes 49160 | tf_op jit(solution)/shard_map/ppermute | solution.py:23
  28.6 3.5 %collective-permute-start.11 = (f32[24,256]{1,0:T(8,128)S(1)}, f32[24,256]{1,0:T(8,128)S(1)}, u32[]{:S(2)}, u32[]{:S(2)}) collective-permute-start(f32[24,256]{1,0:T(8,128)S(1)} %get-tuple-element.40.refs_6_), channel_id=1, source_target_pairs={{0,3},{1,2},{2,1},{3,0},{4,7},{5,6},{6,5},{7,4},{8,11},{9,10},{10,... | collective-permute-start | bytes 73736 | tf_op jit(solution)/shard_map/ppermute | solution.py:23
  28.6 3.9 %collective-permute-start.10 = (f32[24,256]{1,0:T(8,128)S(1)}, f32[24,256]{1,0:T(8,128)S(1)}, u32[]{:S(2)}, u32[]{:S(2)}) collective-permute-start(f32[24,256]{1,0:T(8,128)S(1)} %get-tuple-element.40.refs_6_), channel_id=1, source_target_pairs={{0,2},{1,3},{2,0},{3,1},{4,6},{5,7},{6,4},{7,5},{8,10},{9,11},{10,... | collective-permute-start | bytes 73736 | tf_op jit(solution)/shard_map/ppermute | solution.py:23
  30.1 2.4 %collective-permute-start.9 = (f32[24,256]{1,0:T(8,128)S(1)}, f32[24,256]{1,0:T(8,128)S(1)}, u32[]{:S(2)}, u32[]{:S(2)}) collective-permute-start(f32[24,256]{1,0:T(8,128)S(1)} %get-tuple-element.40.refs_6_), channel_id=1, source_target_pairs={{0,1},{1,0},{2,3},{3,2},{4,5},{5,4},{6,7},{7,6},{8,9},{9,8},{10,11... | collective-permute-start | bytes 73736 | tf_op jit(solution)/shard_map/ppermute | solution.py:23
  33.9 5.8 %collective-permute-start.14 = (f32[24,256]{1,0:T(8,128)S(1)}, f32[24,256]{1,0:T(8,128)S(1)}, u32[]{:S(2)}, u32[]{:S(2)}) collective-permute-start(f32[24,256]{1,0:T(8,128)S(1)} %get-tuple-element.42.refs_8_), channel_id=1, source_target_pairs={{0,12},{4,8},{8,4},{12,0},{1,13},{5,9},{9,5},{13,1},{2,14},{6,10},... | collective-permute-start | bytes 73736 | tf_op jit(solution)/shard_map/ppermute | solution.py:23
  35.6 4.8 %collective-permute-start.13 = (f32[24,256]{1,0:T(8,128)S(1)}, f32[24,256]{1,0:T(8,128)S(1)}, u32[]{:S(2)}, u32[]{:S(2)}) collective-permute-start(f32[24,256]{1,0:T(8,128)S(1)} %get-tuple-element.42.refs_8_), channel_id=1, source_target_pairs={{0,8},{4,12},{8,0},{12,4},{1,9},{5,13},{9,1},{13,5},{2,10},{6,14},... | collective-permute-start | bytes 73736 | tf_op jit(solution)/shard_map/ppermute | solution.py:23
  36.5 4.1 %collective-permute-start.12 = (f32[24,256]{1,0:T(8,128)S(1)}, f32[24,256]{1,0:T(8,128)S(1)}, u32[]{:S(2)}, u32[]{:S(2)}) collective-permute-start(f32[24,256]{1,0:T(8,128)S(1)} %get-tuple-element.42.refs_8_), channel_id=1, source_target_pairs={{0,4},{4,0},{8,12},{12,8},{1,5},{5,1},{9,13},{13,9},{2,6},{6,2},{1... | collective-permute-start | bytes 73736 | tf_op jit(solution)/shard_map/ppermute | solution.py:23
  42.1 3.5 %collective-permute-start.17 = (f32[24,256]{1,0:T(8,128)S(1)}, f32[24,256]{1,0:T(8,128)S(1)}, u32[]{:S(2)}, u32[]{:S(2)}) collective-permute-start(f32[24,256]{1,0:T(8,128)S(1)} %get-tuple-element.46.refs_8_), channel_id=1, source_target_pairs={{0,3},{1,2},{2,1},{3,0},{4,7},{5,6},{6,5},{7,4},{8,11},{9,10},{10,... | collective-permute-start | bytes 73736 | tf_op jit(solution)/shard_map/ppermute | solution.py:23
  42.1 3.9 %collective-permute-start.16 = (f32[24,256]{1,0:T(8,128)S(1)}, f32[24,256]{1,0:T(8,128)S(1)}, u32[]{:S(2)}, u32[]{:S(2)}) collective-permute-start(f32[24,256]{1,0:T(8,128)S(1)} %get-tuple-element.46.refs_8_), channel_id=1, source_target_pairs={{0,2},{1,3},{2,0},{3,1},{4,6},{5,7},{6,4},{7,5},{8,10},{9,11},{10,... | collective-permute-start | bytes 73736 | tf_op jit(solution)/shard_map/ppermute | solution.py:23
  43.6 2.4 %collective-permute-start.15 = (f32[24,256]{1,0:T(8,128)S(1)}, f32[24,256]{1,0:T(8,128)S(1)}, u32[]{:S(2)}, u32[]{:S(2)}) collective-permute-start(f32[24,256]{1,0:T(8,128)S(1)} %get-tuple-element.46.refs_8_), channel_id=1, source_target_pairs={{0,1},{1,0},{2,3},{3,2},{4,5},{5,4},{6,7},{7,6},{8,9},{9,8},{10,11... | collective-permute-start | bytes 73736 | tf_op jit(solution)/shard_map/ppermute | solution.py:23
  47.5 4.4 %collective-permute-start.18 = (f32[8,256]{1,0:T(8,128)S(1)}, f32[8,256]{1,0:T(8,128)S(1)}, u32[]{:S(2)}, u32[]{:S(2)}) collective-permute-start(f32[8,256]{1,0:T(8,128)S(1)} %get-tuple-element.49), channel_id=1, source_target_pairs={{0,4},{4,0},{8,12},{12,8},{1,5},{5,1},{9,13},{13,9},{2,6},{6,2},{1... | collective-permute-start | bytes 24584 | tf_op jit(solution)/shard_map/ppermute | solution.py:23
  49.2 4.5 %collective-permute-start.19 = (f32[8,256]{1,0:T(8,128)S(1)}, f32[8,256]{1,0:T(8,128)S(1)}, u32[]{:S(2)}, u32[]{:S(2)}) collective-permute-start(f32[8,256]{1,0:T(8,128)S(1)} %get-tuple-element.50), channel_id=1, source_target_pairs={{0,8},{4,12},{8,0},{12,4},{1,9},{5,13},{9,1},{13,5},{2,10},{6,14},... | collective-permute-start | bytes 24584 | tf_op jit(solution)/shard_map/ppermute | solution.py:23
  50.3 5.4 %collective-permute-start.20 = (f32[8,256]{1,0:T(8,128)S(1)}, f32[8,256]{1,0:T(8,128)S(1)}, u32[]{:S(2)}, u32[]{:S(2)}) collective-permute-start(f32[8,256]{1,0:T(8,128)S(1)} %get-tuple-element.51), channel_id=1, source_target_pairs={{0,12},{4,8},{8,4},{12,0},{1,13},{5,9},{9,5},{13,1},{2,14},{6,10},... | collective-permute-start | bytes 24584 | tf_op jit(solution)/shard_map/ppermute | solution.py:23
where the time goes:
time: 56.8 us; the launch traced here: 56.6 us
  starting transfers between devices  24.6 us (43%)
  waiting for transfers between devices  16.1 us (28%)
  Pallas kernels  15.1 us (27%)
  between operations  0.73 us (1%)
    ppermute x21, starting transfers between devices, exchange(): parts[shift] = lax.ppermute(values[shift], axes, perm)  24.6 us
    ppermute x21, waiting for transfers between devices, exchange(): parts[shift] = lax.ppermute(values[shift], axes, perm)  16.1 us
    pallas_call x9, Pallas kernels, call(): pl.pallas_call(body, out_shape=[jax.ShapeDtypeStruct(shape, dtype) for sh...  15.1 us
  transfers between devices with their start and end apart: 21, of which 14 were waited for; matrix products, arithmetic and copies ran while one was open for 0% of the time, Pallas kernels for 5%

commit v1 on v0

--- a/solution.py
+++ b/solution.py
@@ -24,6 +24,17 @@
     return parts
 
 
+def doubling(value, axes, size):
+    shift = 1
+    while True:
+        perm = [(i, i ^ shift) for i in range(size)]
+        other = lax.ppermute(value, axes, perm)
+        shift *= 2
+        if shift == size:
+            return value, other
+        value = value + other
+
+
 def total_rows(parts):
     total = parts[0][...]
     for part in parts[1:]:
@@ -31,23 +42,20 @@
     return total
 
 
-def total_blocks(parts, blocks):
-    count = len(parts)
-    groups = []
-    for group in range(count):
-        total = None
-        for shift in range(count):
-            start = (group ^ shift) * blocks
-            piece = parts[shift][start : start + blocks, :]
-            total = piece if total is None else total + piece
-        groups.append(total)
-    return jnp.concatenate(groups, axis=0)
-
-
-def extra_rows(parts, start):
-    total = parts[0][start : start + EXTRA, :]
-    for part in parts[1:]:
-        total = total + part[start : start + EXTRA, :]
+def placed(values, here):
+    ordered = []
+    for place in range(len(values)):
+        total = values[0]
+        for shift in range(1, len(values)):
+            total = jnp.where(jnp.bitwise_xor(here, shift) == place, values[shift], total)
+        ordered.append(total)
+    return ordered
+
+
+def own_rows(value, here, blocks):
+    total = value[:blocks, :]
+    for place in range(1, value.shape[0] // blocks):
+        total = jnp.where(here == place, value[place * blocks : (place + 1) * blocks, :], total)
     return total
 
 
@@ -152,14 +160,14 @@
     data_rows = out.shape[0]
     here = place[0]
     columns_of = column[...]
-    source = jnp.where(columns_of < blocks, columns_of, 0)
+    source = jnp.where(columns_of < blocks, here * blocks + columns_of, 0)
     lane = lax.broadcasted_iota(jnp.int32, (1, width), 1)
     for shift in range(count):
         other = jnp.bitwise_xor(here, shift)
         for slot in range(slots):
             named = parts[shift][2 * blocks + slot : 2 * blocks + slot + 1, :]
             mine = jnp.where(lane == here, named, 0.0)
-            block = jnp.sum(mine, axis=1, keepdims=True).astype(jnp.int32) + shift * blocks
+            block = jnp.sum(mine, axis=1, keepdims=True).astype(jnp.int32) + other * blocks
             source = jnp.where(columns_of == blocks + other * slots + slot, block, source)
 
     def tables(index, values, picks, pairs):
@@ -171,9 +179,10 @@
         return turned
 
     source_table = tables(source, count * blocks, source_pick, source_pair)
-    field = jnp.concatenate([part[:blocks, :] for part in parts], axis=0)
+    pairs = placed([part[: 2 * blocks, :] for part in parts], here)
+    field = jnp.concatenate([pair[:blocks, :] for pair in pairs], axis=0)
     start[...] = field
-    weight[...] = jnp.concatenate([part[blocks : 2 * blocks, :] for part in parts], axis=0)
+    weight[...] = jnp.concatenate([pair[blocks:, :] for pair in pairs], axis=0)
     tables(row[...], data_rows, rows_pick, rows_pair)
     square = (tiles, tiles)
     same = lax.broadcasted_iota(jnp.int32, square, 0) == lax.broadcasted_iota(jnp.int32, square, 1)
@@ -199,22 +208,21 @@
     out[...] = gather(rows_pair[...], scales, terms)
 
 
-def start_data_kernel(count, *refs):
+def start_data_kernel(*refs):
     low, high, rows_pick, source_pair, scale, observed, data_weight = refs[:7]
-    parts = refs[7 : 7 + count]
-    out = refs[7 + count]
+    parts, out = refs[7:-1], refs[-1]
     total = total_rows(parts)
     data = (data_weight[...] * (observed[...] - total)).astype(BF16)
     terms = products(kept_tiles(low, high), pick(rows_pick[...], data))
     out[...] = gather(source_pair[...], scale[...], terms)
 
 
-def start_residual_kernel(blocks, count, *refs):
+def start_residual_kernel(*refs):
     low, high, source_pick, rows_pair, scale, start, weight = refs[:7]
-    parts = refs[7 : 7 + count]
-    out, residual = refs[7 + count :]
+    parts = refs[7:-2]
+    out, residual = refs[-2:]
     weights = weight[...]
-    value = total_blocks(parts, blocks) - weights * start[...]
+    value = total_rows(parts) - weights * start[...]
     residual[...] = value
     terms = products(kept_tiles(low, high), pick(source_pick[...], value.astype(BF16)))
     data_rows = rows_pair.shape[0]
@@ -224,10 +232,10 @@
     )
 
 
-def image_data_kernel(count, *refs):
+def image_data_kernel(*refs):
     low, high, rows_pick, source_pair, scale, data_weight = refs[:6]
-    parts = refs[6 : 6 + count]
-    out, predicted, sums = refs[6 + count :]
+    parts = refs[6:-3]
+    out, predicted, sums = refs[-3:]
     data_rows = data_weight.shape[0]
     whole_part = total_rows(parts)
     total = whole_part[:data_rows, :]
@@ -240,15 +248,16 @@
     out[cells:, :] = pack_rows([columns(total * data.astype(F32))], total.shape[1])
 
 
-def residual_kernel(blocks, count, *refs):
+def residual_kernel(*refs):
     low, high, source_pick, rows_pair, scale, weight, direction, sums = refs[:8]
-    parts = refs[8 : 8 + count]
-    out, residual, step = refs[8 + count :]
+    parts = refs[8:-3]
+    out, residual, step = refs[-3:]
     cells = source_pick.shape[1]
     weights = weight[...]
     along = direction[...]
-    image = weights * along - total_blocks(parts, blocks)
-    curve = whole(sums[1:2, :]) - whole(extra_rows(parts, cells)[0:1, :])
+    total = total_rows(parts)
+    image = weights * along - total[:cells, :]
+    curve = whole(sums[1:2, :]) - whole(total[cells : cells + 1, :])
     alpha = whole(sums[0:1, :]) / curve
     step[...] = jnp.broadcast_to(alpha, step.shape)
     value = residual_of(along, alpha, image)
@@ -267,10 +276,10 @@
     return residual - alpha * image
 
 
-def second_data_kernel(blocks, count, *refs):
+def second_data_kernel(*refs):
     low, high, rows_pick, source_pair, scale, data_weight, predicted, sums = refs[:8]
-    parts = refs[8 : 8 + count]
-    outs, scalars = refs[8 + count : -1], refs[-1]
+    parts = refs[8:-2]
+    out, scalars = refs[-2:]
     data_rows = data_weight.shape[0]
     whole_part = total_rows(parts)
     norm = whole(whole_part[data_rows : data_rows + 1, :])
@@ -283,31 +292,33 @@
     total = whole_part[:data_rows, :] + beta * predicted[...]
     data = (data_weight[...] * (0.0 - total)).astype(BF16)
     terms = products(kept_tiles(low, high), pick(rows_pick[...], data))
-    cells = gather(source_pair[...], scale[...], terms)
-    curved = columns(total * data.astype(F32))
-    for group, out in enumerate(outs):
-        out[:blocks, :] = cells[group * blocks : (group + 1) * blocks, :]
-        out[blocks:, :] = jnp.broadcast_to(curved, (out.shape[0] - blocks, total.shape[1]))
+    cells = source_pair.shape[0]
+    out[:cells, :] = gather(source_pair[...], scale[...], terms)
+    out[cells:, :] = pack_rows([columns(total * data.astype(F32))], total.shape[1])
     wide = (1, scalars.shape[1])
     scalars[...] = pack_rows(
         [jnp.broadcast_to(value, wide) for value in (norm, beta, curve)], scalars.shape[1]
     )
 
 
-def last_kernel(blocks, count, *refs):
-    weight, start, first, second, step, scalars = refs[:6]
-    parts = refs[6 : 6 + count]
-    model, residual = refs[6 + count :]
+def last_kernel(*refs):
+    weight, start, first, second, step, scalars, place = refs[:7]
+    parts = refs[7:-2]
+    model, residual = refs[-2:]
+    blocks = model.shape[0]
+    cells = weight.shape[0]
+    here = place[0]
     norm = scalars[0:1, 0:1]
     beta = scalars[1:2, 0:1]
     curve = scalars[2:3, 0:1]
-    along = first[:blocks, :]
-    left = second[:blocks, :]
+    total = total_rows(parts)
+    along = own_rows(first[...], here, blocks)
+    left = own_rows(second[...], here, blocks)
     direction = left + beta * along
-    whole_part = total_rows(parts)
-    image = weight[:blocks, :] * direction - whole_part[:blocks, :]
-    alpha = norm / (curve - whole(whole_part[blocks : blocks + 1, :]))
-    model[...] = start[:blocks, :] + step[0:1, 0:1] * along + alpha * direction
+    held = own_rows(weight[...], here, blocks)
+    image = held * direction - own_rows(total[:cells, :], here, blocks)
+    alpha = norm / (curve - whole(total[cells : cells + 1, :]))
+    model[...] = own_rows(start[...], here, blocks) + step[0:1, 0:1] * along + alpha * direction
     residual[...] = left - alpha * image
 
 
@@ -350,11 +361,11 @@
     half_shape = (half, width, width)
     place = lax.axis_index("tiles").astype(jnp.int32).reshape(1)
 
-    def across(values):
-        return exchange(values, "tiles", count)
+    def across(value):
+        return doubling(value, "tiles", count)
 
     def within(value):
-        return exchange([value] * sharing, ("split", "depth"), sharing)
+        return doubling(value, ("split", "depth"), sharing)
 
     named = jnp.transpose(send_index, (0, 2, 1)).reshape(slots, count)
     (opening,) = call(
@@ -370,7 +381,7 @@
             pltpu.SemaphoreType.DMA((3,)),
         ],
     )
-    begin = across([opening] * count)
+    begin = exchange([opening] * count, "tiles", count)
     low, low_turned = call(
         loading_kernel,
         [(half_shape, BF16)] * 2,
@@ -402,7 +413,7 @@
         scratch=[pltpu.SemaphoreType.DMA((half // CHUNK,))],
     )
     (part,) = call(
-        functools.partial(start_data_kernel, sharing),
+        start_data_kernel,
         [((cells, width), F32)],
         low,
         high,
@@ -414,7 +425,7 @@
         *within(part),
     )
     part, first = call(
-        functools.partial(start_residual_kernel, blocks, count),
+        start_residual_kernel,
         [((data_rows + EXTRA, width), F32), ((cells, width), F32)],
         low_turned,
         high_turned,
@@ -423,10 +434,10 @@
         scale,
         start,
         weight,
-        *across([part] * count),
+        *across(part),
     )
     part, predicted, sums = call(
-        functools.partial(image_data_kernel, sharing),
+        image_data_kernel,
         [((cells + EXTRA, width), F32), ((data_rows, width), F32), ((EXTRA, width), F32)],
         low,
         high,
@@ -437,7 +448,7 @@
         *within(part),
     )
     part, second, step = call(
-        functools.partial(residual_kernel, blocks, count),
+        residual_kernel,
         [((data_rows + EXTRA, width), F32), ((cells, width), F32), ((8, 128), F32)],
         low_turned,
         high_turned,
@@ -447,11 +458,11 @@
         weight,
         first,
         sums,
-        *across([part] * count),
-    )
-    *part, scalars = call(
-        functools.partial(second_data_kernel, blocks, sharing),
-        [((blocks + 4, width), F32)] * count + [((EXTRA, width), F32)],
+        *across(part),
+    )
+    part, scalars = call(
+        second_data_kernel,
+        [((cells + EXTRA, width), F32), ((EXTRA, width), F32)],
         low,
         high,
         rows_pick,
@@ -463,7 +474,7 @@
         *within(part),
     )
     model, residual = call(
-        functools.partial(last_kernel, blocks, count),
+        last_kernel,
         [((blocks, width), F32), ((blocks, width), F32)],
         weight,
         start,
@@ -471,6 +482,7 @@
         second,
         step,
         scalars,
+        place,
         *across(part),
     )
     return (model, residual)

time: 56.8 us -> 63.7 us (1.12)
  waiting for transfers between devices: 16.1 us -> 30.7 us
  starting transfers between devices: 24.6 us -> 16.9 us
    ppermute x0 -> x12, waiting for transfers between devices: none -> 29.3 us  [doubling(): other = lax.ppermute(value, axes, perm)]
    ppermute x21 -> x3, starting transfers between devices: 24.6 us -> 5.76 us  [exchange(): parts[shift] = lax.ppermute(values[shift], axes, perm)]
    ppermute x21 -> x3, waiting for transfers between devices: 16.1 us -> 1.38 us  [exchange(): parts[shift] = lax.ppermute(values[shift], axes, perm)]
    ppermute x0 -> x12, starting transfers between devices: none -> 11.2 us  [doubling(): other = lax.ppermute(value, axes, perm)]
  transfers between devices with their start and end apart: 21 -> 15, of which waited for: 14 -> 13; matrix products, arithmetic and copies ran while one was open for 0% -> 0% of each run, Pallas kernels for 5% -> 4%
where the time goes in v1:
time: 63.7 us; the launch traced here: 63.5 us
  waiting for transfers between devices  30.7 us (48%)
  starting transfers between devices  16.9 us (27%)
  Pallas kernels  15.1 us (24%)
  between operations  0.72 us (1%)
    ppermute x12, waiting for transfers between devices, doubling(): other = lax.ppermute(value, axes, perm)  29.3 us
    pallas_call x9, Pallas kernels, call(): pl.pallas_call(body, out_shape=[jax.ShapeDtypeStruct(shape, dtype) for sh...  15.1 us
    ppermute x12, starting transfers between devices, doubling(): other = lax.ppermute(value, axes, perm)  11.2 us
    ppermute x3, starting transfers between devices, exchange(): parts[shift] = lax.ppermute(values[shift], axes, perm)  5.76 us
    ppermute x3, waiting for transfers between devices, exchange(): parts[shift] = lax.ppermute(values[shift], axes, perm)  1.38 us
  transfers between devices with their start and end apart: 15, of which 13 were waited for; matrix products, arithmetic and copies ran while one was open for 0% of the time, Pallas kernels for 4%

profile of v1, /device:TPU:0, one launch (start us, length us, event | category | flops | bytes accessed | tf_op | source)
XLA Modules:
  0.0 63.5 jit_solution(3087385763618910031)
XLA Ops:
  0.6 0.7 %shard_map.104.opening.refs_6_ = f32[16,256]{1,0:T(8,128)S(1)} custom-call(f32[4,256]{1,0:T(4,128)} %start.1, f32[4,256]{1,0:T(4,128)} %weight.1, s32[2,4]{1,0:T(2,128)} %bitcast.10), custom_call_target="tpu_custom_call" | custom-call | tf_op jit(solution)/shard_map/pallas_call | solution.py:331
  1.4 5.1 %collective-permute-start.2 = (f32[16,256]{1,0:T(8,128)S(1)}, f32[16,256]{1,0:T(8,128)S(1)}, u32[]{:S(2)}, u32[]{:S(2)}) collective-permute-start(f32[16,256]{1,0:T(8,128)S(1)} %shard_map.104.opening.refs_6_), channel_id=1, source_target_pairs={{0,12},{4,8},{8,4},{12,0},{1,13},{5,9},{9,5},{13,1},{2,14},{6,10},... | collective-permute-start | bytes 49160 | tf_op jit(solution)/shard_map/ppermute | solution.py:23
  6.5 0.0 collective-permute-start.1
  6.5 0.6 %collective-permute-start = (f32[16,256]{1,0:T(8,128)S(1)}, f32[16,256]{1,0:T(8,128)S(1)}, u32[]{:S(2)}, u32[]{:S(2)}) collective-permute-start(f32[16,256]{1,0:T(8,128)S(1)} %shard_map.104.opening.refs_6_), channel_id=1, source_target_pairs={{0,4},{4,0},{8,12},{12,8},{1,5},{5,1},{9,13},{13,9},{2,6},{6,2},{1... | collective-permute-start | bytes 49160 | tf_op jit(solution)/shard_map/ppermute | solution.py:23
  7.1 0.0 copy-start.2
  7.1 0.0 copy-start.3
  7.1 0.0 copy-start.4
  7.1 2.6 %shard_map.105 = (bf16[32,256,256]{2,1,0:T(8,128)(2,1)S(1)}, bf16[32,256,256]{2,1,0:T(8,128)(2,1)S(1)}) custom-call(bf16[64,256,256]{2,1,0:T(8,128)(2,1)} %refs_0_.1, f32[16,256]{1,0:T(8,128)S(1)} %shard_map.104.opening.refs_6_), custom_call_target="tpu_custom_call" | custom-call | tf_op jit(solution)/shard_map/pallas_call | solution.py:331
  9.8 0.0 collective-permute-done.2.refs_9_
  9.8 1.4 %collective-permute-done.1.refs_8_ = f32[16,256]{1,0:T(8,128)S(1)} collective-permute-done((f32[16,256]{1,0:T(8,128)S(1)}, f32[16,256]{1,0:T(8,128)S(1)}, u32[]{:S(2)}, u32[]{:S(2)}) %collective-permute-start.1) | collective-permute-done | bytes 16416 | tf_op jit(solution)/shard_map/ppermute | solution.py:23
  11.1 0.0 collective-permute-done.refs_7_
  11.1 0.0 copy-done.2
  11.1 0.0 copy-done.3
  11.1 0.0 copy-done.4
  11.2 0.0 copy-start
  11.2 0.0 copy-start.1
  11.2 3.6 %shard_map.106 = (f32[16,256]{1,0:T(8,128)S(1)}, bf16[32,256,256]{2,1,0:T(8,128)(2,1)S(1)}, bf16[32,256,256]{2,1,0:T(8,128)(2,1)S(1)}, bf16[64,16]{1,0:T(8,128)(...) custom-call(bf16[64,256,256]{2,1,0:T(8,128)(2,1)} %refs_0_.1, ...), custom_call_target="tpu_custom_call" | custom-call | tf_op jit(solution)/shard_map/pallas_call | solution.py:331
  14.8 0.1 collective-permute-start.3
  14.8 1.2 %collective-permute-done.3 = f32[16,256]{1,0:T(8,128)S(1)} collective-permute-done((f32[16,256]{1,0:T(8,128)S(1)}, f32[16,256]{1,0:T(8,128)S(1)}, u32[]{:S(2)}, u32[]{:S(2)}) %collective-permute-start.3) | collective-permute-done | bytes 16416 | tf_op jit(solution)/shard_map/ppermute | solution.py:31
  16.0 1.5 %collective-permute-start.4 = (f32[16,256]{1,0:T(8,128)S(1)}, f32[16,256]{1,0:T(8,128)S(1)}, u32[]{:S(2)}, u32[]{:S(2)}) collective-permute-start(f32[16,256]{1,0:T(8,128)S(1)} %add.18.refs_7_), channel_id=1, source_target_pairs={{0,2},{1,3},{2,0},{3,1},{4,6},{5,7},{6,4},{7,5},{8,10},{9,11},{10,... | collective-permute-start | bytes 49160 | tf_op jit(solution)/shard_map/ppermute | solution.py:31
  17.5 2.2 %collective-permute-done.4.refs_8_ = f32[16,256]{1,0:T(8,128)S(1)} collective-permute-done((f32[16,256]{1,0:T(8,128)S(1)}, f32[16,256]{1,0:T(8,128)S(1)}, u32[]{:S(2)}, u32[]{:S(2)}) %collective-permute-start.4) | collective-permute-done | bytes 16416 | tf_op jit(solution)/shard_map/ppermute | solution.py:31
  19.8 0.0 copy-done
  19.8 0.0 copy-done.1
  19.8 1.4 %shard_map.107 = f32[16,256]{1,0:T(8,128)S(1)} custom-call(bf16[32,256,256]{2,1,0:T(8,128)(2,1)S(1)} %get-tuple-element.31.refs_0_, bf16[32,256,256]{2,1,0:T(8,128)(2,1)S(1)} %get-tuple-element.32.refs_1_, bf16[64,16]{1,0:T(8,128)(2,1)S(1)} %get-tuple-element.33.refs_2_, bf16[16,128]{1,0:T(8,128)(2,1)S(1)} %get-tuple-element.34.refs_3_, ...), custom_call_target="tpu_custom_call" | custom-call | tf_op jit(solution)/shard_map/pallas_call | solution.py:331
  21.2 0.1 collective-permute-start.5
  21.2 3.7 %collective-permute-done.5 = f32[16,256]{1,0:T(8,128)S(1)} collective-permute-done((f32[16,256]{1,0:T(8,128)S(1)}, f32[16,256]{1,0:T(8,128)S(1)}, u32[]{:S(2)}, u32[]{:S(2)}) %collective-permute-start.5) | collective-permute-done | bytes 16416 | tf_op jit(solution)/shard_map/ppermute | solution.py:31
  24.9 2.0 %collective-permute-start.6 = (f32[16,256]{1,0:T(8,128)S(1)}, f32[16,256]{1,0:T(8,128)S(1)}, u32[]{:S(2)}, u32[]{:S(2)}) collective-permute-start(f32[16,256]{1,0:T(8,128)S(1)} %add.19.refs_7_), channel_id=1, source_target_pairs={{0,8},{4,12},{8,0},{12,4},{1,9},{5,13},{9,1},{13,5},{2,10},{6,14},... | collective-permute-start | bytes 49160 | tf_op jit(solution)/shard_map/ppermute | solution.py:31
  27.0 2.6 %collective-permute-done.6.refs_8_ = f32[16,256]{1,0:T(8,128)S(1)} collective-permute-done((f32[16,256]{1,0:T(8,128)S(1)}, f32[16,256]{1,0:T(8,128)S(1)}, u32[]{:S(2)}, u32[]{:S(2)}) %collective-permute-start.6) | collective-permute-done | bytes 16416 | tf_op jit(solution)/shard_map/ppermute | solution.py:31
  29.6 1.4 %shard_map.108 = (f32[24,256]{1,0:T(8,128)S(1)}, f32[16,256]{1,0:T(8,128)S(1)}) custom-call(bf16[32,256,256]{2,1,0:T(8,128)(2,1)S(1)} %get-tuple-element.24.refs_1_.refs_0_, bf16[32,256,256]{2,1,0:T(8,128)(2,1)S(1)} %get-tuple-element.27.refs_1_, bf16[64,16]{1,0:T(8,128)(2,1)S(1)} %get-tuple-element.28.refs_2_, ...), custom_call_target="tpu_custom_call" | custom-call | tf_op jit(solution)/shard_map/pallas_call | solution.py:331
  31.0 0.0 collective-permute-start.7
  31.0 1.2 %collective-permute-done.7 = f32[24,256]{1,0:T(8,128)S(1)} collective-permute-done((f32[24,256]{1,0:T(8,128)S(1)}, f32[24,256]{1,0:T(8,128)S(1)}, u32[]{:S(2)}, u32[]{:S(2)}) %collective-permute-start.7) | collective-permute-done | bytes 24608 | tf_op jit(solution)/shard_map/ppermute | solution.py:31
  32.2 1.5 %collective-permute-start.8 = (f32[24,256]{1,0:T(8,128)S(1)}, f32[24,256]{1,0:T(8,128)S(1)}, u32[]{:S(2)}, u32[]{:S(2)}) collective-permute-start(f32[24,256]{1,0:T(8,128)S(1)} %add.20.refs_6_), channel_id=1, source_target_pairs={{0,2},{1,3},{2,0},{3,1},{4,6},{5,7},{6,4},{7,5},{8,10},{9,11},{10,... | collective-permute-start | bytes 73736 | tf_op jit(solution)/shard_map/ppermute | solution.py:31
  33.7 2.3 %collective-permute-done.8.refs_7_ = f32[24,256]{1,0:T(8,128)S(1)} collective-permute-done((f32[24,256]{1,0:T(8,128)S(1)}, f32[24,256]{1,0:T(8,128)S(1)}, u32[]{:S(2)}, u32[]{:S(2)}) %collective-permute-start.8) | collective-permute-done | bytes 24608 | tf_op jit(solution)/shard_map/ppermute | solution.py:31
  36.0 1.4 %shard_map.109 = (f32[24,256]{1,0:T(8,128)S(1)}, f32[16,256]{1,0:T(8,128)S(1)}, f32[8,256]{1,0:T(8,128)S(1)}) custom-call(bf16[32,256,256]{2,1,0:T(8,128)(2,1)S(1)} %get-tuple-element.31.refs_0_, bf16[32,256,256]{2,1,0:T(8,128)(2,1)S(1)} %get-tuple-element.32.refs_1_, bf16[64,16]{1,0:T(8,128)(2,1)S(1)} %get-tuple-element.33.refs_2_, ...), custom_call_target="tpu_custom_call" | custom-call | tf_op jit(solution)/shard_map/pallas_call | solution.py:331
  37.5 0.1 collective-permute-start.9
  37.5 3.8 %collective-permute-done.9 = f32[24,256]{1,0:T(8,128)S(1)} collective-permute-done((f32[24,256]{1,0:T(8,128)S(1)}, f32[24,256]{1,0:T(8,128)S(1)}, u32[]{:S(2)}, u32[]{:S(2)}) %collective-permute-start.9) | collective-permute-done | bytes 24608 | tf_op jit(solution)/shard_map/ppermute | solution.py:31
  41.3 2.2 %collective-permute-start.10 = (f32[24,256]{1,0:T(8,128)S(1)}, f32[24,256]{1,0:T(8,128)S(1)}, u32[]{:S(2)}, u32[]{:S(2)}) collective-permute-start(f32[24,256]{1,0:T(8,128)S(1)} %add.21.refs_8_), channel_id=1, source_target_pairs={{0,8},{4,12},{8,0},{12,4},{1,9},{5,13},{9,1},{13,5},{2,10},{6,14},... | collective-permute-start | bytes 73736 | tf_op jit(solution)/shard_map/ppermute | solution.py:31
  43.5 2.5 %collective-permute-done.10.refs_9_ = f32[24,256]{1,0:T(8,128)S(1)} collective-permute-done((f32[24,256]{1,0:T(8,128)S(1)}, f32[24,256]{1,0:T(8,128)S(1)}, u32[]{:S(2)}, u32[]{:S(2)}) %collective-permute-start.10) | collective-permute-done | bytes 24608 | tf_op jit(solution)/shard_map/ppermute | solution.py:31
  46.0 1.5 %shard_map.110 = (f32[24,256]{1,0:T(8,128)S(1)}, f32[16,256]{1,0:T(8,128)S(1)}, f32[8,128]{1,0:T(8,128)S(1)}) custom-call(bf16[32,256,256]{2,1,0:T(8,128)(2,1)S(1)} %get-tuple-element.24.refs_1_.refs_0_, bf16[32,256,256]{2,1,0:T(8,128)(2,1)S(1)} %get-tuple-element.27.refs_1_, bf16[64,16]{1,0:T(8,128)(2,1)S(1)} %get-tuple-element.28.refs_2_, ...), custom_call_target="tpu_custom_call" | custom-call | tf_op jit(solution)/shard_map/pallas_call | solution.py:331
  47.6 0.0 collective-permute-start.11
  47.6 1.2 %collective-permute-done.11 = f32[24,256]{1,0:T(8,128)S(1)} collective-permute-done((f32[24,256]{1,0:T(8,128)S(1)}, f32[24,256]{1,0:T(8,128)S(1)}, u32[]{:S(2)}, u32[]{:S(2)}) %collective-permute-start.11) | collective-permute-done | bytes 24608 | tf_op jit(solution)/shard_map/ppermute | solution.py:31
  48.8 1.5 %collective-permute-start.12 = (f32[24,256]{1,0:T(8,128)S(1)}, f32[24,256]{1,0:T(8,128)S(1)}, u32[]{:S(2)}, u32[]{:S(2)}) collective-permute-start(f32[24,256]{1,0:T(8,128)S(1)} %add.22.refs_8_), channel_id=1, source_target_pairs={{0,2},{1,3},{2,0},{3,1},{4,6},{5,7},{6,4},{7,5},{8,10},{9,11},{10,... | collective-permute-start | bytes 73736 | tf_op jit(solution)/shard_map/ppermute | solution.py:31
  50.3 2.3 %collective-permute-done.12.refs_9_ = f32[24,256]{1,0:T(8,128)S(1)} collective-permute-done((f32[24,256]{1,0:T(8,128)S(1)}, f32[24,256]{1,0:T(8,128)S(1)}, u32[]{:S(2)}, u32[]{:S(2)}) %collective-permute-start.12) | collective-permute-done | bytes 24608 | tf_op jit(solution)/shard_map/ppermute | solution.py:31
  52.6 1.5 %shard_map.111 = (f32[24,256]{1,0:T(8,128)S(1)}, f32[8,256]{1,0:T(8,128)S(1)}) custom-call(bf16[32,256,256]{2,1,0:T(8,128)(2,1)S(1)} %get-tuple-element.31.refs_0_, bf16[32,256,256]{2,1,0:T(8,128)(2,1)S(1)} %get-tuple-element.32.refs_1_, bf16[64,16]{1,0:T(8,128)(2,1)S(1)} %get-tuple-element.33.refs_2_, bf16[16,128]{1,0:T(8,128)(2,1)S(1)} %get-tuple-element.34.refs_3_, ...), custom_call_target="tpu_custom_call" | custom-call | tf_op jit(solution)/shard_map/pallas_call | solution.py:331
  54.1 0.1 collective-permute-start.13
  54.2 3.8 %collective-permute-done.13 = f32[24,256]{1,0:T(8,128)S(1)} collective-permute-done((f32[24,256]{1,0:T(8,128)S(1)}, f32[24,256]{1,0:T(8,128)S(1)}, u32[]{:S(2)}, u32[]{:S(2)}) %collective-permute-start.13) | collective-permute-done | bytes 24608 | tf_op jit(solution)/shard_map/ppermute | solution.py:31
  58.0 2.2 %collective-permute-start.14 = (f32[24,256]{1,0:T(8,128)S(1)}, f32[24,256]{1,0:T(8,128)S(1)}, u32[]{:S(2)}, u32[]{:S(2)}) collective-permute-start(f32[24,256]{1,0:T(8,128)S(1)} %add.23.refs_7_), channel_id=1, source_target_pairs={{0,8},{4,12},{8,0},{12,4},{1,9},{5,13},{9,1},{13,5},{2,10},{6,14},... | collective-permute-start | bytes 73736 | tf_op jit(solution)/shard_map/ppermute | solution.py:31
  60.2 2.5 %collective-permute-done.14.refs_8_ = f32[24,256]{1,0:T(8,128)S(1)} collective-permute-done((f32[24,256]{1,0:T(8,128)S(1)}, f32[24,256]{1,0:T(8,128)S(1)}, u32[]{:S(2)}, u32[]{:S(2)}) %collective-permute-start.14) | collective-permute-done | bytes 24608 | tf_op jit(solution)/shard_map/ppermute | solution.py:31
  62.7 0.8 %shard_map.112 = (f32[4,256]{1,0:T(4,128)}, f32[4,256]{1,0:T(4,128)}) custom-call(f32[16,256]{1,0:T(8,128)S(1)} %get-tuple-element.25.refs_6_.refs_5_.refs_0_, f32[16,256]{1,0:T(8,128)S(1)} %get-tuple-element.26.refs_5_.refs_1_, f32[16,256]{1,0:T(8,128)S(1)} %get-tuple-element.36.refs_6_.refs_2_, f32[16,256]{1,0:T(8,128)S(1)} %get-tuple-element.40.refs_3_, ...), custom_call_target="tpu_custom_call" | custom-call | tf_op jit(solution)/shard_map/pallas_call | solution.py:331
  (6 shorter events, 0.0 us)
Async XLA Ops:
  1.4 8.4 %collective-permute-start.2 = (f32[16,256]{1,0:T(8,128)S(1)}, f32[16,256]{1,0:T(8,128)S(1)}, u32[]{:S(2)}, u32[]{:S(2)}) collective-permute-start(f32[16,256]{1,0:T(8,128)S(1)} %shard_map.104.opening.refs_6_), channel_id=1, source_target_pairs={{0,12},{4,8},{8,4},{12,0},{1,13},{5,9},{9,5},{13,1},{2,14},{6,10},... | collective-permute-start | bytes 49160 | tf_op jit(solution)/shard_map/ppermute | solution.py:23
  6.5 4.6 %collective-permute-start.1 = (f32[16,256]{1,0:T(8,128)S(1)}, f32[16,256]{1,0:T(8,128)S(1)}, u32[]{:S(2)}, u32[]{:S(2)}) collective-permute-start(f32[16,256]{1,0:T(8,128)S(1)} %shard_map.104.opening.refs_6_), channel_id=1, source_target_pairs={{0,8},{4,12},{8,0},{12,4},{1,9},{5,13},{9,1},{13,5},{2,10},{6,14},... | collective-permute-start | bytes 49160 | tf_op jit(solution)/shard_map/ppermute | solution.py:23
  6.5 4.6 %collective-permute-start = (f32[16,256]{1,0:T(8,128)S(1)}, f32[16,256]{1,0:T(8,128)S(1)}, u32[]{:S(2)}, u32[]{:S(2)}) collective-permute-start(f32[16,256]{1,0:T(8,128)S(1)} %shard_map.104.opening.refs_6_), channel_id=1, source_target_pairs={{0,4},{4,0},{8,12},{12,8},{1,5},{5,1},{9,13},{13,9},{2,6},{6,2},{1... | collective-permute-start | bytes 49160 | tf_op jit(solution)/shard_map/ppermute | solution.py:23
  7.1 4.0 %copy-start.2 = (f32[64]{0:T(128)S(1)}, f32[64]{0:T(128)}, u32[]{:S(2)}) copy-start(f32[64]{0:T(128)} %param.10) | copy-start | bytes 772
  7.1 4.0 %copy-start.3 = (s32[64]{0:T(128)S(1)}, s32[64]{0:T(128)}, u32[]{:S(2)}) copy-start(s32[64]{0:T(128)} %param.11) | copy-start | bytes 772
  7.1 4.0 %copy-start.4 = (s32[64]{0:T(128)S(1)}, s32[64]{0:T(128)}, u32[]{:S(2)}) copy-start(s32[64]{0:T(128)} %param.12) | copy-start | bytes 772
  11.2 8.6 %copy-start = (f32[16,256]{1,0:T(8,128)S(1)}, f32[16,256]{1,0:T(8,128)}, u32[]{:S(2)}) copy-start(f32[16,256]{1,0:T(8,128)} %refs_5_.5) | copy-start | bytes 49156
  11.2 8.6 %copy-start.1 = (f32[16,256]{1,0:T(8,128)S(1)}, f32[16,256]{1,0:T(8,128)}, u32[]{:S(2)}) copy-start(f32[16,256]{1,0:T(8,128)} %refs_5_.3) | copy-start | bytes 49156
  14.8 1.2 %collective-permute-start.3 = (f32[16,256]{1,0:T(8,128)S(1)}, f32[16,256]{1,0:T(8,128)S(1)}, u32[]{:S(2)}, u32[]{:S(2)}) collective-permute-start(f32[16,256]{1,0:T(8,128)S(1)} %get-tuple-element.35), channel_id=1, source_target_pairs={{0,1},{1,0},{2,3},{3,2},{4,5},{5,4},{6,7},{7,6},{8,9},{9,8},{10,11... | collective-permute-start | bytes 49160 | tf_op jit(solution)/shard_map/ppermute | solution.py:31
  16.0 3.7 %collective-permute-start.4 = (f32[16,256]{1,0:T(8,128)S(1)}, f32[16,256]{1,0:T(8,128)S(1)}, u32[]{:S(2)}, u32[]{:S(2)}) collective-permute-start(f32[16,256]{1,0:T(8,128)S(1)} %add.18.refs_7_), channel_id=1, source_target_pairs={{0,2},{1,3},{2,0},{3,1},{4,6},{5,7},{6,4},{7,5},{8,10},{9,11},{10,... | collective-permute-start | bytes 49160 | tf_op jit(solution)/shard_map/ppermute | solution.py:31
  21.2 3.7 %collective-permute-start.5 = (f32[16,256]{1,0:T(8,128)S(1)}, f32[16,256]{1,0:T(8,128)S(1)}, u32[]{:S(2)}, u32[]{:S(2)}) collective-permute-start(f32[16,256]{1,0:T(8,128)S(1)} %shard_map.107), channel_id=1, source_target_pairs={{0,4},{4,0},{8,12},{12,8},{1,5},{5,1},{9,13},{13,9},{2,6},{6,2},{1... | collective-permute-start | bytes 49160 | tf_op jit(solution)/shard_map/ppermute | solution.py:31
  24.9 4.6 %collective-permute-start.6 = (f32[16,256]{1,0:T(8,128)S(1)}, f32[16,256]{1,0:T(8,128)S(1)}, u32[]{:S(2)}, u32[]{:S(2)}) collective-permute-start(f32[16,256]{1,0:T(8,128)S(1)} %add.19.refs_7_), channel_id=1, source_target_pairs={{0,8},{4,12},{8,0},{12,4},{1,9},{5,13},{9,1},{13,5},{2,10},{6,14},... | collective-permute-start | bytes 49160 | tf_op jit(solution)/shard_map/ppermute | solution.py:31
  31.0 1.2 %collective-permute-start.7 = (f32[24,256]{1,0:T(8,128)S(1)}, f32[24,256]{1,0:T(8,128)S(1)}, u32[]{:S(2)}, u32[]{:S(2)}) collective-permute-start(f32[24,256]{1,0:T(8,128)S(1)} %get-tuple-element.37), channel_id=1, source_target_pairs={{0,1},{1,0},{2,3},{3,2},{4,5},{5,4},{6,7},{7,6},{8,9},{9,8},{10,11... | collective-permute-start | bytes 73736 | tf_op jit(solution)/shard_map/ppermute | solution.py:31
  32.2 3.8 %collective-permute-start.8 = (f32[24,256]{1,0:T(8,128)S(1)}, f32[24,256]{1,0:T(8,128)S(1)}, u32[]{:S(2)}, u32[]{:S(2)}) collective-permute-start(f32[24,256]{1,0:T(8,128)S(1)} %add.20.refs_6_), channel_id=1, source_target_pairs={{0,2},{1,3},{2,0},{3,1},{4,6},{5,7},{6,4},{7,5},{8,10},{9,11},{10,... | collective-permute-start | bytes 73736 | tf_op jit(solution)/shard_map/ppermute | solution.py:31
  37.5 3.8 %collective-permute-start.9 = (f32[24,256]{1,0:T(8,128)S(1)}, f32[24,256]{1,0:T(8,128)S(1)}, u32[]{:S(2)}, u32[]{:S(2)}) collective-permute-start(f32[24,256]{1,0:T(8,128)S(1)} %get-tuple-element.39), channel_id=1, source_target_pairs={{0,4},{4,0},{8,12},{12,8},{1,5},{5,1},{9,13},{13,9},{2,6},{6,2},{1... | collective-permute-start | bytes 73736 | tf_op jit(solution)/shard_map/ppermute | solution.py:31
  41.3 4.7 %collective-permute-start.10 = (f32[24,256]{1,0:T(8,128)S(1)}, f32[24,256]{1,0:T(8,128)S(1)}, u32[]{:S(2)}, u32[]{:S(2)}) collective-permute-start(f32[24,256]{1,0:T(8,128)S(1)} %add.21.refs_8_), channel_id=1, source_target_pairs={{0,8},{4,12},{8,0},{12,4},{1,9},{5,13},{9,1},{13,5},{2,10},{6,14},... | collective-permute-start | bytes 73736 | tf_op jit(solution)/shard_map/ppermute | solution.py:31
  47.6 1.2 %collective-permute-start.11 = (f32[24,256]{1,0:T(8,128)S(1)}, f32[24,256]{1,0:T(8,128)S(1)}, u32[]{:S(2)}, u32[]{:S(2)}) collective-permute-start(f32[24,256]{1,0:T(8,128)S(1)} %get-tuple-element.43), channel_id=1, source_target_pairs={{0,1},{1,0},{2,3},{3,2},{4,5},{5,4},{6,7},{7,6},{8,9},{9,8},{10,11... | collective-permute-start | bytes 73736 | tf_op jit(solution)/shard_map/ppermute | solution.py:31
  48.8 3.8 %collective-permute-start.12 = (f32[24,256]{1,0:T(8,128)S(1)}, f32[24,256]{1,0:T(8,128)S(1)}, u32[]{:S(2)}, u32[]{:S(2)}) collective-permute-start(f32[24,256]{1,0:T(8,128)S(1)} %add.22.refs_8_), channel_id=1, source_target_pairs={{0,2},{1,3},{2,0},{3,1},{4,6},{5,7},{6,4},{7,5},{8,10},{9,11},{10,... | collective-permute-start | bytes 73736 | tf_op jit(solution)/shard_map/ppermute | solution.py:31
  54.1 3.8 %collective-permute-start.13 = (f32[24,256]{1,0:T(8,128)S(1)}, f32[24,256]{1,0:T(8,128)S(1)}, u32[]{:S(2)}, u32[]{:S(2)}) collective-permute-start(f32[24,256]{1,0:T(8,128)S(1)} %get-tuple-element.45), channel_id=1, source_target_pairs={{0,4},{4,0},{8,12},{12,8},{1,5},{5,1},{9,13},{13,9},{2,6},{6,2},{1... | collective-permute-start | bytes 73736 | tf_op jit(solution)/shard_map/ppermute | solution.py:31
  58.0 4.7 %collective-permute-start.14 = (f32[24,256]{1,0:T(8,128)S(1)}, f32[24,256]{1,0:T(8,128)S(1)}, u32[]{:S(2)}, u32[]{:S(2)}) collective-permute-start(f32[24,256]{1,0:T(8,128)S(1)} %add.23.refs_7_), channel_id=1, source_target_pairs={{0,8},{4,12},{8,0},{12,4},{1,9},{5,13},{9,1},{13,5},{2,10},{6,14},... | collective-permute-start | bytes 73736 | tf_op jit(solution)/shard_map/ppermute | solution.py:31

commit v2 on v0

--- a/solution.py
+++ b/solution.py
@@ -66,15 +66,16 @@
     return jnp.concatenate(filled, axis=0)
 
 
-def products(tile_of, picked):
+def products(tile_of, picked, turn=False):
     tiles, width = picked.shape
     index = lax.broadcasted_iota(jnp.int32, (GROUP, width), 0)
+    dims = (((1,), (1 if turn else 0,)), ((), ()))
     pieces = []
     for first in range(0, tiles, GROUP):
         rows = picked[first : first + GROUP, :]
         total = None
         for i in range(GROUP):
-            value = jnp.dot(rows, tile_of(first + i), preferred_element_type=F32)
+            value = lax.dot_general(rows, tile_of(first + i), dims, preferred_element_type=F32)
             total = value if total is None else jnp.where(index == i, value, total)
         pieces.append(total)
     return jnp.concatenate(pieces, axis=0)
@@ -97,17 +98,54 @@
     return jnp.dot(table, both, preferred_element_type=F32)
 
 
-def loading_kernel(codes, opening, low, low_turned, done):
-    half = low.shape[0]
+def tables(index, values, picks, pairs):
+    tiles = index.shape[1]
+    hits = lax.broadcasted_iota(jnp.int32, (values, tiles), 0) == index
+    ones = jnp.where(hits, 1.0, 0.0)
+    picks[...] = ones.T.astype(BF16)
+    pairs[...] = jnp.concatenate([ones, ones], axis=1).astype(BF16)
+
+
+def chunk_copies(codes, first, kept, done):
     copies = []
-    for chunk in range(half // CHUNK):
-        span = pl.ds(chunk * CHUNK, CHUNK)
-        copies.append(pltpu.make_async_copy(codes.at[span], low.at[span], done.at[chunk]))
+    for chunk in range(kept.shape[0] // CHUNK):
+        source = codes.at[pl.ds(first + chunk * CHUNK, CHUNK)]
+        target = kept.at[pl.ds(chunk * CHUNK, CHUNK)]
+        copies.append(pltpu.make_async_copy(source, target, done.at[chunk]))
         copies[-1].start()
-    for chunk, copy in enumerate(copies):
+    return copies
+
+
+def loading_kernel(
+    codes, opening, far_scale, far_row, low, rows_pick, rows_pair, wide_scale, scale, row, done, small
+):
+    near = [
+        pltpu.make_async_copy(far_scale, scale, small.at[0]),
+        pltpu.make_async_copy(far_row, row, small.at[1]),
+    ]
+    for copy in near:
+        copy.start()
+    copies = chunk_copies(codes, 0, low, done)
+    tiles, width = wide_scale.shape
+    for copy in near:
         copy.wait()
-        for k in range(chunk * CHUNK, (chunk + 1) * CHUNK):
-            low_turned[k] = low[k].T
+    tables(row[...], rows_pick.shape[1], rows_pick, rows_pair)
+    square = (tiles, tiles)
+    same = lax.broadcasted_iota(jnp.int32, square, 0) == lax.broadcasted_iota(jnp.int32, square, 1)
+    wide_scale[...] = jnp.dot(
+        jnp.where(same, scale[...], 0.0),
+        jnp.ones((tiles, width), F32),
+        precision=HIGH,
+        preferred_element_type=F32,
+    )
+    for copy in copies:
+        copy.wait()
+
+
+def turning_kernel(first, low, high, part, turned):
+    tile_of = kept_tiles(low, high)
+    for k in range(turned.shape[0]):
+        turned[k] = tile_of(first + k).T
 
 
 def opening_kernel(start, weight, named, out, sources, weights, names, done):
@@ -130,26 +168,12 @@
 
 
 def first_kernel(blocks, slots, count, *refs):
-    codes, low_turned, scale, row, column, place = refs[:6]
+    codes, low, scale, rows_pair, column, place = refs[:6]
     parts = refs[6 : 6 + count]
-    (out, high, high_turned, rows_pick, rows_pair, source_pick, source_pair, wide_scale) = refs[
-        6 + count : 14 + count
-    ]
-    start, weight, done = refs[14 + count :]
-    half = low_turned.shape[0]
-    copies = []
-    for chunk in range(high.shape[0] // CHUNK):
-        copies.append(
-            pltpu.make_async_copy(
-                codes.at[pl.ds(half + chunk * CHUNK, CHUNK)],
-                high.at[pl.ds(chunk * CHUNK, CHUNK)],
-                done.at[chunk],
-            )
-        )
-        copies[-1].start()
-    tiles = scale.shape[1]
+    out, high, source_pick, source_pair, start, weight, done = refs[6 + count :]
+    loaded = low.shape[0]
+    copies = chunk_copies(codes, loaded, high, done)
     width = out.shape[1]
-    data_rows = out.shape[0]
     here = place[0]
     columns_of = column[...]
     source = jnp.where(columns_of < blocks, columns_of, 0)
@@ -161,48 +185,27 @@
             mine = jnp.where(lane == here, named, 0.0)
             block = jnp.sum(mine, axis=1, keepdims=True).astype(jnp.int32) + shift * blocks
             source = jnp.where(columns_of == blocks + other * slots + slot, block, source)
-
-    def tables(index, values, picks, pairs):
-        hits = lax.broadcasted_iota(jnp.int32, (values, tiles), 0) == index
-        ones = jnp.where(hits, 1.0, 0.0)
-        turned = ones.T.astype(BF16)
-        picks[...] = turned
-        pairs[...] = jnp.concatenate([ones, ones], axis=1).astype(BF16)
-        return turned
-
-    source_table = tables(source, count * blocks, source_pick, source_pair)
+    tables(source, count * blocks, source_pick, source_pair)
     field = jnp.concatenate([part[:blocks, :] for part in parts], axis=0)
     start[...] = field
     weight[...] = jnp.concatenate([part[blocks : 2 * blocks, :] for part in parts], axis=0)
-    tables(row[...], data_rows, rows_pick, rows_pair)
-    square = (tiles, tiles)
-    same = lax.broadcasted_iota(jnp.int32, square, 0) == lax.broadcasted_iota(jnp.int32, square, 1)
-    scales = jnp.dot(
-        jnp.where(same, scale[...], 0.0),
-        jnp.ones((tiles, width), F32),
-        precision=HIGH,
-        preferred_element_type=F32,
-    )
-    wide_scale[...] = scales
 
     def tile_of(k):
-        if k < half:
-            return low_turned[k]
-        k -= half
+        if k < loaded:
+            return low[k]
+        k -= loaded
         if k % CHUNK == 0:
             copies[k // CHUNK].wait()
-        tile = high[k].T
-        high_turned[k] = tile
-        return tile
-
-    terms = products(tile_of, pick(source_table, field.astype(BF16)))
-    out[...] = gather(rows_pair[...], scales, terms)
+        return high[k]
+
+    terms = products(tile_of, pick(source_pick[...], field.astype(BF16)), turn=True)
+    out[...] = gather(rows_pair[...], scale[...], terms)
 
 
 def start_data_kernel(count, *refs):
-    low, high, rows_pick, source_pair, scale, observed, data_weight = refs[:7]
-    parts = refs[7 : 7 + count]
-    out = refs[7 + count]
+    low, high, rows_pick, source_pair, scale, observed, data_weight, turned = refs[:8]
+    parts = refs[8 : 8 + count]
+    out = refs[8 + count]
     total = total_rows(parts)
     data = (data_weight[...] * (observed[...] - total)).astype(BF16)
     terms = products(kept_tiles(low, high), pick(rows_pick[...], data))
@@ -346,6 +349,7 @@
     sharing = lax.axis_size(("split", "depth"))
     cells = count * blocks
     half = tiles // 2
+    loaded = tiles * 3 // 4
     codes = pltpu.with_memory_space_constraint(tile_codes, pltpu.HBM)
     half_shape = (half, width, width)
     place = lax.axis_index("tiles").astype(jnp.int32).reshape(1)
@@ -371,36 +375,53 @@
         ],
     )
     begin = across([opening] * count)
-    low, low_turned = call(
+    low, rows_pick, rows_pair, scale = call(
         loading_kernel,
-        [(half_shape, BF16)] * 2,
+        [
+            ((loaded, width, width), BF16),
+            ((tiles, data_rows), BF16),
+            ((data_rows, 2 * tiles), BF16),
+            ((tiles, width), F32),
+        ],
         codes,
         opening,
-        scratch=[pltpu.SemaphoreType.DMA((half // CHUNK,))],
-    )
-    (part, high, high_turned, rows_pick, rows_pair, source_pick, source_pair, scale, start, weight) = call(
+        pltpu.with_memory_space_constraint(tile_scale.reshape(1, -1), pltpu.HBM),
+        pltpu.with_memory_space_constraint(tile_row.reshape(1, -1), pltpu.HBM),
+        scratch=[
+            pltpu.VMEM((1, tiles), F32),
+            pltpu.VMEM((1, tiles), jnp.int32),
+            pltpu.SemaphoreType.DMA((loaded // CHUNK,)),
+            pltpu.SemaphoreType.DMA((2,)),
+        ],
+    )
+    part, high, source_pick, source_pair, start, weight = call(
         functools.partial(first_kernel, blocks, slots, count),
         [
             ((data_rows, width), F32),
-            (half_shape, BF16),
-            (half_shape, BF16),
-            ((tiles, data_rows), BF16),
-            ((data_rows, 2 * tiles), BF16),
+            ((tiles - loaded, width, width), BF16),
             ((tiles, cells), BF16),
             ((cells, 2 * tiles), BF16),
-            ((tiles, width), F32),
             ((cells, width), F32),
             ((cells, width), F32),
         ],
         codes,
-        low_turned,
-        tile_scale.reshape(1, -1),
-        tile_row.reshape(1, -1),
+        low,
+        scale,
+        rows_pair,
         tile_column.reshape(1, -1),
         place,
         *begin,
-        scratch=[pltpu.SemaphoreType.DMA((half // CHUNK,))],
-    )
+        scratch=[pltpu.SemaphoreType.DMA(((tiles - loaded) // CHUNK,))],
+    )
+
+    def turned_half(first, part):
+        (turned,) = call(
+            functools.partial(turning_kernel, first), [(half_shape, BF16)], low, high, part
+        )
+        return turned
+
+    parts = within(part)
+    low_turned = turned_half(0, part)
     (part,) = call(
         functools.partial(start_data_kernel, sharing),
         [((cells, width), F32)],
@@ -411,8 +432,11 @@
         scale,
         observed,
         data_weight,
-        *within(part),
-    )
+        low_turned,
+        *parts,
+    )
+    parts = across([part] * count)
+    high_turned = turned_half(half, part)
     part, first = call(
         functools.partial(start_residual_kernel, blocks, count),
         [((data_rows + EXTRA, width), F32), ((cells, width), F32)],
@@ -423,7 +447,7 @@
         scale,
         start,
         weight,
-        *across([part] * count),
+        *parts,
     )
     part, predicted, sums = call(
         functools.partial(image_data_kernel, sharing),

time: 56.8 us -> 56.4 us (level)
  waiting for transfers between devices: 16.1 us -> 13.8 us
  Pallas kernels: 15.1 us -> 17 us
    ppermute x21, waiting for transfers between devices: 16.1 us -> 13.8 us  [exchange(): parts[shift] = lax.ppermute(values[shift], axes, perm)]
    pallas_call x9 -> x11, Pallas kernels: 15.1 us -> 17 us  [call(): pl.pallas_call(body, out_shape=[jax.ShapeDtypeStruct(shape, dtype) for sh...]
  transfers between devices with their start and end apart: 21 -> 21, of which waited for: 14 -> 13; matrix products, arithmetic and copies ran while one was open for 0% -> 0% of each run, Pallas kernels for 5% -> 9%
where the time goes in v2:
time: 56.4 us; the launch traced here: 56.2 us
  starting transfers between devices  24.6 us (44%)
  Pallas kernels  17 us (30%)
  waiting for transfers between devices  13.8 us (24%)
  between operations  0.72 us (1%)
    ppermute x21, starting transfers between devices, exchange(): parts[shift] = lax.ppermute(values[shift], axes, perm)  24.6 us
    pallas_call x11, Pallas kernels, call(): pl.pallas_call(body, out_shape=[jax.ShapeDtypeStruct(shape, dtype) for sh...  17 us
    ppermute x21, waiting for transfers between devices, exchange(): parts[shift] = lax.ppermute(values[shift], axes, perm)  13.8 us
  transfers between devices with their start and end apart: 21, of which 13 were waited for; matrix products, arithmetic and copies ran while one was open for 0% of the time, Pallas kernels for 9%

profile of v2, /device:TPU:0, one launch (start us, length us, event | category | flops | bytes accessed | tf_op | source)
XLA Modules:
  0.0 56.2 jit_solution(10068191533967237770)
XLA Ops:
  0.6 0.7 %shard_map.104.opening.refs_6_ = f32[16,256]{1,0:T(8,128)S(1)} custom-call(f32[4,256]{1,0:T(4,128)} %start.1, f32[4,256]{1,0:T(4,128)} %weight.1, s32[2,4]{1,0:T(2,128)} %bitcast.8), custom_call_target="tpu_custom_call" | custom-call | tf_op jit(solution)/shard_map/pallas_call | solution.py:323
  1.4 5.1 %collective-permute-start.2 = (f32[16,256]{1,0:T(8,128)S(1)}, f32[16,256]{1,0:T(8,128)S(1)}, u32[]{:S(2)}, u32[]{:S(2)}) collective-permute-start(f32[16,256]{1,0:T(8,128)S(1)} %shard_map.104.opening.refs_6_), channel_id=1, source_target_pairs={{0,12},{4,8},{8,4},{12,0},{1,13},{5,9},{9,5},{13,1},{2,14},{6,10},... | collective-permute-start | bytes 49160 | tf_op jit(solution)/shard_map/ppermute | solution.py:23
  6.5 0.0 collective-permute-start.1
  6.5 0.6 %collective-permute-start = (f32[16,256]{1,0:T(8,128)S(1)}, f32[16,256]{1,0:T(8,128)S(1)}, u32[]{:S(2)}, u32[]{:S(2)}) collective-permute-start(f32[16,256]{1,0:T(8,128)S(1)} %shard_map.104.opening.refs_6_), channel_id=1, source_target_pairs={{0,4},{4,0},{8,12},{12,8},{1,5},{5,1},{9,13},{13,9},{2,6},{6,2},{1... | collective-permute-start | bytes 49160 | tf_op jit(solution)/shard_map/ppermute | solution.py:23
  7.1 0.0 copy-start.2
  7.1 2.9 %shard_map.105 = (bf16[48,256,256]{2,1,0:T(8,128)(2,1)S(1)}, bf16[64,16]{1,0:T(8,128)(2,1)S(1)}, bf16[16,128]{1,0:T(8,128)(2,1)S(1)}, f32[64,256]{1,0:T(8,128)S(1)}) custom-call(bf16[64,256,256]{2,1,0:T(8,128)(2,1)} %refs_0_.1, f32[16,256]{1,0:T(8,128)S(1)} %shard_map.104.opening.refs_6_, f32[1,64]{1,0:T(1,128)} %bitcast.9, s32[1,64]{1,0:T(1,128)} %bitcast.10), custom_call_target="tpu_custom_call" | custom-call | tf_op jit(solution)/shard_map/pallas_call | solution.py:323
  10.1 0.0 collective-permute-done.2.refs_9_
  10.1 1.1 %collective-permute-done.1.refs_8_ = f32[16,256]{1,0:T(8,128)S(1)} collective-permute-done((f32[16,256]{1,0:T(8,128)S(1)}, f32[16,256]{1,0:T(8,128)S(1)}, u32[]{:S(2)}, u32[]{:S(2)}) %collective-permute-start.1) | collective-permute-done | bytes 16416 | tf_op jit(solution)/shard_map/ppermute | solution.py:23
  11.1 0.0 collective-permute-done.refs_7_
  11.1 0.0 copy-done.2
  11.1 2.9 %shard_map.106 = (f32[16,256]{1,0:T(8,128)S(1)}, bf16[16,256,256]{2,1,0:T(8,128)(2,1)S(1)}, bf16[64,16]{1,0:T(8,128)(2,1)S(1)}, bf16[16,128]{1,0:T(8,128)(2,1)S(...) custom-call(bf16[64,256,256]{2,1,0:T(8,128)(2,1)} %refs_0_.1, ...), custom_call_target="tpu_custom_call" | custom-call | tf_op jit(solution)/shard_map/pallas_call | solution.py:323
  14.0 0.1 collective-permute-start.5
  14.1 1.6 %collective-permute-start.4 = (f32[16,256]{1,0:T(8,128)S(1)}, f32[16,256]{1,0:T(8,128)S(1)}, u32[]{:S(2)}, u32[]{:S(2)}) collective-permute-start(f32[16,256]{1,0:T(8,128)S(1)} %get-tuple-element.31.part.refs_8_), channel_id=1, source_target_pairs={{0,2},{1,3},{2,0},{3,1},{4,6},{5,7},{6,4},{7,5},{8,10},{9,11},{10,... | collective-permute-start | bytes 49160 | tf_op jit(solution)/shard_map/ppermute | solution.py:23
  15.7 0.3 collective-permute-start.3
  16.0 0.0 copy-start
  16.0 0.0 copy-start.1
  16.0 1.1 %shard_map.107.refs_7_.refs_0_ = bf16[32,256,256]{2,1,0:T(8,128)(2,1)S(1)} custom-call(bf16[48,256,256]{2,1,0:T(8,128)(2,1)S(1)} %get-tuple-element.25.refs_1_.low.refs_0_, bf16[16,256,256]{2,1,0:T(8,128)(2,1)S(1)} %get-tuple-element.30.high.refs_1_, f32[16,256]{1,0:T(8,128)S(1)} %get-tuple-element.31.part.refs_8_), custom_call_target="tpu_custom_call" | custom-call | tf_op jit(solution)/shard_map/pallas_call | solution.py:323
  17.1 0.3 collective-permute-done.5.refs_11_
  17.4 0.5 collective-permute-done.4.refs_10_
  17.9 0.0 collective-permute-done.3.refs_9_
  17.9 0.0 copy-done
  17.9 0.0 copy-done.1
  17.9 1.4 %shard_map.108.part.refs_7_ = f32[16,256]{1,0:T(8,128)S(1)} custom-call(bf16[48,256,256]{2,1,0:T(8,128)(2,1)S(1)} %get-tuple-element.25.refs_1_.low.refs_0_, bf16[16,256,256]{2,1,0:T(8,128)(2,1)S(1)} %get-tuple-element.30.high.refs_1_, bf16[64,16]{1,0:T(8,128)(2,1)S(1)} %get-tuple-element.32.refs_2_, bf16[16,128]{1,0:T(8,128)(2,1)S(1)} %get-tuple-element.33.refs_3_, ...), custom_call_target="tpu_custom_call" | custom-call | tf_op jit(solution)/shard_map/pallas_call | solution.py:323
  19.4 2.7 %collective-permute-start.8 = (f32[16,256]{1,0:T(8,128)S(1)}, f32[16,256]{1,0:T(8,128)S(1)}, u32[]{:S(2)}, u32[]{:S(2)}) collective-permute-start(f32[16,256]{1,0:T(8,128)S(1)} %shard_map.108.part.refs_7_), channel_id=1, source_target_pairs={{0,12},{4,8},{8,4},{12,0},{1,13},{5,9},{9,5},{13,1},{2,14},{6,10},... | collective-permute-start | bytes 49160 | tf_op jit(solution)/shard_map/ppermute | solution.py:23
  22.1 0.0 collective-permute-start.7
  22.1 1.7 %collective-permute-start.6 = (f32[16,256]{1,0:T(8,128)S(1)}, f32[16,256]{1,0:T(8,128)S(1)}, u32[]{:S(2)}, u32[]{:S(2)}) collective-permute-start(f32[16,256]{1,0:T(8,128)S(1)} %shard_map.108.part.refs_7_), channel_id=1, source_target_pairs={{0,4},{4,0},{8,12},{12,8},{1,5},{5,1},{9,13},{13,9},{2,6},{6,2},{1... | collective-permute-start | bytes 49160 | tf_op jit(solution)/shard_map/ppermute | solution.py:23
  23.8 1.1 %shard_map.109.refs_1_ = bf16[32,256,256]{2,1,0:T(8,128)(2,1)S(1)} custom-call(bf16[48,256,256]{2,1,0:T(8,128)(2,1)S(1)} %get-tuple-element.25.refs_1_.low.refs_0_, bf16[16,256,256]{2,1,0:T(8,128)(2,1)S(1)} %get-tuple-element.30.high.refs_1_, f32[16,256]{1,0:T(8,128)S(1)} %shard_map.108.part.refs_7_), custom_call_target="tpu_custom_call" | custom-call | tf_op jit(solution)/shard_map/pallas_call | solution.py:323
  24.9 0.0 collective-permute-done.8.refs_10_
  24.9 1.8 %collective-permute-done.7.refs_9_ = f32[16,256]{1,0:T(8,128)S(1)} collective-permute-done((f32[16,256]{1,0:T(8,128)S(1)}, f32[16,256]{1,0:T(8,128)S(1)}, u32[]{:S(2)}, u32[]{:S(2)}) %collective-permute-start.7) | collective-permute-done | bytes 16416 | tf_op jit(solution)/shard_map/ppermute | solution.py:23
  26.7 0.0 collective-permute-done.6.refs_8_
  26.8 1.4 %shard_map.110 = (f32[24,256]{1,0:T(8,128)S(1)}, f32[16,256]{1,0:T(8,128)S(1)}) custom-call(bf16[32,256,256]{2,1,0:T(8,128)(2,1)S(1)} %shard_map.107.refs_7_.refs_0_, bf16[32,256,256]{2,1,0:T(8,128)(2,1)S(1)} %shard_map.109.refs_1_, bf16[64,16]{1,0:T(8,128)(2,1)S(1)} %get-tuple-element.34.refs_2_, bf16[16,128]{1,0:T(8,128)(2,1)S(1)} %get-tuple-element.27.refs_3_, ...), custom_call_target="tpu_custom_call" | custom-call | tf_op jit(solution)/shard_map/pallas_call | solution.py:323
  28.2 0.0 collective-permute-start.11
  28.2 1.5 %collective-permute-start.10 = (f32[24,256]{1,0:T(8,128)S(1)}, f32[24,256]{1,0:T(8,128)S(1)}, u32[]{:S(2)}, u32[]{:S(2)}) collective-permute-start(f32[24,256]{1,0:T(8,128)S(1)} %get-tuple-element.36.refs_6_), channel_id=1, source_target_pairs={{0,2},{1,3},{2,0},{3,1},{4,6},{5,7},{6,4},{7,5},{8,10},{9,11},{10,... | collective-permute-start | bytes 73736 | tf_op jit(solution)/shard_map/ppermute | solution.py:23
  29.7 0.3 collective-permute-start.9
  30.0 1.6 %collective-permute-done.11.refs_9_ = f32[24,256]{1,0:T(8,128)S(1)} collective-permute-done((f32[24,256]{1,0:T(8,128)S(1)}, f32[24,256]{1,0:T(8,128)S(1)}, u32[]{:S(2)}, u32[]{:S(2)}) %collective-permute-start.11) | collective-permute-done | bytes 24608 | tf_op jit(solution)/shard_map/ppermute | solution.py:23
  31.7 0.4 collective-permute-done.10.refs_8_
  32.1 0.0 collective-permute-done.9.refs_7_
  32.1 1.4 %shard_map.111 = (f32[24,256]{1,0:T(8,128)S(1)}, f32[16,256]{1,0:T(8,128)S(1)}, f32[8,256]{1,0:T(8,128)S(1)}) custom-call(bf16[48,256,256]{2,1,0:T(8,128)(2,1)S(1)} %get-tuple-element.25.refs_1_.low.refs_0_, bf16[16,256,256]{2,1,0:T(8,128)(2,1)S(1)} %get-tuple-element.30.high.refs_1_, bf16[64,16]{1,0:T(8,128)(2,1)S(1)} %get-tuple-element.32.refs_2_, ...), custom_call_target="tpu_custom_call" | custom-call | tf_op jit(solution)/shard_map/pallas_call | solution.py:323
  33.5 1.5 %collective-permute-start.14 = (f32[24,256]{1,0:T(8,128)S(1)}, f32[24,256]{1,0:T(8,128)S(1)}, u32[]{:S(2)}, u32[]{:S(2)}) collective-permute-start(f32[24,256]{1,0:T(8,128)S(1)} %get-tuple-element.38.refs_8_), channel_id=1, source_target_pairs={{0,12},{4,8},{8,4},{12,0},{1,13},{5,9},{9,5},{13,1},{2,14},{6,10},... | collective-permute-start | bytes 73736 | tf_op jit(solution)/shard_map/ppermute | solution.py:23
  35.0 0.8 %collective-permute-start.13 = (f32[24,256]{1,0:T(8,128)S(1)}, f32[24,256]{1,0:T(8,128)S(1)}, u32[]{:S(2)}, u32[]{:S(2)}) collective-permute-start(f32[24,256]{1,0:T(8,128)S(1)} %get-tuple-element.38.refs_8_), channel_id=1, source_target_pairs={{0,8},{4,12},{8,0},{12,4},{1,9},{5,13},{9,1},{13,5},{2,10},{6,14},... | collective-permute-start | bytes 73736 | tf_op jit(solution)/shard_map/ppermute | solution.py:23
  35.8 2.2 %collective-permute-start.12 = (f32[24,256]{1,0:T(8,128)S(1)}, f32[24,256]{1,0:T(8,128)S(1)}, u32[]{:S(2)}, u32[]{:S(2)}) collective-permute-start(f32[24,256]{1,0:T(8,128)S(1)} %get-tuple-element.38.refs_8_), channel_id=1, source_target_pairs={{0,4},{4,0},{8,12},{12,8},{1,5},{5,1},{9,13},{13,9},{2,6},{6,2},{1... | collective-permute-start | bytes 73736 | tf_op jit(solution)/shard_map/ppermute | solution.py:23
  37.9 1.3 %collective-permute-done.14.refs_11_ = f32[24,256]{1,0:T(8,128)S(1)} collective-permute-done((f32[24,256]{1,0:T(8,128)S(1)}, f32[24,256]{1,0:T(8,128)S(1)}, u32[]{:S(2)}, u32[]{:S(2)}) %collective-permute-start.14) | collective-permute-done | bytes 24608 | tf_op jit(solution)/shard_map/ppermute | solution.py:23
  39.2 0.6 collective-permute-done.13.refs_10_
  39.7 0.2 collective-permute-done.12.refs_9_
  40.0 1.5 %shard_map.112 = (f32[24,256]{1,0:T(8,128)S(1)}, f32[16,256]{1,0:T(8,128)S(1)}, f32[8,128]{1,0:T(8,128)S(1)}) custom-call(bf16[32,256,256]{2,1,0:T(8,128)(2,1)S(1)} %shard_map.107.refs_7_.refs_0_, bf16[32,256,256]{2,1,0:T(8,128)(2,1)S(1)} %shard_map.109.refs_1_, bf16[64,16]{1,0:T(8,128)(2,1)S(1)} %get-tuple-element.34.refs_2_, ...), custom_call_target="tpu_custom_call" | custom-call | tf_op jit(solution)/shard_map/pallas_call | solution.py:323
  41.5 0.0 collective-permute-start.17
  41.5 1.5 %collective-permute-start.16 = (f32[24,256]{1,0:T(8,128)S(1)}, f32[24,256]{1,0:T(8,128)S(1)}, u32[]{:S(2)}, u32[]{:S(2)}) collective-permute-start(f32[24,256]{1,0:T(8,128)S(1)} %get-tuple-element.42.refs_8_), channel_id=1, source_target_pairs={{0,2},{1,3},{2,0},{3,1},{4,6},{5,7},{6,4},{7,5},{8,10},{9,11},{10,... | collective-permute-start | bytes 73736 | tf_op jit(solution)/shard_map/ppermute | solution.py:23
  43.0 0.4 collective-permute-start.15
  43.4 1.7 %collective-permute-done.17.refs_11_ = f32[24,256]{1,0:T(8,128)S(1)} collective-permute-done((f32[24,256]{1,0:T(8,128)S(1)}, f32[24,256]{1,0:T(8,128)S(1)}, u32[]{:S(2)}, u32[]{:S(2)}) %collective-permute-start.17) | collective-permute-done | bytes 24608 | tf_op jit(solution)/shard_map/ppermute | solution.py:23
  45.0 0.4 collective-permute-done.16.refs_10_
  45.4 0.0 collective-permute-done.15.refs_9_
  45.4 1.6 %shard_map.113 = (f32[8,256]{1,0:T(8,128)S(1)}, f32[8,256]{1,0:T(8,128)S(1)}, f32[8,256]{1,0:T(8,128)S(1)}, f32[8,256]{1,0:T(8,128)S(1)}, f32[8,256]{1,0:T(8,128)S(1)}) custom-call(bf16[48,256,256]{2,1,0:T(8,128)(2,1)S(1)} %get-tuple-element.25.refs_1_.low.refs_0_, bf16[16,256,256]{2,1,0:T(8,128)(2,1)S(1)} %get-tuple-element.30.high.refs_1_, ...), custom_call_target="tpu_custom_call" | custom-call | tf_op jit(solution)/shard_map/pallas_call | solution.py:323
  47.0 1.8 %collective-permute-start.18 = (f32[8,256]{1,0:T(8,128)S(1)}, f32[8,256]{1,0:T(8,128)S(1)}, u32[]{:S(2)}, u32[]{:S(2)}) collective-permute-start(f32[8,256]{1,0:T(8,128)S(1)} %get-tuple-element.45), channel_id=1, source_target_pairs={{0,4},{4,0},{8,12},{12,8},{1,5},{5,1},{9,13},{13,9},{2,6},{6,2},{1... | collective-permute-start | bytes 24584 | tf_op jit(solution)/shard_map/ppermute | solution.py:23
  48.7 1.2 %collective-permute-start.19 = (f32[8,256]{1,0:T(8,128)S(1)}, f32[8,256]{1,0:T(8,128)S(1)}, u32[]{:S(2)}, u32[]{:S(2)}) collective-permute-start(f32[8,256]{1,0:T(8,128)S(1)} %get-tuple-element.46), channel_id=1, source_target_pairs={{0,8},{4,12},{8,0},{12,4},{1,9},{5,13},{9,1},{13,5},{2,10},{6,14},... | collective-permute-start | bytes 24584 | tf_op jit(solution)/shard_map/ppermute | solution.py:23
  49.9 1.5 %collective-permute-start.20 = (f32[8,256]{1,0:T(8,128)S(1)}, f32[8,256]{1,0:T(8,128)S(1)}, u32[]{:S(2)}, u32[]{:S(2)}) collective-permute-start(f32[8,256]{1,0:T(8,128)S(1)} %get-tuple-element.47), channel_id=1, source_target_pairs={{0,12},{4,8},{8,4},{12,0},{1,13},{5,9},{9,5},{13,1},{2,14},{6,10},... | collective-permute-start | bytes 24584 | tf_op jit(solution)/shard_map/ppermute | solution.py:23
  51.4 0.0 collective-permute-done.18.refs_7_
  51.4 1.9 %collective-permute-done.19.refs_8_ = f32[8,256]{1,0:T(8,128)S(1)} collective-permute-done((f32[8,256]{1,0:T(8,128)S(1)}, f32[8,256]{1,0:T(8,128)S(1)}, u32[]{:S(2)}, u32[]{:S(2)}) %collective-permute-start.19) | collective-permute-done | bytes 8224 | tf_op jit(solution)/shard_map/ppermute | solution.py:23
  53.3 2.1 %collective-permute-done.20.refs_9_ = f32[8,256]{1,0:T(8,128)S(1)} collective-permute-done((f32[8,256]{1,0:T(8,128)S(1)}, f32[8,256]{1,0:T(8,128)S(1)}, u32[]{:S(2)}, u32[]{:S(2)}) %collective-permute-start.20) | collective-permute-done | bytes 8224 | tf_op jit(solution)/shard_map/ppermute | solution.py:23
  55.4 0.8 %shard_map.114 = (f32[4,256]{1,0:T(4,128)}, f32[4,256]{1,0:T(4,128)}) custom-call(f32[16,256]{1,0:T(8,128)S(1)} %get-tuple-element.28.refs_6_.refs_5_.refs_0_, f32[16,256]{1,0:T(8,128)S(1)} %get-tuple-element.29.refs_5_.refs_1_, f32[16,256]{1,0:T(8,128)S(1)} %get-tuple-element.35.refs_6_.refs_2_, f32[16,256]{1,0:T(8,128)S(1)} %get-tuple-element.39.refs_3_, ...), custom_call_target="tpu_custom_call" | custom-call | tf_op jit(solution)/shard_map/pallas_call | solution.py:323
Async XLA Ops:
  1.4 8.7 %collective-permute-start.2 = (f32[16,256]{1,0:T(8,128)S(1)}, f32[16,256]{1,0:T(8,128)S(1)}, u32[]{:S(2)}, u32[]{:S(2)}) collective-permute-start(f32[16,256]{1,0:T(8,128)S(1)} %shard_map.104.opening.refs_6_), channel_id=1, source_target_pairs={{0,12},{4,8},{8,4},{12,0},{1,13},{5,9},{9,5},{13,1},{2,14},{6,10},... | collective-permute-start | bytes 49160 | tf_op jit(solution)/shard_map/ppermute | solution.py:23
  6.5 4.6 %collective-permute-start.1 = (f32[16,256]{1,0:T(8,128)S(1)}, f32[16,256]{1,0:T(8,128)S(1)}, u32[]{:S(2)}, u32[]{:S(2)}) collective-permute-start(f32[16,256]{1,0:T(8,128)S(1)} %shard_map.104.opening.refs_6_), channel_id=1, source_target_pairs={{0,8},{4,12},{8,0},{12,4},{1,9},{5,13},{9,1},{13,5},{2,10},{6,14},... | collective-permute-start | bytes 49160 | tf_op jit(solution)/shard_map/ppermute | solution.py:23
  6.5 4.6 %collective-permute-start = (f32[16,256]{1,0:T(8,128)S(1)}, f32[16,256]{1,0:T(8,128)S(1)}, u32[]{:S(2)}, u32[]{:S(2)}) collective-permute-start(f32[16,256]{1,0:T(8,128)S(1)} %shard_map.104.opening.refs_6_), channel_id=1, source_target_pairs={{0,4},{4,0},{8,12},{12,8},{1,5},{5,1},{9,13},{13,9},{2,6},{6,2},{1... | collective-permute-start | bytes 49160 | tf_op jit(solution)/shard_map/ppermute | solution.py:23
  7.1 4.0 %copy-start.2 = (s32[64]{0:T(128)S(1)}, s32[64]{0:T(128)}, u32[]{:S(2)}) copy-start(s32[64]{0:T(128)} %param.12) | copy-start | bytes 772
  14.0 3.4 %collective-permute-start.5 = (f32[16,256]{1,0:T(8,128)S(1)}, f32[16,256]{1,0:T(8,128)S(1)}, u32[]{:S(2)}, u32[]{:S(2)}) collective-permute-start(f32[16,256]{1,0:T(8,128)S(1)} %get-tuple-element.31.part.refs_8_), channel_id=1, source_target_pairs={{0,3},{1,2},{2,1},{3,0},{4,7},{5,6},{6,5},{7,4},{8,11},{9,10},{10,... | collective-permute-start | bytes 49160 | tf_op jit(solution)/shard_map/ppermute | solution.py:23
  14.1 3.8 %collective-permute-start.4 = (f32[16,256]{1,0:T(8,128)S(1)}, f32[16,256]{1,0:T(8,128)S(1)}, u32[]{:S(2)}, u32[]{:S(2)}) collective-permute-start(f32[16,256]{1,0:T(8,128)S(1)} %get-tuple-element.31.part.refs_8_), channel_id=1, source_target_pairs={{0,2},{1,3},{2,0},{3,1},{4,6},{5,7},{6,4},{7,5},{8,10},{9,11},{10,... | collective-permute-start | bytes 49160 | tf_op jit(solution)/shard_map/ppermute | solution.py:23
  15.7 2.3 %collective-permute-start.3 = (f32[16,256]{1,0:T(8,128)S(1)}, f32[16,256]{1,0:T(8,128)S(1)}, u32[]{:S(2)}, u32[]{:S(2)}) collective-permute-start(f32[16,256]{1,0:T(8,128)S(1)} %get-tuple-element.31.part.refs_8_), channel_id=1, source_target_pairs={{0,1},{1,0},{2,3},{3,2},{4,5},{5,4},{6,7},{7,6},{8,9},{9,8},{10,11... | collective-permute-start | bytes 49160 | tf_op jit(solution)/shard_map/ppermute | solution.py:23
  16.0 2.0 %copy-start = (f32[16,256]{1,0:T(8,128)S(1)}, f32[16,256]{1,0:T(8,128)}, u32[]{:S(2)}) copy-start(f32[16,256]{1,0:T(8,128)} %refs_5_.5) | copy-start | bytes 49156
  16.0 2.0 %copy-start.1 = (f32[16,256]{1,0:T(8,128)S(1)}, f32[16,256]{1,0:T(8,128)}, u32[]{:S(2)}) copy-start(f32[16,256]{1,0:T(8,128)} %refs_5_.3) | copy-start | bytes 49156
  19.4 5.6 %collective-permute-start.8 = (f32[16,256]{1,0:T(8,128)S(1)}, f32[16,256]{1,0:T(8,128)S(1)}, u32[]{:S(2)}, u32[]{:S(2)}) collective-permute-start(f32[16,256]{1,0:T(8,128)S(1)} %shard_map.108.part.refs_7_), channel_id=1, source_target_pairs={{0,12},{4,8},{8,4},{12,0},{1,13},{5,9},{9,5},{13,1},{2,14},{6,10},... | collective-permute-start | bytes 49160 | tf_op jit(solution)/shard_map/ppermute | solution.py:23
  22.1 4.6 %collective-permute-start.7 = (f32[16,256]{1,0:T(8,128)S(1)}, f32[16,256]{1,0:T(8,128)S(1)}, u32[]{:S(2)}, u32[]{:S(2)}) collective-permute-start(f32[16,256]{1,0:T(8,128)S(1)} %shard_map.108.part.refs_7_), channel_id=1, source_target_pairs={{0,8},{4,12},{8,0},{12,4},{1,9},{5,13},{9,1},{13,5},{2,10},{6,14},... | collective-permute-start | bytes 49160 | tf_op jit(solution)/shard_map/ppermute | solution.py:23
  22.1 4.6 %collective-permute-start.6 = (f32[16,256]{1,0:T(8,128)S(1)}, f32[16,256]{1,0:T(8,128)S(1)}, u32[]{:S(2)}, u32[]{:S(2)}) collective-permute-start(f32[16,256]{1,0:T(8,128)S(1)} %shard_map.108.part.refs_7_), channel_id=1, source_target_pairs={{0,4},{4,0},{8,12},{12,8},{1,5},{5,1},{9,13},{13,9},{2,6},{6,2},{1... | collective-permute-start | bytes 49160 | tf_op jit(solution)/shard_map/ppermute | solution.py:23
  28.2 3.5 %collective-permute-start.11 = (f32[24,256]{1,0:T(8,128)S(1)}, f32[24,256]{1,0:T(8,128)S(1)}, u32[]{:S(2)}, u32[]{:S(2)}) collective-permute-start(f32[24,256]{1,0:T(8,128)S(1)} %get-tuple-element.36.refs_6_), channel_id=1, source_target_pairs={{0,3},{1,2},{2,1},{3,0},{4,7},{5,6},{6,5},{7,4},{8,11},{9,10},{10,... | collective-permute-start | bytes 73736 | tf_op jit(solution)/shard_map/ppermute | solution.py:23
  28.2 3.9 %collective-permute-start.10 = (f32[24,256]{1,0:T(8,128)S(1)}, f32[24,256]{1,0:T(8,128)S(1)}, u32[]{:S(2)}, u32[]{:S(2)}) collective-permute-start(f32[24,256]{1,0:T(8,128)S(1)} %get-tuple-element.36.refs_6_), channel_id=1, source_target_pairs={{0,2},{1,3},{2,0},{3,1},{4,6},{5,7},{6,4},{7,5},{8,10},{9,11},{10,... | collective-permute-start | bytes 73736 | tf_op jit(solution)/shard_map/ppermute | solution.py:23
  29.7 2.4 %collective-permute-start.9 = (f32[24,256]{1,0:T(8,128)S(1)}, f32[24,256]{1,0:T(8,128)S(1)}, u32[]{:S(2)}, u32[]{:S(2)}) collective-permute-start(f32[24,256]{1,0:T(8,128)S(1)} %get-tuple-element.36.refs_6_), channel_id=1, source_target_pairs={{0,1},{1,0},{2,3},{3,2},{4,5},{5,4},{6,7},{7,6},{8,9},{9,8},{10,11... | collective-permute-start | bytes 73736 | tf_op jit(solution)/shard_map/ppermute | solution.py:23
  33.5 5.7 %collective-permute-start.14 = (f32[24,256]{1,0:T(8,128)S(1)}, f32[24,256]{1,0:T(8,128)S(1)}, u32[]{:S(2)}, u32[]{:S(2)}) collective-permute-start(f32[24,256]{1,0:T(8,128)S(1)} %get-tuple-element.38.refs_8_), channel_id=1, source_target_pairs={{0,12},{4,8},{8,4},{12,0},{1,13},{5,9},{9,5},{13,1},{2,14},{6,10},... | collective-permute-start | bytes 73736 | tf_op jit(solution)/shard_map/ppermute | solution.py:23
  35.0 4.8 %collective-permute-start.13 = (f32[24,256]{1,0:T(8,128)S(1)}, f32[24,256]{1,0:T(8,128)S(1)}, u32[]{:S(2)}, u32[]{:S(2)}) collective-permute-start(f32[24,256]{1,0:T(8,128)S(1)} %get-tuple-element.38.refs_8_), channel_id=1, source_target_pairs={{0,8},{4,12},{8,0},{12,4},{1,9},{5,13},{9,1},{13,5},{2,10},{6,14},... | collective-permute-start | bytes 73736 | tf_op jit(solution)/shard_map/ppermute | solution.py:23
  35.8 4.2 %collective-permute-start.12 = (f32[24,256]{1,0:T(8,128)S(1)}, f32[24,256]{1,0:T(8,128)S(1)}, u32[]{:S(2)}, u32[]{:S(2)}) collective-permute-start(f32[24,256]{1,0:T(8,128)S(1)} %get-tuple-element.38.refs_8_), channel_id=1, source_target_pairs={{0,4},{4,0},{8,12},{12,8},{1,5},{5,1},{9,13},{13,9},{2,6},{6,2},{1... | collective-permute-start | bytes 73736 | tf_op jit(solution)/shard_map/ppermute | solution.py:23
  41.5 3.5 %collective-permute-start.17 = (f32[24,256]{1,0:T(8,128)S(1)}, f32[24,256]{1,0:T(8,128)S(1)}, u32[]{:S(2)}, u32[]{:S(2)}) collective-permute-start(f32[24,256]{1,0:T(8,128)S(1)} %get-tuple-element.42.refs_8_), channel_id=1, source_target_pairs={{0,3},{1,2},{2,1},{3,0},{4,7},{5,6},{6,5},{7,4},{8,11},{9,10},{10,... | collective-permute-start | bytes 73736 | tf_op jit(solution)/shard_map/ppermute | solution.py:23
  41.5 3.9 %collective-permute-start.16 = (f32[24,256]{1,0:T(8,128)S(1)}, f32[24,256]{1,0:T(8,128)S(1)}, u32[]{:S(2)}, u32[]{:S(2)}) collective-permute-start(f32[24,256]{1,0:T(8,128)S(1)} %get-tuple-element.42.refs_8_), channel_id=1, source_target_pairs={{0,2},{1,3},{2,0},{3,1},{4,6},{5,7},{6,4},{7,5},{8,10},{9,11},{10,... | collective-permute-start | bytes 73736 | tf_op jit(solution)/shard_map/ppermute | solution.py:23
  43.0 2.4 %collective-permute-start.15 = (f32[24,256]{1,0:T(8,128)S(1)}, f32[24,256]{1,0:T(8,128)S(1)}, u32[]{:S(2)}, u32[]{:S(2)}) collective-permute-start(f32[24,256]{1,0:T(8,128)S(1)} %get-tuple-element.42.refs_8_), channel_id=1, source_target_pairs={{0,1},{1,0},{2,3},{3,2},{4,5},{5,4},{6,7},{7,6},{8,9},{9,8},{10,11... | collective-permute-start | bytes 73736 | tf_op jit(solution)/shard_map/ppermute | solution.py:23
  47.0 4.4 %collective-permute-start.18 = (f32[8,256]{1,0:T(8,128)S(1)}, f32[8,256]{1,0:T(8,128)S(1)}, u32[]{:S(2)}, u32[]{:S(2)}) collective-permute-start(f32[8,256]{1,0:T(8,128)S(1)} %get-tuple-element.45), channel_id=1, source_target_pairs={{0,4},{4,0},{8,12},{12,8},{1,5},{5,1},{9,13},{13,9},{2,6},{6,2},{1... | collective-permute-start | bytes 24584 | tf_op jit(solution)/shard_map/ppermute | solution.py:23
  48.7 4.5 %collective-permute-start.19 = (f32[8,256]{1,0:T(8,128)S(1)}, f32[8,256]{1,0:T(8,128)S(1)}, u32[]{:S(2)}, u32[]{:S(2)}) collective-permute-start(f32[8,256]{1,0:T(8,128)S(1)} %get-tuple-element.46), channel_id=1, source_target_pairs={{0,8},{4,12},{8,0},{12,4},{1,9},{5,13},{9,1},{13,5},{2,10},{6,14},... | collective-permute-start | bytes 24584 | tf_op jit(solution)/shard_map/ppermute | solution.py:23
  49.9 5.4 %collective-permute-start.20 = (f32[8,256]{1,0:T(8,128)S(1)}, f32[8,256]{1,0:T(8,128)S(1)}, u32[]{:S(2)}, u32[]{:S(2)}) collective-permute-start(f32[8,256]{1,0:T(8,128)S(1)} %get-tuple-element.47), channel_id=1, source_target_pairs={{0,12},{4,8},{8,4},{12,0},{1,13},{5,9},{9,5},{13,1},{2,14},{6,10},... | collective-permute-start | bytes 24584 | tf_op jit(solution)/shard_map/ppermute | solution.py:23

commit v3 on v2

--- a/solution.py
+++ b/solution.py
@@ -66,24 +66,18 @@
     return jnp.concatenate(filled, axis=0)
 
 
-def products(tile_of, picked, turn=False):
+def products(codes, picked):
     tiles, width = picked.shape
     index = lax.broadcasted_iota(jnp.int32, (GROUP, width), 0)
-    dims = (((1,), (1 if turn else 0,)), ((), ()))
     pieces = []
     for first in range(0, tiles, GROUP):
         rows = picked[first : first + GROUP, :]
         total = None
         for i in range(GROUP):
-            value = lax.dot_general(rows, tile_of(first + i), dims, preferred_element_type=F32)
+            value = jnp.dot(rows, codes[first + i], preferred_element_type=F32)
             total = value if total is None else jnp.where(index == i, value, total)
         pieces.append(total)
     return jnp.concatenate(pieces, axis=0)
-
-
-def kept_tiles(low, high):
-    half = low.shape[0]
-    return lambda k: low[k] if k < half else high[k - half]
 
 
 def pick(table, values):
@@ -106,28 +100,18 @@
     pairs[...] = jnp.concatenate([ones, ones], axis=1).astype(BF16)
 
 
-def chunk_copies(codes, first, kept, done):
-    copies = []
-    for chunk in range(kept.shape[0] // CHUNK):
-        source = codes.at[pl.ds(first + chunk * CHUNK, CHUNK)]
-        target = kept.at[pl.ds(chunk * CHUNK, CHUNK)]
-        copies.append(pltpu.make_async_copy(source, target, done.at[chunk]))
-        copies[-1].start()
-    return copies
-
-
-def loading_kernel(
-    codes, opening, far_scale, far_row, low, rows_pick, rows_pair, wide_scale, scale, row, done, small
-):
-    near = [
-        pltpu.make_async_copy(far_scale, scale, small.at[0]),
-        pltpu.make_async_copy(far_row, row, small.at[1]),
+def turning_kernel(codes, opening, far_scale, far_row, *refs):
+    turned, rows_pick, rows_pair, wide_scale, scale, row, done = refs
+    copies = [
+        pltpu.make_async_copy(far_scale, scale, done.at[0]),
+        pltpu.make_async_copy(far_row, row, done.at[1]),
     ]
-    for copy in near:
+    for copy in copies:
         copy.start()
-    copies = chunk_copies(codes, 0, low, done)
     tiles, width = wide_scale.shape
-    for copy in near:
+    for k in range(tiles):
+        turned[k] = codes[k].T
+    for copy in copies:
         copy.wait()
     tables(row[...], rows_pick.shape[1], rows_pick, rows_pair)
     square = (tiles, tiles)
@@ -138,14 +122,6 @@
         precision=HIGH,
         preferred_element_type=F32,
     )
-    for copy in copies:
-        copy.wait()
-
-
-def turning_kernel(first, low, high, part, turned):
-    tile_of = kept_tiles(low, high)
-    for k in range(turned.shape[0]):
-        turned[k] = tile_of(first + k).T
 
 
 def opening_kernel(start, weight, named, out, sources, weights, names, done):
@@ -168,11 +144,9 @@
 
 
 def first_kernel(blocks, slots, count, *refs):
-    codes, low, scale, rows_pair, column, place = refs[:6]
-    parts = refs[6 : 6 + count]
-    out, high, source_pick, source_pair, start, weight, done = refs[6 + count :]
-    loaded = low.shape[0]
-    copies = chunk_copies(codes, loaded, high, done)
+    turned, scale, rows_pair, column, place = refs[:5]
+    parts = refs[5 : 5 + count]
+    out, source_pick, source_pair, start, weight = refs[5 + count :]
     width = out.shape[1]
     here = place[0]
     columns_of = column[...]
@@ -190,36 +164,28 @@
     start[...] = field
     weight[...] = jnp.concatenate([part[blocks : 2 * blocks, :] for part in parts], axis=0)
 
-    def tile_of(k):
-        if k < loaded:
-            return low[k]
-        k -= loaded
-        if k % CHUNK == 0:
-            copies[k // CHUNK].wait()
-        return high[k]
-
-    terms = products(tile_of, pick(source_pick[...], field.astype(BF16)), turn=True)
+    terms = products(turned, pick(source_pick[...], field.astype(BF16)))
     out[...] = gather(rows_pair[...], scale[...], terms)
 
 
 def start_data_kernel(count, *refs):
-    low, high, rows_pick, source_pair, scale, observed, data_weight, turned = refs[:8]
-    parts = refs[8 : 8 + count]
-    out = refs[8 + count]
+    codes, rows_pick, source_pair, scale, observed, data_weight = refs[:6]
+    parts = refs[6 : 6 + count]
+    out = refs[6 + count]
     total = total_rows(parts)
     data = (data_weight[...] * (observed[...] - total)).astype(BF16)
-    terms = products(kept_tiles(low, high), pick(rows_pick[...], data))
+    terms = products(codes, pick(rows_pick[...], data))
     out[...] = gather(source_pair[...], scale[...], terms)
 
 
 def start_residual_kernel(blocks, count, *refs):
-    low, high, source_pick, rows_pair, scale, start, weight = refs[:7]
-    parts = refs[7 : 7 + count]
-    out, residual = refs[7 + count :]
+    codes, source_pick, rows_pair, scale, start, weight = refs[:6]
+    parts = refs[6 : 6 + count]
+    out, residual = refs[6 + count :]
     weights = weight[...]
     value = total_blocks(parts, blocks) - weights * start[...]
     residual[...] = value
-    terms = products(kept_tiles(low, high), pick(source_pick[...], value.astype(BF16)))
+    terms = products(codes, pick(source_pick[...], value.astype(BF16)))
     data_rows = rows_pair.shape[0]
     out[:data_rows, :] = gather(rows_pair[...], scale[...], terms)
     out[data_rows:, :] = pack_rows(
@@ -228,25 +194,25 @@
 
 
 def image_data_kernel(count, *refs):
-    low, high, rows_pick, source_pair, scale, data_weight = refs[:6]
-    parts = refs[6 : 6 + count]
-    out, predicted, sums = refs[6 + count :]
+    codes, rows_pick, source_pair, scale, data_weight = refs[:5]
+    parts = refs[5 : 5 + count]
+    out, predicted, sums = refs[5 + count :]
     data_rows = data_weight.shape[0]
     whole_part = total_rows(parts)
     total = whole_part[:data_rows, :]
     predicted[...] = total
     sums[...] = whole_part[data_rows:, :]
     data = (data_weight[...] * (0.0 - total)).astype(BF16)
-    terms = products(kept_tiles(low, high), pick(rows_pick[...], data))
+    terms = products(codes, pick(rows_pick[...], data))
     cells = source_pair.shape[0]
     out[:cells, :] = gather(source_pair[...], scale[...], terms)
     out[cells:, :] = pack_rows([columns(total * data.astype(F32))], total.shape[1])
 
 
 def residual_kernel(blocks, count, *refs):
-    low, high, source_pick, rows_pair, scale, weight, direction, sums = refs[:8]
-    parts = refs[8 : 8 + count]
-    out, residual, step = refs[8 + count :]
+    codes, source_pick, rows_pair, scale, weight, direction, sums = refs[:7]
+    parts = refs[7 : 7 + count]
+    out, residual, step = refs[7 + count :]
     cells = source_pick.shape[1]
     weights = weight[...]
     along = direction[...]
@@ -256,7 +222,7 @@
     step[...] = jnp.broadcast_to(alpha, step.shape)
     value = residual_of(along, alpha, image)
     residual[...] = value
-    terms = products(kept_tiles(low, high), pick(source_pick[...], value.astype(BF16)))
+    terms = products(codes, pick(source_pick[...], value.astype(BF16)))
     data_rows = rows_pair.shape[0]
     out[:data_rows, :] = gather(rows_pair[...], scale[...], terms)
     weighted = value * weights
@@ -271,9 +237,9 @@
 
 
 def second_data_kernel(blocks, count, *refs):
-    low, high, rows_pick, source_pair, scale, data_weight, predicted, sums = refs[:8]
-    parts = refs[8 : 8 + count]
-    outs, scalars = refs[8 + count : -1], refs[-1]
+    codes, rows_pick, source_pair, scale, data_weight, predicted, sums = refs[:7]
+    parts = refs[7 : 7 + count]
+    outs, scalars = refs[7 + count : -1], refs[-1]
     data_rows = data_weight.shape[0]
     whole_part = total_rows(parts)
     norm = whole(whole_part[data_rows : data_rows + 1, :])
@@ -285,7 +251,7 @@
     )
     total = whole_part[:data_rows, :] + beta * predicted[...]
     data = (data_weight[...] * (0.0 - total)).astype(BF16)
-    terms = products(kept_tiles(low, high), pick(rows_pick[...], data))
+    terms = products(codes, pick(rows_pick[...], data))
     cells = gather(source_pair[...], scale[...], terms)
     curved = columns(total * data.astype(F32))
     for group, out in enumerate(outs):
@@ -314,7 +280,7 @@
     residual[...] = left - alpha * image
 
 
-def call(body, outs, *args, scratch=()):
+def call(body, outs, *args, scratch=(), cost=None):
     specs = []
     for arg in args:
         far = getattr(jax.typeof(arg), "memory_space", None) == pltpu.HBM
@@ -326,6 +292,7 @@
         in_specs=specs,
         out_specs=[pl.BlockSpec(memory_space=pltpu.VMEM)] * len(outs),
         scratch_shapes=list(scratch),
+        cost_estimate=cost,
         compiler_params=pltpu.CompilerParams(vmem_limit_bytes=LIMIT),
     )(*args)
 
@@ -348,10 +315,7 @@
     count = lax.axis_size("tiles")
     sharing = lax.axis_size(("split", "depth"))
     cells = count * blocks
-    half = tiles // 2
-    loaded = tiles * 3 // 4
-    codes = pltpu.with_memory_space_constraint(tile_codes, pltpu.HBM)
-    half_shape = (half, width, width)
+    codes = tile_codes
     place = lax.axis_index("tiles").astype(jnp.int32).reshape(1)
 
     def across(values):
@@ -373,12 +337,13 @@
             pltpu.VMEM((slots, count), jnp.int32),
             pltpu.SemaphoreType.DMA((3,)),
         ],
+        cost=pl.CostEstimate(flops=16 * width * codes.size, transcendentals=0, bytes_accessed=0),
     )
     begin = across([opening] * count)
-    low, rows_pick, rows_pair, scale = call(
-        loading_kernel,
+    turned, rows_pick, rows_pair, scale = call(
+        turning_kernel,
         [
-            ((loaded, width, width), BF16),
+            (codes.shape, BF16),
             ((tiles, data_rows), BF16),
             ((data_rows, 2 * tiles), BF16),
             ((tiles, width), F32),
@@ -390,70 +355,51 @@
         scratch=[
             pltpu.VMEM((1, tiles), F32),
             pltpu.VMEM((1, tiles), jnp.int32),
-            pltpu.SemaphoreType.DMA((loaded // CHUNK,)),
             pltpu.SemaphoreType.DMA((2,)),
         ],
     )
-    part, high, source_pick, source_pair, start, weight = call(
+    part, source_pick, source_pair, start, weight = call(
         functools.partial(first_kernel, blocks, slots, count),
         [
             ((data_rows, width), F32),
-            ((tiles - loaded, width, width), BF16),
             ((tiles, cells), BF16),
             ((cells, 2 * tiles), BF16),
             ((cells, width), F32),
             ((cells, width), F32),
         ],
-        codes,
-        low,
+        turned,
         scale,
         rows_pair,
         tile_column.reshape(1, -1),
         place,
         *begin,
-        scratch=[pltpu.SemaphoreType.DMA(((tiles - loaded) // CHUNK,))],
-    )
-
-    def turned_half(first, part):
-        (turned,) = call(
-            functools.partial(turning_kernel, first), [(half_shape, BF16)], low, high, part
-        )
-        return turned
-
-    parts = within(part)
-    low_turned = turned_half(0, part)
+    )
     (part,) = call(
         functools.partial(start_data_kernel, sharing),
         [((cells, width), F32)],
-        low,
-        high,
+        codes,
         rows_pick,
         source_pair,
         scale,
         observed,
         data_weight,
-        low_turned,
-        *parts,
-    )
-    parts = across([part] * count)
-    high_turned = turned_half(half, part)
+        *within(part),
+    )
     part, first = call(
         functools.partial(start_residual_kernel, blocks, count),
         [((data_rows + EXTRA, width), F32), ((cells, width), F32)],
-        low_turned,
-        high_turned,
+        turned,
         source_pick,
         rows_pair,
         scale,
         start,
         weight,
-        *parts,
+        *across([part] * count),
     )
     part, predicted, sums = call(
         functools.partial(image_data_kernel, sharing),
         [((cells + EXTRA, width), F32), ((data_rows, width), F32), ((EXTRA, width), F32)],
-        low,
-        high,
+        codes,
         rows_pick,
         source_pair,
         scale,
@@ -463,8 +409,7 @@
     part, second, step = call(
         functools.partial(residual_kernel, blocks, count),
         [((data_rows + EXTRA, width), F32), ((cells, width), F32), ((8, 128), F32)],
-        low_turned,
-        high_turned,
+        turned,
         source_pick,
         rows_pair,
         scale,
@@ -476,8 +421,7 @@
     *part, scalars = call(
         functools.partial(second_data_kernel, blocks, sharing),
         [((blocks + 4, width), F32)] * count + [((EXTRA, width), F32)],
-        low,
-        high,
+        codes,
         rows_pick,
         source_pair,
         scale,

time: 56.4 us -> 57.9 us (1.027)
  Pallas kernels: 17 us -> 12.9 us
  local copies, waits for them, and re-layouts: 0.01 us -> 3.41 us
  waiting for transfers between devices: 13.8 us -> 16.1 us
    pallas_call x11 -> x9, Pallas kernels: 17 us -> 12.9 us  [call(): pl.pallas_call(body, out_shape=[jax.ShapeDtypeStruct(shape, dtype) for sh...]
    unnamed x6 -> x12, local copies, waits for them, and re-layouts: 0.01 us -> 3.41 us
    ppermute x21, waiting for transfers between devices: 13.8 us -> 16.1 us  [exchange(): parts[shift] = lax.ppermute(values[shift], axes, perm)]
  transfers between devices with their start and end apart: 21 -> 21, of which waited for: 13 -> 13; matrix products, arithmetic and copies ran while one was open for 0% -> 0% of each run, Pallas kernels for 9% -> 4%
where the time goes in v3:
time: 57.9 us; the launch traced here: 57.7 us
  starting transfers between devices  24.5 us (42%)
  waiting for transfers between devices  16.1 us (28%)
  Pallas kernels  12.9 us (22%)
  local copies, waits for them, and re-layouts  3.41 us (6%)
  between operations  0.75 us (1%)
    ppermute x21, starting transfers between devices, exchange(): parts[shift] = lax.ppermute(values[shift], axes, perm)  24.5 us
    ppermute x21, waiting for transfers between devices, exchange(): parts[shift] = lax.ppermute(values[shift], axes, perm)  16.1 us
    pallas_call x9, Pallas kernels, call(): pl.pallas_call(body, out_shape=[jax.ShapeDtypeStruct(shape, dtype) for sh...  12.9 us
    unnamed x12, local copies, waits for them, and re-layouts  3.41 us
  transfers between devices with their start and end apart: 21, of which 13 were waited for; matrix products, arithmetic and copies ran while one was open for 0% of the time, Pallas kernels for 4%

profile of v3, /device:TPU:0, one launch (start us, length us, event | category | flops | bytes accessed | tf_op | source)
XLA Modules:
  0.0 57.7 jit_solution(2677096309574369008)
XLA Ops:
  0.6 0.7 %shard_map.104.opening.refs_5_ = f32[16,256]{1,0:T(8,128)S(1)} custom-call(f32[4,256]{1,0:T(4,128)} %start.1, f32[4,256]{1,0:T(4,128)} %weight.1, s32[2,4]{1,0:T(2,128)} %bitcast.12), custom_call_target="tpu_custom_call" | custom-call | flops 17179869184 | tf_op jit(solution)/shard_map/pallas_call | solution.py:289
  1.4 0.0 copy-start.3
  1.4 5.1 %collective-permute-start.2 = (f32[16,256]{1,0:T(8,128)S(1)}, f32[16,256]{1,0:T(8,128)S(1)}, u32[]{:S(2)}, u32[]{:S(2)}) collective-permute-start(f32[16,256]{1,0:T(8,128)S(1)} %shard_map.104.opening.refs_5_), channel_id=1, source_target_pairs={{0,12},{4,8},{8,4},{12,0},{1,13},{5,9},{9,5},{13,1},{2,14},{6,10},... | collective-permute-start | bytes 49160 | tf_op jit(solution)/shard_map/ppermute | solution.py:23
  6.5 0.0 collective-permute-start.1
  6.5 0.6 %collective-permute-start = (f32[16,256]{1,0:T(8,128)S(1)}, f32[16,256]{1,0:T(8,128)S(1)}, u32[]{:S(2)}, u32[]{:S(2)}) collective-permute-start(f32[16,256]{1,0:T(8,128)S(1)} %shard_map.104.opening.refs_5_), channel_id=1, source_target_pairs={{0,4},{4,0},{8,12},{12,8},{1,5},{5,1},{9,13},{13,9},{2,6},{6,2},{1... | collective-permute-start | bytes 49160 | tf_op jit(solution)/shard_map/ppermute | solution.py:23
  7.1 0.0 copy-start
  7.2 3.4 %copy-done = bf16[64,256,256]{2,1,0:T(8,128)(2,1)S(1)} copy-done((bf16[64,256,256]{2,1,0:T(8,128)(2,1)S(1)}, bf16[64,256,256]{2,1,0:T(8,128)(2,1)}, u32[]{:S(2)}) %copy-start) | copy-done | bytes 8388632
  10.5 0.0 slice-start
  10.5 0.0 copy-start.1
  10.5 0.0 copy-start.2
  10.5 2.4 %shard_map.105 = (bf16[64,256,256]{2,1,0:T(8,128)(2,1)S(1)}, bf16[64,16]{1,0:T(8,128)(2,1)S(1)}, bf16[16,128]{1,0:T(8,128)(2,1)S(1)}, f32[64,256]{1,0:T(8,128)S(1)}) custom-call(bf16[64,256,256]{2,1,0:T(8,128)(2,1)S(1)} %copy-done, f32[16,256]{1,0:T(8,128)S(1)} %shard_map.104.opening.refs_5_, f32[1,64]{1,0:T(1,128)} %bitcast.10, s32[1,64]{1,0:T(1,128)} %bitcast.11), custom_call_target="tpu_custom_call" | custom-call | tf_op jit(solution)/shard_map/pallas_call | solution.py:289
  13.0 0.0 collective-permute-done.2.refs_8_
  13.0 0.0 collective-permute-done.1.refs_7_
  13.0 0.0 collective-permute-done.refs_6_
  13.0 0.0 copy-done.3
  13.0 0.0 slice-start.1
  13.0 1.6 %shard_map.106 = (f32[16,256]{1,0:T(8,128)S(1)}, bf16[64,16]{1,0:T(8,128)(2,1)S(1)}, bf16[16,128]{1,0:T(8,128)(2,1)S(1)}, f32[16,256]{1,0:T(8,128)S(1)}, f32[16,256]{1,0:T(8,128)S(1)}) custom-call(bf16[64,256,256]{2,1,0:T(8,128)(2,1)S(1)} %get-tuple-element.24.refs_0_, f32[64,256]{1,0:T(8,128)S(1)} %get-tuple-element.25.refs_1_.refs_3_, ...), custom_call_target="tpu_custom_call" | custom-call | tf_op jit(solution)/shard_map/pallas_call | solution.py:289
  14.6 0.4 collective-permute-start.5
  15.0 1.3 %collective-permute-start.4 = (f32[16,256]{1,0:T(8,128)S(1)}, f32[16,256]{1,0:T(8,128)S(1)}, u32[]{:S(2)}, u32[]{:S(2)}) collective-permute-start(f32[16,256]{1,0:T(8,128)S(1)} %get-tuple-element.32.refs_6_), channel_id=1, source_target_pairs={{0,2},{1,3},{2,0},{3,1},{4,6},{5,7},{6,4},{7,5},{8,10},{9,11},{10,... | collective-permute-start | bytes 49160 | tf_op jit(solution)/shard_map/ppermute | solution.py:23
  16.3 0.2 collective-permute-start.3
  16.5 1.3 %collective-permute-done.5.refs_9_ = f32[16,256]{1,0:T(8,128)S(1)} collective-permute-done((f32[16,256]{1,0:T(8,128)S(1)}, f32[16,256]{1,0:T(8,128)S(1)}, u32[]{:S(2)}, u32[]{:S(2)}) %collective-permute-start.5) | collective-permute-done | bytes 16416 | tf_op jit(solution)/shard_map/ppermute | solution.py:23
  17.8 0.9 %collective-permute-done.4.refs_8_ = f32[16,256]{1,0:T(8,128)S(1)} collective-permute-done((f32[16,256]{1,0:T(8,128)S(1)}, f32[16,256]{1,0:T(8,128)S(1)}, u32[]{:S(2)}, u32[]{:S(2)}) %collective-permute-start.4) | collective-permute-done | bytes 16416 | tf_op jit(solution)/shard_map/ppermute | solution.py:23
  18.7 0.0 collective-permute-done.3.refs_7_
  18.7 0.0 slice-done
  18.7 0.0 copy-done.1
  18.7 0.0 copy-done.2
  18.7 0.0 slice-done.1
  18.8 1.4 %shard_map.107.refs_6_ = f32[16,256]{1,0:T(8,128)S(1)} custom-call(bf16[64,256,256]{2,1,0:T(8,128)(2,1)S(1)} %bitcast.8, bf16[64,16]{1,0:T(8,128)(2,1)S(1)} %get-tuple-element.30.refs_1_, bf16[16,128]{1,0:T(8,128)(2,1)S(1)} %get-tuple-element.31.refs_2_, f32[64,256]{1,0:T(8,128)S(1)} %get-tuple-element.25.refs_1_.refs_3_, f32[16,256]{1,0:T(8,128)S(1)} %copy-done.2, ...), custom_call_target="tpu_custom_call" | custom-call | tf_op jit(solution)/shard_map/pallas_call | solution.py:289
  20.2 3.5 %collective-permute-start.8 = (f32[16,256]{1,0:T(8,128)S(1)}, f32[16,256]{1,0:T(8,128)S(1)}, u32[]{:S(2)}, u32[]{:S(2)}) collective-permute-start(f32[16,256]{1,0:T(8,128)S(1)} %shard_map.107.refs_6_), channel_id=1, source_target_pairs={{0,12},{4,8},{8,4},{12,0},{1,13},{5,9},{9,5},{13,1},{2,14},{6,10},... | collective-permute-start | bytes 49160 | tf_op jit(solution)/shard_map/ppermute | solution.py:23
  23.7 0.0 collective-permute-start.7
  23.7 0.9 %collective-permute-start.6 = (f32[16,256]{1,0:T(8,128)S(1)}, f32[16,256]{1,0:T(8,128)S(1)}, u32[]{:S(2)}, u32[]{:S(2)}) collective-permute-start(f32[16,256]{1,0:T(8,128)S(1)} %shard_map.107.refs_6_), channel_id=1, source_target_pairs={{0,4},{4,0},{8,12},{12,8},{1,5},{5,1},{9,13},{13,9},{2,6},{6,2},{1... | collective-permute-start | bytes 49160 | tf_op jit(solution)/shard_map/ppermute | solution.py:23
  24.6 1.1 %collective-permute-done.8.refs_9_ = f32[16,256]{1,0:T(8,128)S(1)} collective-permute-done((f32[16,256]{1,0:T(8,128)S(1)}, f32[16,256]{1,0:T(8,128)S(1)}, u32[]{:S(2)}, u32[]{:S(2)}) %collective-permute-start.8) | collective-permute-done | bytes 16416 | tf_op jit(solution)/shard_map/ppermute | solution.py:23
  25.7 2.6 %collective-permute-done.7.refs_8_ = f32[16,256]{1,0:T(8,128)S(1)} collective-permute-done((f32[16,256]{1,0:T(8,128)S(1)}, f32[16,256]{1,0:T(8,128)S(1)}, u32[]{:S(2)}, u32[]{:S(2)}) %collective-permute-start.7) | collective-permute-done | bytes 16416 | tf_op jit(solution)/shard_map/ppermute | solution.py:23
  28.3 0.0 collective-permute-done.6.refs_7_
  28.3 1.4 %shard_map.108 = (f32[24,256]{1,0:T(8,128)S(1)}, f32[16,256]{1,0:T(8,128)S(1)}) custom-call(bf16[64,256,256]{2,1,0:T(8,128)(2,1)S(1)} %get-tuple-element.24.refs_0_, bf16[64,16]{1,0:T(8,128)(2,1)S(1)} %get-tuple-element.29.refs_1_, bf16[16,128]{1,0:T(8,128)(2,1)S(1)} %get-tuple-element.26.refs_2_, f32[64,256]{1,0:T(8,128)S(1)} %get-tuple-element.25.refs_1_.refs_3_, ...), custom_call_target="tpu_custom_call" | custom-call | tf_op jit(solution)/shard_map/pallas_call | solution.py:289
  29.7 0.0 collective-permute-start.11
  29.7 1.5 %collective-permute-start.10 = (f32[24,256]{1,0:T(8,128)S(1)}, f32[24,256]{1,0:T(8,128)S(1)}, u32[]{:S(2)}, u32[]{:S(2)}) collective-permute-start(f32[24,256]{1,0:T(8,128)S(1)} %get-tuple-element.34.refs_5_), channel_id=1, source_target_pairs={{0,2},{1,3},{2,0},{3,1},{4,6},{5,7},{6,4},{7,5},{8,10},{9,11},{10,... | collective-permute-start | bytes 73736 | tf_op jit(solution)/shard_map/ppermute | solution.py:23
  31.2 0.4 collective-permute-start.9
  31.6 1.6 %collective-permute-done.11.refs_8_ = f32[24,256]{1,0:T(8,128)S(1)} collective-permute-done((f32[24,256]{1,0:T(8,128)S(1)}, f32[24,256]{1,0:T(8,128)S(1)}, u32[]{:S(2)}, u32[]{:S(2)}) %collective-permute-start.11) | collective-permute-done | bytes 24608 | tf_op jit(solution)/shard_map/ppermute | solution.py:23
  33.2 0.4 collective-permute-done.10.refs_7_
  33.6 0.0 collective-permute-done.9.refs_6_
  33.6 1.4 %shard_map.109 = (f32[24,256]{1,0:T(8,128)S(1)}, f32[16,256]{1,0:T(8,128)S(1)}, f32[8,256]{1,0:T(8,128)S(1)}) custom-call(bf16[64,256,256]{2,1,0:T(8,128)(2,1)S(1)} %bitcast.8, bf16[64,16]{1,0:T(8,128)(2,1)S(1)} %get-tuple-element.30.refs_1_, bf16[16,128]{1,0:T(8,128)(2,1)S(1)} %get-tuple-element.31.refs_2_, ...), custom_call_target="tpu_custom_call" | custom-call | tf_op jit(solution)/shard_map/pallas_call | solution.py:289
  35.1 1.5 %collective-permute-start.14 = (f32[24,256]{1,0:T(8,128)S(1)}, f32[24,256]{1,0:T(8,128)S(1)}, u32[]{:S(2)}, u32[]{:S(2)}) collective-permute-start(f32[24,256]{1,0:T(8,128)S(1)} %get-tuple-element.36.refs_7_), channel_id=1, source_target_pairs={{0,12},{4,8},{8,4},{12,0},{1,13},{5,9},{9,5},{13,1},{2,14},{6,10},... | collective-permute-start | bytes 73736 | tf_op jit(solution)/shard_map/ppermute | solution.py:23
  36.5 0.6 %collective-permute-start.13 = (f32[24,256]{1,0:T(8,128)S(1)}, f32[24,256]{1,0:T(8,128)S(1)}, u32[]{:S(2)}, u32[]{:S(2)}) collective-permute-start(f32[24,256]{1,0:T(8,128)S(1)} %get-tuple-element.36.refs_7_), channel_id=1, source_target_pairs={{0,8},{4,12},{8,0},{12,4},{1,9},{5,13},{9,1},{13,5},{2,10},{6,14},... | collective-permute-start | bytes 73736 | tf_op jit(solution)/shard_map/ppermute | solution.py:23
  37.1 2.3 %collective-permute-start.12 = (f32[24,256]{1,0:T(8,128)S(1)}, f32[24,256]{1,0:T(8,128)S(1)}, u32[]{:S(2)}, u32[]{:S(2)}) collective-permute-start(f32[24,256]{1,0:T(8,128)S(1)} %get-tuple-element.36.refs_7_), channel_id=1, source_target_pairs={{0,4},{4,0},{8,12},{12,8},{1,5},{5,1},{9,13},{13,9},{2,6},{6,2},{1... | collective-permute-start | bytes 73736 | tf_op jit(solution)/shard_map/ppermute | solution.py:23
  39.4 1.3 %collective-permute-done.14.refs_10_ = f32[24,256]{1,0:T(8,128)S(1)} collective-permute-done((f32[24,256]{1,0:T(8,128)S(1)}, f32[24,256]{1,0:T(8,128)S(1)}, u32[]{:S(2)}, u32[]{:S(2)}) %collective-permute-start.14) | collective-permute-done | bytes 24608 | tf_op jit(solution)/shard_map/ppermute | solution.py:23
  40.7 0.5 collective-permute-done.13.refs_9_
  41.3 0.2 collective-permute-done.12.refs_8_
  41.5 1.5 %shard_map.110 = (f32[24,256]{1,0:T(8,128)S(1)}, f32[16,256]{1,0:T(8,128)S(1)}, f32[8,128]{1,0:T(8,128)S(1)}) custom-call(bf16[64,256,256]{2,1,0:T(8,128)(2,1)S(1)} %get-tuple-element.24.refs_0_, bf16[64,16]{1,0:T(8,128)(2,1)S(1)} %get-tuple-element.29.refs_1_, bf16[16,128]{1,0:T(8,128)(2,1)S(1)} %get-tuple-element.26.refs_2_, ...), custom_call_target="tpu_custom_call" | custom-call | tf_op jit(solution)/shard_map/pallas_call | solution.py:289
  43.1 0.0 collective-permute-start.17
  43.1 1.5 %collective-permute-start.16 = (f32[24,256]{1,0:T(8,128)S(1)}, f32[24,256]{1,0:T(8,128)S(1)}, u32[]{:S(2)}, u32[]{:S(2)}) collective-permute-start(f32[24,256]{1,0:T(8,128)S(1)} %get-tuple-element.40.refs_7_), channel_id=1, source_target_pairs={{0,2},{1,3},{2,0},{3,1},{4,6},{5,7},{6,4},{7,5},{8,10},{9,11},{10,... | collective-permute-start | bytes 73736 | tf_op jit(solution)/shard_map/ppermute | solution.py:23
  44.5 0.4 collective-permute-start.15
  44.9 1.6 %collective-permute-done.17.refs_10_ = f32[24,256]{1,0:T(8,128)S(1)} collective-permute-done((f32[24,256]{1,0:T(8,128)S(1)}, f32[24,256]{1,0:T(8,128)S(1)}, u32[]{:S(2)}, u32[]{:S(2)}) %collective-permute-start.17) | collective-permute-done | bytes 24608 | tf_op jit(solution)/shard_map/ppermute | solution.py:23
  46.6 0.4 collective-permute-done.16.refs_9_
  46.9 0.0 collective-permute-done.15.refs_8_
  46.9 1.6 %shard_map.111 = (f32[8,256]{1,0:T(8,128)S(1)}, f32[8,256]{1,0:T(8,128)S(1)}, f32[8,256]{1,0:T(8,128)S(1)}, f32[8,256]{1,0:T(8,128)S(1)}, f32[8,256]{1,0:T(8,128)S(1)}) custom-call(bf16[64,256,256]{2,1,0:T(8,128)(2,1)S(1)} %bitcast.8, bf16[64,16]{1,0:T(8,128)(2,1)S(1)} %get-tuple-element.30.refs_1_, bf16[16,128]{1,0:T(8,128)(2,1)S(1)} %get-tuple-element.31.refs_2_, ...), custom_call_target="tpu_custom_call" | custom-call | tf_op jit(solution)/shard_map/pallas_call | solution.py:289
  48.5 1.8 %collective-permute-start.18 = (f32[8,256]{1,0:T(8,128)S(1)}, f32[8,256]{1,0:T(8,128)S(1)}, u32[]{:S(2)}, u32[]{:S(2)}) collective-permute-start(f32[8,256]{1,0:T(8,128)S(1)} %get-tuple-element.43), channel_id=1, source_target_pairs={{0,4},{4,0},{8,12},{12,8},{1,5},{5,1},{9,13},{13,9},{2,6},{6,2},{1... | collective-permute-start | bytes 24584 | tf_op jit(solution)/shard_map/ppermute | solution.py:23
  50.3 1.2 %collective-permute-start.19 = (f32[8,256]{1,0:T(8,128)S(1)}, f32[8,256]{1,0:T(8,128)S(1)}, u32[]{:S(2)}, u32[]{:S(2)}) collective-permute-start(f32[8,256]{1,0:T(8,128)S(1)} %get-tuple-element.44), channel_id=1, source_target_pairs={{0,8},{4,12},{8,0},{12,4},{1,9},{5,13},{9,1},{13,5},{2,10},{6,14},... | collective-permute-start | bytes 24584 | tf_op jit(solution)/shard_map/ppermute | solution.py:23
  51.4 1.5 %collective-permute-start.20 = (f32[8,256]{1,0:T(8,128)S(1)}, f32[8,256]{1,0:T(8,128)S(1)}, u32[]{:S(2)}, u32[]{:S(2)}) collective-permute-start(f32[8,256]{1,0:T(8,128)S(1)} %get-tuple-element.45), channel_id=1, source_target_pairs={{0,12},{4,8},{8,4},{12,0},{1,13},{5,9},{9,5},{13,1},{2,14},{6,10},... | collective-permute-start | bytes 24584 | tf_op jit(solution)/shard_map/ppermute | solution.py:23
  52.9 0.0 collective-permute-done.18.refs_7_
  52.9 1.9 %collective-permute-done.19.refs_8_ = f32[8,256]{1,0:T(8,128)S(1)} collective-permute-done((f32[8,256]{1,0:T(8,128)S(1)}, f32[8,256]{1,0:T(8,128)S(1)}, u32[]{:S(2)}, u32[]{:S(2)}) %collective-permute-start.19) | collective-permute-done | bytes 8224 | tf_op jit(solution)/shard_map/ppermute | solution.py:23
  54.8 2.1 %collective-permute-done.20.refs_9_ = f32[8,256]{1,0:T(8,128)S(1)} collective-permute-done((f32[8,256]{1,0:T(8,128)S(1)}, f32[8,256]{1,0:T(8,128)S(1)}, u32[]{:S(2)}, u32[]{:S(2)}) %collective-permute-start.20) | collective-permute-done | bytes 8224 | tf_op jit(solution)/shard_map/ppermute | solution.py:23
  56.9 0.8 %shard_map.112 = (f32[4,256]{1,0:T(4,128)}, f32[4,256]{1,0:T(4,128)}) custom-call(f32[16,256]{1,0:T(8,128)S(1)} %get-tuple-element.27.refs_5_.refs_4_.refs_0_, f32[16,256]{1,0:T(8,128)S(1)} %get-tuple-element.28.refs_4_.refs_1_, f32[16,256]{1,0:T(8,128)S(1)} %get-tuple-element.33.refs_5_.refs_2_, f32[16,256]{1,0:T(8,128)S(1)} %get-tuple-element.37.refs_3_, ...), custom_call_target="tpu_custom_call" | custom-call | tf_op jit(solution)/shard_map/pallas_call | solution.py:289
  (1 shorter events, 0.0 us)
Async XLA Ops:
  1.4 11.6 %copy-start.3 = (s32[64]{0:T(128)S(1)}, s32[64]{0:T(128)}, u32[]{:S(2)}) copy-start(s32[64]{0:T(128)} %param.12) | copy-start | bytes 772
  1.4 11.6 %collective-permute-start.2 = (f32[16,256]{1,0:T(8,128)S(1)}, f32[16,256]{1,0:T(8,128)S(1)}, u32[]{:S(2)}, u32[]{:S(2)}) collective-permute-start(f32[16,256]{1,0:T(8,128)S(1)} %shard_map.104.opening.refs_5_), channel_id=1, source_target_pairs={{0,12},{4,8},{8,4},{12,0},{1,13},{5,9},{9,5},{13,1},{2,14},{6,10},... | collective-permute-start | bytes 49160 | tf_op jit(solution)/shard_map/ppermute | solution.py:23
  6.5 6.5 %collective-permute-start.1 = (f32[16,256]{1,0:T(8,128)S(1)}, f32[16,256]{1,0:T(8,128)S(1)}, u32[]{:S(2)}, u32[]{:S(2)}) collective-permute-start(f32[16,256]{1,0:T(8,128)S(1)} %shard_map.104.opening.refs_5_), channel_id=1, source_target_pairs={{0,8},{4,12},{8,0},{12,4},{1,9},{5,13},{9,1},{13,5},{2,10},{6,14},... | collective-permute-start | bytes 49160 | tf_op jit(solution)/shard_map/ppermute | solution.py:23
  6.5 6.5 %collective-permute-start = (f32[16,256]{1,0:T(8,128)S(1)}, f32[16,256]{1,0:T(8,128)S(1)}, u32[]{:S(2)}, u32[]{:S(2)}) collective-permute-start(f32[16,256]{1,0:T(8,128)S(1)} %shard_map.104.opening.refs_5_), channel_id=1, source_target_pairs={{0,4},{4,0},{8,12},{12,8},{1,5},{5,1},{9,13},{13,9},{2,6},{6,2},{1... | collective-permute-start | bytes 49160 | tf_op jit(solution)/shard_map/ppermute | solution.py:23
  7.1 3.4 %copy-start = (bf16[64,256,256]{2,1,0:T(8,128)(2,1)S(1)}, bf16[64,256,256]{2,1,0:T(8,128)(2,1)}, u32[]{:S(2)}) copy-start(bf16[64,256,256]{2,1,0:T(8,128)(2,1)} %refs_0_.5) | copy-start | bytes 25165828
  10.5 8.2 %slice-start = ((s8[8388608]{0:T(1024)(128)(4,1)}), s8[4194304]{0:T(1024)(128)(4,1)S(1)}, s32[]{:S(2)}) async-start(s8[8388608]{0:T(1024)(128)(4,1)} %bitcast.7), calls=%async_computation | async-start | bytes 8388608
  10.5 8.2 %copy-start.1 = (f32[16,256]{1,0:T(8,128)S(1)}, f32[16,256]{1,0:T(8,128)}, u32[]{:S(2)}) copy-start(f32[16,256]{1,0:T(8,128)} %refs_4_.5) | copy-start | bytes 49156
  10.5 8.2 %copy-start.2 = (f32[16,256]{1,0:T(8,128)S(1)}, f32[16,256]{1,0:T(8,128)}, u32[]{:S(2)}) copy-start(f32[16,256]{1,0:T(8,128)} %refs_4_.3) | copy-start | bytes 49156
  13.0 5.7 %slice-start.1 = ((s8[8388608]{0:T(1024)(128)(4,1)}), s8[4194304]{0:T(1024)(128)(4,1)S(1)}, s32[]{:S(2)}) async-start(s8[8388608]{0:T(1024)(128)(4,1)} %bitcast.7), calls=%async_computation.1 | async-start | bytes 8388608
  14.6 3.2 %collective-permute-start.5 = (f32[16,256]{1,0:T(8,128)S(1)}, f32[16,256]{1,0:T(8,128)S(1)}, u32[]{:S(2)}, u32[]{:S(2)}) collective-permute-start(f32[16,256]{1,0:T(8,128)S(1)} %get-tuple-element.32.refs_6_), channel_id=1, source_target_pairs={{0,3},{1,2},{2,1},{3,0},{4,7},{5,6},{6,5},{7,4},{8,11},{9,10},{10,... | collective-permute-start | bytes 49160 | tf_op jit(solution)/shard_map/ppermute | solution.py:23
  15.0 3.7 %collective-permute-start.4 = (f32[16,256]{1,0:T(8,128)S(1)}, f32[16,256]{1,0:T(8,128)S(1)}, u32[]{:S(2)}, u32[]{:S(2)}) collective-permute-start(f32[16,256]{1,0:T(8,128)S(1)} %get-tuple-element.32.refs_6_), channel_id=1, source_target_pairs={{0,2},{1,3},{2,0},{3,1},{4,6},{5,7},{6,4},{7,5},{8,10},{9,11},{10,... | collective-permute-start | bytes 49160 | tf_op jit(solution)/shard_map/ppermute | solution.py:23
  16.3 2.4 %collective-permute-start.3 = (f32[16,256]{1,0:T(8,128)S(1)}, f32[16,256]{1,0:T(8,128)S(1)}, u32[]{:S(2)}, u32[]{:S(2)}) collective-permute-start(f32[16,256]{1,0:T(8,128)S(1)} %get-tuple-element.32.refs_6_), channel_id=1, source_target_pairs={{0,1},{1,0},{2,3},{3,2},{4,5},{5,4},{6,7},{7,6},{8,9},{9,8},{10,11... | collective-permute-start | bytes 49160 | tf_op jit(solution)/shard_map/ppermute | solution.py:23
  20.2 5.5 %collective-permute-start.8 = (f32[16,256]{1,0:T(8,128)S(1)}, f32[16,256]{1,0:T(8,128)S(1)}, u32[]{:S(2)}, u32[]{:S(2)}) collective-permute-start(f32[16,256]{1,0:T(8,128)S(1)} %shard_map.107.refs_6_), channel_id=1, source_target_pairs={{0,12},{4,8},{8,4},{12,0},{1,13},{5,9},{9,5},{13,1},{2,14},{6,10},... | collective-permute-start | bytes 49160 | tf_op jit(solution)/shard_map/ppermute | solution.py:23
  23.7 4.6 %collective-permute-start.7 = (f32[16,256]{1,0:T(8,128)S(1)}, f32[16,256]{1,0:T(8,128)S(1)}, u32[]{:S(2)}, u32[]{:S(2)}) collective-permute-start(f32[16,256]{1,0:T(8,128)S(1)} %shard_map.107.refs_6_), channel_id=1, source_target_pairs={{0,8},{4,12},{8,0},{12,4},{1,9},{5,13},{9,1},{13,5},{2,10},{6,14},... | collective-permute-start | bytes 49160 | tf_op jit(solution)/shard_map/ppermute | solution.py:23
  23.7 4.6 %collective-permute-start.6 = (f32[16,256]{1,0:T(8,128)S(1)}, f32[16,256]{1,0:T(8,128)S(1)}, u32[]{:S(2)}, u32[]{:S(2)}) collective-permute-start(f32[16,256]{1,0:T(8,128)S(1)} %shard_map.107.refs_6_), channel_id=1, source_target_pairs={{0,4},{4,0},{8,12},{12,8},{1,5},{5,1},{9,13},{13,9},{2,6},{6,2},{1... | collective-permute-start | bytes 49160 | tf_op jit(solution)/shard_map/ppermute | solution.py:23
  29.7 3.5 %collective-permute-start.11 = (f32[24,256]{1,0:T(8,128)S(1)}, f32[24,256]{1,0:T(8,128)S(1)}, u32[]{:S(2)}, u32[]{:S(2)}) collective-permute-start(f32[24,256]{1,0:T(8,128)S(1)} %get-tuple-element.34.refs_5_), channel_id=1, source_target_pairs={{0,3},{1,2},{2,1},{3,0},{4,7},{5,6},{6,5},{7,4},{8,11},{9,10},{10,... | collective-permute-start | bytes 73736 | tf_op jit(solution)/shard_map/ppermute | solution.py:23
  29.7 3.9 %collective-permute-start.10 = (f32[24,256]{1,0:T(8,128)S(1)}, f32[24,256]{1,0:T(8,128)S(1)}, u32[]{:S(2)}, u32[]{:S(2)}) collective-permute-start(f32[24,256]{1,0:T(8,128)S(1)} %get-tuple-element.34.refs_5_), channel_id=1, source_target_pairs={{0,2},{1,3},{2,0},{3,1},{4,6},{5,7},{6,4},{7,5},{8,10},{9,11},{10,... | collective-permute-start | bytes 73736 | tf_op jit(solution)/shard_map/ppermute | solution.py:23
  31.2 2.4 %collective-permute-start.9 = (f32[24,256]{1,0:T(8,128)S(1)}, f32[24,256]{1,0:T(8,128)S(1)}, u32[]{:S(2)}, u32[]{:S(2)}) collective-permute-start(f32[24,256]{1,0:T(8,128)S(1)} %get-tuple-element.34.refs_5_), channel_id=1, source_target_pairs={{0,1},{1,0},{2,3},{3,2},{4,5},{5,4},{6,7},{7,6},{8,9},{9,8},{10,11... | collective-permute-start | bytes 73736 | tf_op jit(solution)/shard_map/ppermute | solution.py:23
  35.1 5.7 %collective-permute-start.14 = (f32[24,256]{1,0:T(8,128)S(1)}, f32[24,256]{1,0:T(8,128)S(1)}, u32[]{:S(2)}, u32[]{:S(2)}) collective-permute-start(f32[24,256]{1,0:T(8,128)S(1)} %get-tuple-element.36.refs_7_), channel_id=1, source_target_pairs={{0,12},{4,8},{8,4},{12,0},{1,13},{5,9},{9,5},{13,1},{2,14},{6,10},... | collective-permute-start | bytes 73736 | tf_op jit(solution)/shard_map/ppermute | solution.py:23
  36.5 4.8 %collective-permute-start.13 = (f32[24,256]{1,0:T(8,128)S(1)}, f32[24,256]{1,0:T(8,128)S(1)}, u32[]{:S(2)}, u32[]{:S(2)}) collective-permute-start(f32[24,256]{1,0:T(8,128)S(1)} %get-tuple-element.36.refs_7_), channel_id=1, source_target_pairs={{0,8},{4,12},{8,0},{12,4},{1,9},{5,13},{9,1},{13,5},{2,10},{6,14},... | collective-permute-start | bytes 73736 | tf_op jit(solution)/shard_map/ppermute | solution.py:23
  37.1 4.4 %collective-permute-start.12 = (f32[24,256]{1,0:T(8,128)S(1)}, f32[24,256]{1,0:T(8,128)S(1)}, u32[]{:S(2)}, u32[]{:S(2)}) collective-permute-start(f32[24,256]{1,0:T(8,128)S(1)} %get-tuple-element.36.refs_7_), channel_id=1, source_target_pairs={{0,4},{4,0},{8,12},{12,8},{1,5},{5,1},{9,13},{13,9},{2,6},{6,2},{1... | collective-permute-start | bytes 73736 | tf_op jit(solution)/shard_map/ppermute | solution.py:23
  43.1 3.5 %collective-permute-start.17 = (f32[24,256]{1,0:T(8,128)S(1)}, f32[24,256]{1,0:T(8,128)S(1)}, u32[]{:S(2)}, u32[]{:S(2)}) collective-permute-start(f32[24,256]{1,0:T(8,128)S(1)} %get-tuple-element.40.refs_7_), channel_id=1, source_target_pairs={{0,3},{1,2},{2,1},{3,0},{4,7},{5,6},{6,5},{7,4},{8,11},{9,10},{10,... | collective-permute-start | bytes 73736 | tf_op jit(solution)/shard_map/ppermute | solution.py:23
  43.1 3.9 %collective-permute-start.16 = (f32[24,256]{1,0:T(8,128)S(1)}, f32[24,256]{1,0:T(8,128)S(1)}, u32[]{:S(2)}, u32[]{:S(2)}) collective-permute-start(f32[24,256]{1,0:T(8,128)S(1)} %get-tuple-element.40.refs_7_), channel_id=1, source_target_pairs={{0,2},{1,3},{2,0},{3,1},{4,6},{5,7},{6,4},{7,5},{8,10},{9,11},{10,... | collective-permute-start | bytes 73736 | tf_op jit(solution)/shard_map/ppermute | solution.py:23
  44.5 2.4 %collective-permute-start.15 = (f32[24,256]{1,0:T(8,128)S(1)}, f32[24,256]{1,0:T(8,128)S(1)}, u32[]{:S(2)}, u32[]{:S(2)}) collective-permute-start(f32[24,256]{1,0:T(8,128)S(1)} %get-tuple-element.40.refs_7_), channel_id=1, source_target_pairs={{0,1},{1,0},{2,3},{3,2},{4,5},{5,4},{6,7},{7,6},{8,9},{9,8},{10,11... | collective-permute-start | bytes 73736 | tf_op jit(solution)/shard_map/ppermute | solution.py:23
  48.5 4.4 %collective-permute-start.18 = (f32[8,256]{1,0:T(8,128)S(1)}, f32[8,256]{1,0:T(8,128)S(1)}, u32[]{:S(2)}, u32[]{:S(2)}) collective-permute-start(f32[8,256]{1,0:T(8,128)S(1)} %get-tuple-element.43), channel_id=1, source_target_pairs={{0,4},{4,0},{8,12},{12,8},{1,5},{5,1},{9,13},{13,9},{2,6},{6,2},{1... | collective-permute-start | bytes 24584 | tf_op jit(solution)/shard_map/ppermute | solution.py:23
  50.3 4.5 %collective-permute-start.19 = (f32[8,256]{1,0:T(8,128)S(1)}, f32[8,256]{1,0:T(8,128)S(1)}, u32[]{:S(2)}, u32[]{:S(2)}) collective-permute-start(f32[8,256]{1,0:T(8,128)S(1)} %get-tuple-element.44), channel_id=1, source_target_pairs={{0,8},{4,12},{8,0},{12,4},{1,9},{5,13},{9,1},{13,5},{2,10},{6,14},... | collective-permute-start | bytes 24584 | tf_op jit(solution)/shard_map/ppermute | solution.py:23
  51.4 5.4 %collective-permute-start.20 = (f32[8,256]{1,0:T(8,128)S(1)}, f32[8,256]{1,0:T(8,128)S(1)}, u32[]{:S(2)}, u32[]{:S(2)}) collective-permute-start(f32[8,256]{1,0:T(8,128)S(1)} %get-tuple-element.45), channel_id=1, source_target_pairs={{0,12},{4,8},{8,4},{12,0},{1,13},{5,9},{9,5},{13,1},{2,14},{6,10},... | collective-permute-start | bytes 24584 | tf_op jit(solution)/shard_map/ppermute | solution.py:23

commit v4 on v3

--- a/solution.py
+++ b/solution.py
@@ -337,7 +337,9 @@
             pltpu.VMEM((slots, count), jnp.int32),
             pltpu.SemaphoreType.DMA((3,)),
         ],
-        cost=pl.CostEstimate(flops=16 * width * codes.size, transcendentals=0, bytes_accessed=0),
+        cost=pl.CostEstimate(
+            flops=2**14 * width * codes.size, transcendentals=codes.size, bytes_accessed=2**14 * codes.size
+        ),
     )
     begin = across([opening] * count)
     turned, rows_pick, rows_pair, scale = call(

time: 57.9 us -> 57.9 us (level)
  no operation moved by 1% of the time
where the time goes in v4:
time: 57.9 us; the launch traced here: 57.7 us
  starting transfers between devices  24.5 us (42%)
  waiting for transfers between devices  16.1 us (28%)
  Pallas kernels  12.9 us (22%)
  local copies, waits for them, and re-layouts  3.41 us (6%)
  between operations  0.75 us (1%)
    ppermute x21, starting transfers between devices, exchange(): parts[shift] = lax.ppermute(values[shift], axes, perm)  24.5 us
    ppermute x21, waiting for transfers between devices, exchange(): parts[shift] = lax.ppermute(values[shift], axes, perm)  16.1 us
    pallas_call x9, Pallas kernels, call(): pl.pallas_call(body, out_shape=[jax.ShapeDtypeStruct(shape, dtype) for sh...  12.9 us
    unnamed x12, local copies, waits for them, and re-layouts  3.41 us
  transfers between devices with their start and end apart: 21, of which 13 were waited for; matrix products, arithmetic and copies ran while one was open for 0% of the time, Pallas kernels for 4%

profile of v4, /device:TPU:0, one launch (start us, length us, event | category | flops | bytes accessed | tf_op | source)
XLA Modules:
  0.0 57.7 jit_solution(15147511564290948634)
XLA Ops:
  0.6 0.7 %shard_map.104.opening.refs_5_ = f32[16,256]{1,0:T(8,128)S(1)} custom-call(f32[4,256]{1,0:T(4,128)} %start.1, f32[4,256]{1,0:T(4,128)} %weight.1, s32[2,4]{1,0:T(2,128)} %bitcast.12), custom_call_target="tpu_custom_call" | custom-call | flops 17592186044416 | bytes 68719476736 | tf_op jit(solution)/shard_map/pallas_call | solution.py:289
  1.4 0.0 copy-start.3
  1.4 5.1 %collective-permute-start.2 = (f32[16,256]{1,0:T(8,128)S(1)}, f32[16,256]{1,0:T(8,128)S(1)}, u32[]{:S(2)}, u32[]{:S(2)}) collective-permute-start(f32[16,256]{1,0:T(8,128)S(1)} %shard_map.104.opening.refs_5_), channel_id=1, source_target_pairs={{0,12},{4,8},{8,4},{12,0},{1,13},{5,9},{9,5},{13,1},{2,14},{6,10},... | collective-permute-start | bytes 49160 | tf_op jit(solution)/shard_map/ppermute | solution.py:23
  6.5 0.0 collective-permute-start.1
  6.5 0.6 %collective-permute-start = (f32[16,256]{1,0:T(8,128)S(1)}, f32[16,256]{1,0:T(8,128)S(1)}, u32[]{:S(2)}, u32[]{:S(2)}) collective-permute-start(f32[16,256]{1,0:T(8,128)S(1)} %shard_map.104.opening.refs_5_), channel_id=1, source_target_pairs={{0,4},{4,0},{8,12},{12,8},{1,5},{5,1},{9,13},{13,9},{2,6},{6,2},{1... | collective-permute-start | bytes 49160 | tf_op jit(solution)/shard_map/ppermute | solution.py:23
  7.1 0.0 copy-start
  7.2 3.4 %copy-done = bf16[64,256,256]{2,1,0:T(8,128)(2,1)S(1)} copy-done((bf16[64,256,256]{2,1,0:T(8,128)(2,1)S(1)}, bf16[64,256,256]{2,1,0:T(8,128)(2,1)}, u32[]{:S(2)}) %copy-start) | copy-done | bytes 8388632
  10.5 0.0 slice-start
  10.5 0.0 copy-start.1
  10.5 0.0 copy-start.2
  10.5 2.4 %shard_map.105 = (bf16[64,256,256]{2,1,0:T(8,128)(2,1)S(1)}, bf16[64,16]{1,0:T(8,128)(2,1)S(1)}, bf16[16,128]{1,0:T(8,128)(2,1)S(1)}, f32[64,256]{1,0:T(8,128)S(1)}) custom-call(bf16[64,256,256]{2,1,0:T(8,128)(2,1)S(1)} %copy-done, f32[16,256]{1,0:T(8,128)S(1)} %shard_map.104.opening.refs_5_, f32[1,64]{1,0:T(1,128)} %bitcast.10, s32[1,64]{1,0:T(1,128)} %bitcast.11), custom_call_target="tpu_custom_call" | custom-call | tf_op jit(solution)/shard_map/pallas_call | solution.py:289
  13.0 0.0 slice-start.1
  13.0 0.0 collective-permute-done.2.refs_8_
  13.0 0.0 collective-permute-done.1.refs_7_
  13.0 0.0 collective-permute-done.refs_6_
  13.0 0.0 copy-done.3
  13.0 1.6 %shard_map.106 = (f32[16,256]{1,0:T(8,128)S(1)}, bf16[64,16]{1,0:T(8,128)(2,1)S(1)}, bf16[16,128]{1,0:T(8,128)(2,1)S(1)}, f32[16,256]{1,0:T(8,128)S(1)}, f32[16,256]{1,0:T(8,128)S(1)}) custom-call(bf16[64,256,256]{2,1,0:T(8,128)(2,1)S(1)} %get-tuple-element.24.refs_0_, f32[64,256]{1,0:T(8,128)S(1)} %get-tuple-element.25.refs_1_.refs_3_, ...), custom_call_target="tpu_custom_call" | custom-call | tf_op jit(solution)/shard_map/pallas_call | solution.py:289
  14.6 0.4 collective-permute-start.5
  15.0 1.3 %collective-permute-start.4 = (f32[16,256]{1,0:T(8,128)S(1)}, f32[16,256]{1,0:T(8,128)S(1)}, u32[]{:S(2)}, u32[]{:S(2)}) collective-permute-start(f32[16,256]{1,0:T(8,128)S(1)} %get-tuple-element.32.refs_6_), channel_id=1, source_target_pairs={{0,2},{1,3},{2,0},{3,1},{4,6},{5,7},{6,4},{7,5},{8,10},{9,11},{10,... | collective-permute-start | bytes 49160 | tf_op jit(solution)/shard_map/ppermute | solution.py:23
  16.3 0.2 collective-permute-start.3
  16.5 1.3 %collective-permute-done.5.refs_9_ = f32[16,256]{1,0:T(8,128)S(1)} collective-permute-done((f32[16,256]{1,0:T(8,128)S(1)}, f32[16,256]{1,0:T(8,128)S(1)}, u32[]{:S(2)}, u32[]{:S(2)}) %collective-permute-start.5) | collective-permute-done | bytes 16416 | tf_op jit(solution)/shard_map/ppermute | solution.py:23
  17.8 0.9 %collective-permute-done.4.refs_8_ = f32[16,256]{1,0:T(8,128)S(1)} collective-permute-done((f32[16,256]{1,0:T(8,128)S(1)}, f32[16,256]{1,0:T(8,128)S(1)}, u32[]{:S(2)}, u32[]{:S(2)}) %collective-permute-start.4) | collective-permute-done | bytes 16416 | tf_op jit(solution)/shard_map/ppermute | solution.py:23
  18.7 0.0 collective-permute-done.3.refs_7_
  18.7 0.0 slice-done
  18.7 0.0 copy-done.1
  18.7 0.0 copy-done.2
  18.7 0.0 slice-done.1
  18.8 1.4 %shard_map.107.refs_6_ = f32[16,256]{1,0:T(8,128)S(1)} custom-call(bf16[64,256,256]{2,1,0:T(8,128)(2,1)S(1)} %bitcast.8, bf16[64,16]{1,0:T(8,128)(2,1)S(1)} %get-tuple-element.30.refs_1_, bf16[16,128]{1,0:T(8,128)(2,1)S(1)} %get-tuple-element.31.refs_2_, f32[64,256]{1,0:T(8,128)S(1)} %get-tuple-element.25.refs_1_.refs_3_, f32[16,256]{1,0:T(8,128)S(1)} %copy-done.2, ...), custom_call_target="tpu_custom_call" | custom-call | tf_op jit(solution)/shard_map/pallas_call | solution.py:289
  20.2 3.5 %collective-permute-start.8 = (f32[16,256]{1,0:T(8,128)S(1)}, f32[16,256]{1,0:T(8,128)S(1)}, u32[]{:S(2)}, u32[]{:S(2)}) collective-permute-start(f32[16,256]{1,0:T(8,128)S(1)} %shard_map.107.refs_6_), channel_id=1, source_target_pairs={{0,12},{4,8},{8,4},{12,0},{1,13},{5,9},{9,5},{13,1},{2,14},{6,10},... | collective-permute-start | bytes 49160 | tf_op jit(solution)/shard_map/ppermute | solution.py:23
  23.7 0.0 collective-permute-start.7
  23.7 0.9 %collective-permute-start.6 = (f32[16,256]{1,0:T(8,128)S(1)}, f32[16,256]{1,0:T(8,128)S(1)}, u32[]{:S(2)}, u32[]{:S(2)}) collective-permute-start(f32[16,256]{1,0:T(8,128)S(1)} %shard_map.107.refs_6_), channel_id=1, source_target_pairs={{0,4},{4,0},{8,12},{12,8},{1,5},{5,1},{9,13},{13,9},{2,6},{6,2},{1... | collective-permute-start | bytes 49160 | tf_op jit(solution)/shard_map/ppermute | solution.py:23
  24.6 1.1 %collective-permute-done.8.refs_9_ = f32[16,256]{1,0:T(8,128)S(1)} collective-permute-done((f32[16,256]{1,0:T(8,128)S(1)}, f32[16,256]{1,0:T(8,128)S(1)}, u32[]{:S(2)}, u32[]{:S(2)}) %collective-permute-start.8) | collective-permute-done | bytes 16416 | tf_op jit(solution)/shard_map/ppermute | solution.py:23
  25.7 2.6 %collective-permute-done.7.refs_8_ = f32[16,256]{1,0:T(8,128)S(1)} collective-permute-done((f32[16,256]{1,0:T(8,128)S(1)}, f32[16,256]{1,0:T(8,128)S(1)}, u32[]{:S(2)}, u32[]{:S(2)}) %collective-permute-start.7) | collective-permute-done | bytes 16416 | tf_op jit(solution)/shard_map/ppermute | solution.py:23
  28.3 0.0 collective-permute-done.6.refs_7_
  28.3 1.4 %shard_map.108 = (f32[24,256]{1,0:T(8,128)S(1)}, f32[16,256]{1,0:T(8,128)S(1)}) custom-call(bf16[64,256,256]{2,1,0:T(8,128)(2,1)S(1)} %get-tuple-element.24.refs_0_, bf16[64,16]{1,0:T(8,128)(2,1)S(1)} %get-tuple-element.29.refs_1_, bf16[16,128]{1,0:T(8,128)(2,1)S(1)} %get-tuple-element.26.refs_2_, f32[64,256]{1,0:T(8,128)S(1)} %get-tuple-element.25.refs_1_.refs_3_, ...), custom_call_target="tpu_custom_call" | custom-call | tf_op jit(solution)/shard_map/pallas_call | solution.py:289
  29.7 0.0 collective-permute-start.11
  29.7 1.5 %collective-permute-start.10 = (f32[24,256]{1,0:T(8,128)S(1)}, f32[24,256]{1,0:T(8,128)S(1)}, u32[]{:S(2)}, u32[]{:S(2)}) collective-permute-start(f32[24,256]{1,0:T(8,128)S(1)} %get-tuple-element.34.refs_5_), channel_id=1, source_target_pairs={{0,2},{1,3},{2,0},{3,1},{4,6},{5,7},{6,4},{7,5},{8,10},{9,11},{10,... | collective-permute-start | bytes 73736 | tf_op jit(solution)/shard_map/ppermute | solution.py:23
  31.2 0.4 collective-permute-start.9
  31.6 1.6 %collective-permute-done.11.refs_8_ = f32[24,256]{1,0:T(8,128)S(1)} collective-permute-done((f32[24,256]{1,0:T(8,128)S(1)}, f32[24,256]{1,0:T(8,128)S(1)}, u32[]{:S(2)}, u32[]{:S(2)}) %collective-permute-start.11) | collective-permute-done | bytes 24608 | tf_op jit(solution)/shard_map/ppermute | solution.py:23
  33.2 0.4 collective-permute-done.10.refs_7_
  33.6 0.0 collective-permute-done.9.refs_6_
  33.6 1.4 %shard_map.109 = (f32[24,256]{1,0:T(8,128)S(1)}, f32[16,256]{1,0:T(8,128)S(1)}, f32[8,256]{1,0:T(8,128)S(1)}) custom-call(bf16[64,256,256]{2,1,0:T(8,128)(2,1)S(1)} %bitcast.8, bf16[64,16]{1,0:T(8,128)(2,1)S(1)} %get-tuple-element.30.refs_1_, bf16[16,128]{1,0:T(8,128)(2,1)S(1)} %get-tuple-element.31.refs_2_, ...), custom_call_target="tpu_custom_call" | custom-call | tf_op jit(solution)/shard_map/pallas_call | solution.py:289
  35.1 1.5 %collective-permute-start.14 = (f32[24,256]{1,0:T(8,128)S(1)}, f32[24,256]{1,0:T(8,128)S(1)}, u32[]{:S(2)}, u32[]{:S(2)}) collective-permute-start(f32[24,256]{1,0:T(8,128)S(1)} %get-tuple-element.36.refs_7_), channel_id=1, source_target_pairs={{0,12},{4,8},{8,4},{12,0},{1,13},{5,9},{9,5},{13,1},{2,14},{6,10},... | collective-permute-start | bytes 73736 | tf_op jit(solution)/shard_map/ppermute | solution.py:23
  36.5 0.6 %collective-permute-start.13 = (f32[24,256]{1,0:T(8,128)S(1)}, f32[24,256]{1,0:T(8,128)S(1)}, u32[]{:S(2)}, u32[]{:S(2)}) collective-permute-start(f32[24,256]{1,0:T(8,128)S(1)} %get-tuple-element.36.refs_7_), channel_id=1, source_target_pairs={{0,8},{4,12},{8,0},{12,4},{1,9},{5,13},{9,1},{13,5},{2,10},{6,14},... | collective-permute-start | bytes 73736 | tf_op jit(solution)/shard_map/ppermute | solution.py:23
  37.1 2.3 %collective-permute-start.12 = (f32[24,256]{1,0:T(8,128)S(1)}, f32[24,256]{1,0:T(8,128)S(1)}, u32[]{:S(2)}, u32[]{:S(2)}) collective-permute-start(f32[24,256]{1,0:T(8,128)S(1)} %get-tuple-element.36.refs_7_), channel_id=1, source_target_pairs={{0,4},{4,0},{8,12},{12,8},{1,5},{5,1},{9,13},{13,9},{2,6},{6,2},{1... | collective-permute-start | bytes 73736 | tf_op jit(solution)/shard_map/ppermute | solution.py:23
  39.4 1.3 %collective-permute-done.14.refs_10_ = f32[24,256]{1,0:T(8,128)S(1)} collective-permute-done((f32[24,256]{1,0:T(8,128)S(1)}, f32[24,256]{1,0:T(8,128)S(1)}, u32[]{:S(2)}, u32[]{:S(2)}) %collective-permute-start.14) | collective-permute-done | bytes 24608 | tf_op jit(solution)/shard_map/ppermute | solution.py:23
  40.7 0.5 collective-permute-done.13.refs_9_
  41.3 0.2 collective-permute-done.12.refs_8_
  41.5 1.5 %shard_map.110 = (f32[24,256]{1,0:T(8,128)S(1)}, f32[16,256]{1,0:T(8,128)S(1)}, f32[8,128]{1,0:T(8,128)S(1)}) custom-call(bf16[64,256,256]{2,1,0:T(8,128)(2,1)S(1)} %get-tuple-element.24.refs_0_, bf16[64,16]{1,0:T(8,128)(2,1)S(1)} %get-tuple-element.29.refs_1_, bf16[16,128]{1,0:T(8,128)(2,1)S(1)} %get-tuple-element.26.refs_2_, ...), custom_call_target="tpu_custom_call" | custom-call | tf_op jit(solution)/shard_map/pallas_call | solution.py:289
  43.1 0.0 collective-permute-start.17
  43.1 1.5 %collective-permute-start.16 = (f32[24,256]{1,0:T(8,128)S(1)}, f32[24,256]{1,0:T(8,128)S(1)}, u32[]{:S(2)}, u32[]{:S(2)}) collective-permute-start(f32[24,256]{1,0:T(8,128)S(1)} %get-tuple-element.40.refs_7_), channel_id=1, source_target_pairs={{0,2},{1,3},{2,0},{3,1},{4,6},{5,7},{6,4},{7,5},{8,10},{9,11},{10,... | collective-permute-start | bytes 73736 | tf_op jit(solution)/shard_map/ppermute | solution.py:23
  44.5 0.4 collective-permute-start.15
  44.9 1.6 %collective-permute-done.17.refs_10_ = f32[24,256]{1,0:T(8,128)S(1)} collective-permute-done((f32[24,256]{1,0:T(8,128)S(1)}, f32[24,256]{1,0:T(8,128)S(1)}, u32[]{:S(2)}, u32[]{:S(2)}) %collective-permute-start.17) | collective-permute-done | bytes 24608 | tf_op jit(solution)/shard_map/ppermute | solution.py:23
  46.6 0.4 collective-permute-done.16.refs_9_
  46.9 0.0 collective-permute-done.15.refs_8_
  46.9 1.6 %shard_map.111 = (f32[8,256]{1,0:T(8,128)S(1)}, f32[8,256]{1,0:T(8,128)S(1)}, f32[8,256]{1,0:T(8,128)S(1)}, f32[8,256]{1,0:T(8,128)S(1)}, f32[8,256]{1,0:T(8,128)S(1)}) custom-call(bf16[64,256,256]{2,1,0:T(8,128)(2,1)S(1)} %bitcast.8, bf16[64,16]{1,0:T(8,128)(2,1)S(1)} %get-tuple-element.30.refs_1_, bf16[16,128]{1,0:T(8,128)(2,1)S(1)} %get-tuple-element.31.refs_2_, ...), custom_call_target="tpu_custom_call" | custom-call | tf_op jit(solution)/shard_map/pallas_call | solution.py:289
  48.5 1.8 %collective-permute-start.18 = (f32[8,256]{1,0:T(8,128)S(1)}, f32[8,256]{1,0:T(8,128)S(1)}, u32[]{:S(2)}, u32[]{:S(2)}) collective-permute-start(f32[8,256]{1,0:T(8,128)S(1)} %get-tuple-element.43), channel_id=1, source_target_pairs={{0,4},{4,0},{8,12},{12,8},{1,5},{5,1},{9,13},{13,9},{2,6},{6,2},{1... | collective-permute-start | bytes 24584 | tf_op jit(solution)/shard_map/ppermute | solution.py:23
  50.3 1.2 %collective-permute-start.19 = (f32[8,256]{1,0:T(8,128)S(1)}, f32[8,256]{1,0:T(8,128)S(1)}, u32[]{:S(2)}, u32[]{:S(2)}) collective-permute-start(f32[8,256]{1,0:T(8,128)S(1)} %get-tuple-element.44), channel_id=1, source_target_pairs={{0,8},{4,12},{8,0},{12,4},{1,9},{5,13},{9,1},{13,5},{2,10},{6,14},... | collective-permute-start | bytes 24584 | tf_op jit(solution)/shard_map/ppermute | solution.py:23
  51.4 1.5 %collective-permute-start.20 = (f32[8,256]{1,0:T(8,128)S(1)}, f32[8,256]{1,0:T(8,128)S(1)}, u32[]{:S(2)}, u32[]{:S(2)}) collective-permute-start(f32[8,256]{1,0:T(8,128)S(1)} %get-tuple-element.45), channel_id=1, source_target_pairs={{0,12},{4,8},{8,4},{12,0},{1,13},{5,9},{9,5},{13,1},{2,14},{6,10},... | collective-permute-start | bytes 24584 | tf_op jit(solution)/shard_map/ppermute | solution.py:23
  52.9 0.0 collective-permute-done.18.refs_7_
  52.9 1.9 %collective-permute-done.19.refs_8_ = f32[8,256]{1,0:T(8,128)S(1)} collective-permute-done((f32[8,256]{1,0:T(8,128)S(1)}, f32[8,256]{1,0:T(8,128)S(1)}, u32[]{:S(2)}, u32[]{:S(2)}) %collective-permute-start.19) | collective-permute-done | bytes 8224 | tf_op jit(solution)/shard_map/ppermute | solution.py:23
  54.8 2.1 %collective-permute-done.20.refs_9_ = f32[8,256]{1,0:T(8,128)S(1)} collective-permute-done((f32[8,256]{1,0:T(8,128)S(1)}, f32[8,256]{1,0:T(8,128)S(1)}, u32[]{:S(2)}, u32[]{:S(2)}) %collective-permute-start.20) | collective-permute-done | bytes 8224 | tf_op jit(solution)/shard_map/ppermute | solution.py:23
  56.9 0.8 %shard_map.112 = (f32[4,256]{1,0:T(4,128)}, f32[4,256]{1,0:T(4,128)}) custom-call(f32[16,256]{1,0:T(8,128)S(1)} %get-tuple-element.27.refs_5_.refs_4_.refs_0_, f32[16,256]{1,0:T(8,128)S(1)} %get-tuple-element.28.refs_4_.refs_1_, f32[16,256]{1,0:T(8,128)S(1)} %get-tuple-element.33.refs_5_.refs_2_, f32[16,256]{1,0:T(8,128)S(1)} %get-tuple-element.37.refs_3_, ...), custom_call_target="tpu_custom_call" | custom-call | tf_op jit(solution)/shard_map/pallas_call | solution.py:289
  (1 shorter events, 0.0 us)
Async XLA Ops:
  1.4 11.6 %copy-start.3 = (s32[64]{0:T(128)S(1)}, s32[64]{0:T(128)}, u32[]{:S(2)}) copy-start(s32[64]{0:T(128)} %param.12) | copy-start | bytes 772
  1.4 11.6 %collective-permute-start.2 = (f32[16,256]{1,0:T(8,128)S(1)}, f32[16,256]{1,0:T(8,128)S(1)}, u32[]{:S(2)}, u32[]{:S(2)}) collective-permute-start(f32[16,256]{1,0:T(8,128)S(1)} %shard_map.104.opening.refs_5_), channel_id=1, source_target_pairs={{0,12},{4,8},{8,4},{12,0},{1,13},{5,9},{9,5},{13,1},{2,14},{6,10},... | collective-permute-start | bytes 49160 | tf_op jit(solution)/shard_map/ppermute | solution.py:23
  6.5 6.5 %collective-permute-start.1 = (f32[16,256]{1,0:T(8,128)S(1)}, f32[16,256]{1,0:T(8,128)S(1)}, u32[]{:S(2)}, u32[]{:S(2)}) collective-permute-start(f32[16,256]{1,0:T(8,128)S(1)} %shard_map.104.opening.refs_5_), channel_id=1, source_target_pairs={{0,8},{4,12},{8,0},{12,4},{1,9},{5,13},{9,1},{13,5},{2,10},{6,14},... | collective-permute-start | bytes 49160 | tf_op jit(solution)/shard_map/ppermute | solution.py:23
  6.5 6.5 %collective-permute-start = (f32[16,256]{1,0:T(8,128)S(1)}, f32[16,256]{1,0:T(8,128)S(1)}, u32[]{:S(2)}, u32[]{:S(2)}) collective-permute-start(f32[16,256]{1,0:T(8,128)S(1)} %shard_map.104.opening.refs_5_), channel_id=1, source_target_pairs={{0,4},{4,0},{8,12},{12,8},{1,5},{5,1},{9,13},{13,9},{2,6},{6,2},{1... | collective-permute-start | bytes 49160 | tf_op jit(solution)/shard_map/ppermute | solution.py:23
  7.1 3.4 %copy-start = (bf16[64,256,256]{2,1,0:T(8,128)(2,1)S(1)}, bf16[64,256,256]{2,1,0:T(8,128)(2,1)}, u32[]{:S(2)}) copy-start(bf16[64,256,256]{2,1,0:T(8,128)(2,1)} %refs_0_.5) | copy-start | bytes 25165828
  10.5 8.2 %slice-start = ((s8[8388608]{0:T(1024)(128)(4,1)}), s8[4194304]{0:T(1024)(128)(4,1)S(1)}, s32[]{:S(2)}) async-start(s8[8388608]{0:T(1024)(128)(4,1)} %bitcast.7), calls=%async_computation | async-start | bytes 8388608
  10.5 8.2 %copy-start.1 = (f32[16,256]{1,0:T(8,128)S(1)}, f32[16,256]{1,0:T(8,128)}, u32[]{:S(2)}) copy-start(f32[16,256]{1,0:T(8,128)} %refs_4_.5) | copy-start | bytes 49156
  10.5 8.2 %copy-start.2 = (f32[16,256]{1,0:T(8,128)S(1)}, f32[16,256]{1,0:T(8,128)}, u32[]{:S(2)}) copy-start(f32[16,256]{1,0:T(8,128)} %refs_4_.3) | copy-start | bytes 49156
  13.0 5.8 %slice-start.1 = ((s8[8388608]{0:T(1024)(128)(4,1)}), s8[4194304]{0:T(1024)(128)(4,1)S(1)}, s32[]{:S(2)}) async-start(s8[8388608]{0:T(1024)(128)(4,1)} %bitcast.7), calls=%async_computation.1 | async-start | bytes 8388608
  14.6 3.2 %collective-permute-start.5 = (f32[16,256]{1,0:T(8,128)S(1)}, f32[16,256]{1,0:T(8,128)S(1)}, u32[]{:S(2)}, u32[]{:S(2)}) collective-permute-start(f32[16,256]{1,0:T(8,128)S(1)} %get-tuple-element.32.refs_6_), channel_id=1, source_target_pairs={{0,3},{1,2},{2,1},{3,0},{4,7},{5,6},{6,5},{7,4},{8,11},{9,10},{10,... | collective-permute-start | bytes 49160 | tf_op jit(solution)/shard_map/ppermute | solution.py:23
  15.0 3.7 %collective-permute-start.4 = (f32[16,256]{1,0:T(8,128)S(1)}, f32[16,256]{1,0:T(8,128)S(1)}, u32[]{:S(2)}, u32[]{:S(2)}) collective-permute-start(f32[16,256]{1,0:T(8,128)S(1)} %get-tuple-element.32.refs_6_), channel_id=1, source_target_pairs={{0,2},{1,3},{2,0},{3,1},{4,6},{5,7},{6,4},{7,5},{8,10},{9,11},{10,... | collective-permute-start | bytes 49160 | tf_op jit(solution)/shard_map/ppermute | solution.py:23
  16.3 2.4 %collective-permute-start.3 = (f32[16,256]{1,0:T(8,128)S(1)}, f32[16,256]{1,0:T(8,128)S(1)}, u32[]{:S(2)}, u32[]{:S(2)}) collective-permute-start(f32[16,256]{1,0:T(8,128)S(1)} %get-tuple-element.32.refs_6_), channel_id=1, source_target_pairs={{0,1},{1,0},{2,3},{3,2},{4,5},{5,4},{6,7},{7,6},{8,9},{9,8},{10,11... | collective-permute-start | bytes 49160 | tf_op jit(solution)/shard_map/ppermute | solution.py:23
  20.2 5.5 %collective-permute-start.8 = (f32[16,256]{1,0:T(8,128)S(1)}, f32[16,256]{1,0:T(8,128)S(1)}, u32[]{:S(2)}, u32[]{:S(2)}) collective-permute-start(f32[16,256]{1,0:T(8,128)S(1)} %shard_map.107.refs_6_), channel_id=1, source_target_pairs={{0,12},{4,8},{8,4},{12,0},{1,13},{5,9},{9,5},{13,1},{2,14},{6,10},... | collective-permute-start | bytes 49160 | tf_op jit(solution)/shard_map/ppermute | solution.py:23
  23.7 4.6 %collective-permute-start.7 = (f32[16,256]{1,0:T(8,128)S(1)}, f32[16,256]{1,0:T(8,128)S(1)}, u32[]{:S(2)}, u32[]{:S(2)}) collective-permute-start(f32[16,256]{1,0:T(8,128)S(1)} %shard_map.107.refs_6_), channel_id=1, source_target_pairs={{0,8},{4,12},{8,0},{12,4},{1,9},{5,13},{9,1},{13,5},{2,10},{6,14},... | collective-permute-start | bytes 49160 | tf_op jit(solution)/shard_map/ppermute | solution.py:23
  23.7 4.6 %collective-permute-start.6 = (f32[16,256]{1,0:T(8,128)S(1)}, f32[16,256]{1,0:T(8,128)S(1)}, u32[]{:S(2)}, u32[]{:S(2)}) collective-permute-start(f32[16,256]{1,0:T(8,128)S(1)} %shard_map.107.refs_6_), channel_id=1, source_target_pairs={{0,4},{4,0},{8,12},{12,8},{1,5},{5,1},{9,13},{13,9},{2,6},{6,2},{1... | collective-permute-start | bytes 49160 | tf_op jit(solution)/shard_map/ppermute | solution.py:23
  29.7 3.5 %collective-permute-start.11 = (f32[24,256]{1,0:T(8,128)S(1)}, f32[24,256]{1,0:T(8,128)S(1)}, u32[]{:S(2)}, u32[]{:S(2)}) collective-permute-start(f32[24,256]{1,0:T(8,128)S(1)} %get-tuple-element.34.refs_5_), channel_id=1, source_target_pairs={{0,3},{1,2},{2,1},{3,0},{4,7},{5,6},{6,5},{7,4},{8,11},{9,10},{10,... | collective-permute-start | bytes 73736 | tf_op jit(solution)/shard_map/ppermute | solution.py:23
  29.7 3.9 %collective-permute-start.10 = (f32[24,256]{1,0:T(8,128)S(1)}, f32[24,256]{1,0:T(8,128)S(1)}, u32[]{:S(2)}, u32[]{:S(2)}) collective-permute-start(f32[24,256]{1,0:T(8,128)S(1)} %get-tuple-element.34.refs_5_), channel_id=1, source_target_pairs={{0,2},{1,3},{2,0},{3,1},{4,6},{5,7},{6,4},{7,5},{8,10},{9,11},{10,... | collective-permute-start | bytes 73736 | tf_op jit(solution)/shard_map/ppermute | solution.py:23
  31.2 2.4 %collective-permute-start.9 = (f32[24,256]{1,0:T(8,128)S(1)}, f32[24,256]{1,0:T(8,128)S(1)}, u32[]{:S(2)}, u32[]{:S(2)}) collective-permute-start(f32[24,256]{1,0:T(8,128)S(1)} %get-tuple-element.34.refs_5_), channel_id=1, source_target_pairs={{0,1},{1,0},{2,3},{3,2},{4,5},{5,4},{6,7},{7,6},{8,9},{9,8},{10,11... | collective-permute-start | bytes 73736 | tf_op jit(solution)/shard_map/ppermute | solution.py:23
  35.1 5.7 %collective-permute-start.14 = (f32[24,256]{1,0:T(8,128)S(1)}, f32[24,256]{1,0:T(8,128)S(1)}, u32[]{:S(2)}, u32[]{:S(2)}) collective-permute-start(f32[24,256]{1,0:T(8,128)S(1)} %get-tuple-element.36.refs_7_), channel_id=1, source_target_pairs={{0,12},{4,8},{8,4},{12,0},{1,13},{5,9},{9,5},{13,1},{2,14},{6,10},... | collective-permute-start | bytes 73736 | tf_op jit(solution)/shard_map/ppermute | solution.py:23
  36.5 4.8 %collective-permute-start.13 = (f32[24,256]{1,0:T(8,128)S(1)}, f32[24,256]{1,0:T(8,128)S(1)}, u32[]{:S(2)}, u32[]{:S(2)}) collective-permute-start(f32[24,256]{1,0:T(8,128)S(1)} %get-tuple-element.36.refs_7_), channel_id=1, source_target_pairs={{0,8},{4,12},{8,0},{12,4},{1,9},{5,13},{9,1},{13,5},{2,10},{6,14},... | collective-permute-start | bytes 73736 | tf_op jit(solution)/shard_map/ppermute | solution.py:23
  37.1 4.4 %collective-permute-start.12 = (f32[24,256]{1,0:T(8,128)S(1)}, f32[24,256]{1,0:T(8,128)S(1)}, u32[]{:S(2)}, u32[]{:S(2)}) collective-permute-start(f32[24,256]{1,0:T(8,128)S(1)} %get-tuple-element.36.refs_7_), channel_id=1, source_target_pairs={{0,4},{4,0},{8,12},{12,8},{1,5},{5,1},{9,13},{13,9},{2,6},{6,2},{1... | collective-permute-start | bytes 73736 | tf_op jit(solution)/shard_map/ppermute | solution.py:23
  43.1 3.5 %collective-permute-start.17 = (f32[24,256]{1,0:T(8,128)S(1)}, f32[24,256]{1,0:T(8,128)S(1)}, u32[]{:S(2)}, u32[]{:S(2)}) collective-permute-start(f32[24,256]{1,0:T(8,128)S(1)} %get-tuple-element.40.refs_7_), channel_id=1, source_target_pairs={{0,3},{1,2},{2,1},{3,0},{4,7},{5,6},{6,5},{7,4},{8,11},{9,10},{10,... | collective-permute-start | bytes 73736 | tf_op jit(solution)/shard_map/ppermute | solution.py:23
  43.1 3.9 %collective-permute-start.16 = (f32[24,256]{1,0:T(8,128)S(1)}, f32[24,256]{1,0:T(8,128)S(1)}, u32[]{:S(2)}, u32[]{:S(2)}) collective-permute-start(f32[24,256]{1,0:T(8,128)S(1)} %get-tuple-element.40.refs_7_), channel_id=1, source_target_pairs={{0,2},{1,3},{2,0},{3,1},{4,6},{5,7},{6,4},{7,5},{8,10},{9,11},{10,... | collective-permute-start | bytes 73736 | tf_op jit(solution)/shard_map/ppermute | solution.py:23
  44.5 2.4 %collective-permute-start.15 = (f32[24,256]{1,0:T(8,128)S(1)}, f32[24,256]{1,0:T(8,128)S(1)}, u32[]{:S(2)}, u32[]{:S(2)}) collective-permute-start(f32[24,256]{1,0:T(8,128)S(1)} %get-tuple-element.40.refs_7_), channel_id=1, source_target_pairs={{0,1},{1,0},{2,3},{3,2},{4,5},{5,4},{6,7},{7,6},{8,9},{9,8},{10,11... | collective-permute-start | bytes 73736 | tf_op jit(solution)/shard_map/ppermute | solution.py:23
  48.5 4.4 %collective-permute-start.18 = (f32[8,256]{1,0:T(8,128)S(1)}, f32[8,256]{1,0:T(8,128)S(1)}, u32[]{:S(2)}, u32[]{:S(2)}) collective-permute-start(f32[8,256]{1,0:T(8,128)S(1)} %get-tuple-element.43), channel_id=1, source_target_pairs={{0,4},{4,0},{8,12},{12,8},{1,5},{5,1},{9,13},{13,9},{2,6},{6,2},{1... | collective-permute-start | bytes 24584 | tf_op jit(solution)/shard_map/ppermute | solution.py:23
  50.3 4.5 %collective-permute-start.19 = (f32[8,256]{1,0:T(8,128)S(1)}, f32[8,256]{1,0:T(8,128)S(1)}, u32[]{:S(2)}, u32[]{:S(2)}) collective-permute-start(f32[8,256]{1,0:T(8,128)S(1)} %get-tuple-element.44), channel_id=1, source_target_pairs={{0,8},{4,12},{8,0},{12,4},{1,9},{5,13},{9,1},{13,5},{2,10},{6,14},... | collective-permute-start | bytes 24584 | tf_op jit(solution)/shard_map/ppermute | solution.py:23
  51.4 5.4 %collective-permute-start.20 = (f32[8,256]{1,0:T(8,128)S(1)}, f32[8,256]{1,0:T(8,128)S(1)}, u32[]{:S(2)}, u32[]{:S(2)}) collective-permute-start(f32[8,256]{1,0:T(8,128)S(1)} %get-tuple-element.45), channel_id=1, source_target_pairs={{0,12},{4,8},{8,4},{12,0},{1,13},{5,9},{9,5},{13,1},{2,14},{6,10},... | collective-permute-start | bytes 24584 | tf_op jit(solution)/shard_map/ppermute | solution.py:23
